TPU v7x, 256 devices: a whole 4x4x8 slice. The times are simulated.
256 devices in a mesh: band: 8 (over x, core), dom: 32 (over z, y).
Axes of the slice: x: 4, y: 4, z: 8, core: 2. Of those that a mesh axis runs over, the one named last changes fastest.
Arguments:
- orbitals: bfloat16 [256, 192, 48, 64], P('band', 'dom'), may hold values from -1.796875 to 1.796875
- potential: float32 [192, 48, 64], P('dom'), may hold values from -2 to 1
- projectors: float32 [2048, 128], P('dom'), may hold values from -1.5 to 1.5
- coupling: float32 [1024], P('dom'), may hold values from 0.5 to 2
- slot_block: int32 [2048], P('dom'), may hold values from 0 to 143
- slot_projector: int32 [2048], P('dom'), may hold values from 0 to 1023, as said below
- slot_count: int32 [32], P('dom'), may hold values from 16 to 64, as said below
- locked: bfloat16 [2048, 192, 3072], P(None, 'dom', 'band'), may hold values from -0.0078125 to 0.0078125
Outputs:
- orthogonal: bfloat16 [256, 192, 3072], P(None, 'dom', 'band')
- margins: float32 [2048, 256], P(('band', 'dom'))
Inputs may be any that keep to these rules, and one draw needn't show every extreme that they name: `slot_projector`: projector p belongs to domain p // 32; a slot of domain d names a projector of domain d - 1, d or d + 1, cyclically; slot 0 of every domain names one of domain d - 1 and slot 1 one of domain d + 1. The used slots of a domain are its first slot_count slots; some domain uses all and some uses 64 // 4.
All inputs are finite; a program needn't handle non-finite values.
Results may differ from a plain program's by a relative error of at most 0.0039.
The roundings to bfloat16 on the way count: a program that leaves them out, or rounds other values in their place, can miss the bound.
Values may be sent and summed in bfloat16 or wider, within the bound.
No kernel may reach another device: no remote copies, remote signals or barrier semaphores. Data moves between devices by JAX's collectives and lax.ppermute only.
A program may use at most 320 MiB of HBM per device.

v0:
```python
import jax
import jax.numpy as jnp
from jax import lax
from jax.sharding import PartitionSpec as P

BS = 128
PROJ_DOM = 32


COEFFS = (
    -5369.0 / 1800.0,
    12.0 / 7.0,
    -15.0 / 56.0,
    10.0 / 189.0,
    -1.0 / 112.0,
    2.0 / 825.0,
    -1.0 / 5544.0,
)


def with_halo(shard, sides, width):
    for axis, dim in sides:
        size, length = (lax.axis_size(axis), shard.shape[dim])
        up = [(i, (i + 1) % size) for i in range(size)]
        down = [(j, i) for i, j in up]
        last = lax.slice_in_dim(shard, length - width, length, axis=dim)
        initial = lax.slice_in_dim(shard, 0, width, axis=dim)
        before = lax.ppermute(last, axis, up)
        after = lax.ppermute(initial, axis, down)
        shard = jnp.concatenate([before, shard, after], axis=dim)
    return shard


def laplacian(orbital, extended):
    planes_x = orbital.shape[1]
    depth_z = orbital.shape[2]
    laplace = 3.0 * COEFFS[0] * orbital
    padded = jnp.pad(orbital, ((0, 0), (0, 0), (6, 6), (0, 0)))
    for offset in range(1, 7):
        weight = COEFFS[offset]
        laplace = laplace + weight * (
            extended[:, 6 + offset : 6 + offset + planes_x]
            + extended[:, 6 - offset : 6 - offset + planes_x]
        )
        laplace = laplace + weight * (jnp.roll(orbital, offset, 3) + jnp.roll(orbital, -offset, 3))
        laplace = laplace + weight * (
            padded[:, :, 6 + offset : 6 + offset + depth_z]
            + padded[:, :, 6 - offset : 6 - offset + depth_z]
        )
    return laplace


def per_device(
    orbitals, potential, projectors, coupling, slot_block, slot_projector, slot_count, locked
):
    orbital = orbitals.astype(jnp.float32)
    extended = with_halo(orbitals, (("dom", 1),), 6).astype(jnp.float32)
    laplace = laplacian(orbital, extended)
    band_rows, planes_x, depth_z, width_y = orbital.shape
    blocks_count = planes_x * depth_z * width_y // BS
    flat = orbital.reshape(band_rows, blocks_count, BS)
    blocks = flat[:, slot_block]
    slots = slot_block.shape[0]
    active = (jnp.arange(slots, dtype=jnp.int32) < slot_count[0]).astype(jnp.float32)
    inner_part = jnp.sum(blocks * projectors[None], axis=2) * active[None]
    domains = lax.axis_size("dom")
    here = lax.axis_index("dom")
    owner = slot_projector // PROJ_DOM
    local_id = slot_projector % PROJ_DOM
    relative = (owner - here + domains) % domains
    column = jnp.where(
        relative == 0,
        PROJ_DOM + local_id,
        jnp.where(relative == 1, 2 * PROJ_DOM + local_id, local_id),
    )
    onehot = (column[:, None] == jnp.arange(3 * PROJ_DOM, dtype=jnp.int32)[None, :]).astype(
        jnp.float32
    )
    partial_value = jnp.dot(inner_part, onehot, precision=lax.Precision.HIGHEST)
    outgoing = jnp.concatenate(
        [partial_value[:, :PROJ_DOM], partial_value[:, 2 * PROJ_DOM :]], axis=1
    )
    arrived = with_halo(outgoing, (("dom", 1),), PROJ_DOM)
    owned = (
        partial_value[:, PROJ_DOM : 2 * PROJ_DOM] + arrived[:, :PROJ_DOM] + arrived[:, -PROJ_DOM:]
    )
    table_local = owned * coupling[None]
    table = with_halo(table_local, (("dom", 1),), PROJ_DOM)
    slot_value = jnp.dot(table, onehot.T, precision=lax.Precision.HIGHEST) * active[None]
    contribution = slot_value[:, :, None] * projectors[None]
    nonlocal_term = jnp.zeros_like(flat).at[:, slot_block].add(contribution).reshape(orbital.shape)
    hamilton = -0.5 * laplace + potential[None] * orbital + nonlocal_term
    numerator, denominator = lax.psum(
        (jnp.sum(orbital * hamilton, axis=(1, 2, 3)), jnp.sum(orbital * orbital, axis=(1, 2, 3))),
        "dom",
    )
    energy = numerator / denominator
    residual = (hamilton - energy[:, None, None, None] * orbital).astype(jnp.bfloat16)
    residual = residual.reshape(band_rows, planes_x, depth_z * width_y)
    moved = lax.all_to_all(residual, "band", split_axis=2, concat_axis=0, tiled=True)
    all_bands = moved.shape[0]
    locked_flat = locked.reshape(locked.shape[0], -1)
    residual_flat = moved.reshape(all_bands, -1)
    contract_cells = (((1,), (1,)), ((), ()))
    share_rows = locked.shape[0] // lax.axis_size(("band", "dom"))
    summed = lax.psum(
        lax.dot_general(
            locked_flat, residual_flat, contract_cells, preferred_element_type=jnp.float32
        ),
        ("band", "dom"),
    )
    margins = lax.dynamic_slice_in_dim(
        summed, lax.axis_index(("band", "dom")) * share_rows, share_rows, 0
    )
    coeffs = summed.astype(jnp.bfloat16)
    correction = lax.dot_general(
        coeffs, locked_flat, (((0,), (0,)), ((), ())), preferred_element_type=jnp.float32
    )
    orthogonal = (
        (residual_flat.astype(jnp.float32) - correction).astype(jnp.bfloat16).reshape(moved.shape)
    )
    return (orthogonal, margins)


def solution(mesh):
    in_specs = (
        P("band", "dom", None, None),
        P("dom", None, None),
        P("dom", None),
        P("dom"),
        P("dom"),
        P("dom"),
        P("dom"),
        P(None, "dom", "band"),
    )
    out_specs = (P(None, "dom", "band"), P(("band", "dom"), None))
    return jax.shard_map(
        per_device, mesh=mesh, in_specs=in_specs, out_specs=out_specs, check_vma=False
    )
```

profile of v0, /device:TPU:1, one launch (start us, length us, event | category | flops | bytes accessed | tf_op | source)
XLA Modules:
  0.0 609.3 jit_solution(6926809845291708726)
XLA Ops:
  7.2 0.0 copy-start.4
  7.2 2.2 collective-permute-start
  9.4 6.8 %collective-permute-start.1 = (bf16[32,6,48,64]{3,2,1,0:T(8,128)(2,1)}, bf16[32,6,48,64]{3,2,1,0:T(8,128)(2,1)}, u32[]{:S(2)}, u32[]{:S(2)}) collective-permute-start(bf16[32,6,48,64]{3,2,1,0:T(8,128)(2,1)} %param.8), channel_id=1, source_target_pairs={{1,0},{2,1},{3,2},{4,3},{5,4},{6,5},{7,6},{8,7},{9,8},{10,9},{11,1... | collective-permute-start | bytes 3538952 | tf_op jit(solution)/shard_map/ppermute | solution.py:29
  16.2 4.4 reshape.34
  20.6 0.0 copy-done.4
  20.6 4.0 copy.30
  25.3 2.3 gather_fusion
  27.6 0.0 copy-done.2
  27.6 0.3 multiply_reduce_fusion
  27.9 0.3 fusion.50
  28.2 0.1 fusion.77
  28.3 0.0 collective-permute-start.2
  28.3 5.2 collective-permute-start.3
  33.5 4.6 fusion.65
  38.1 4.7 fusion.66
  42.8 4.7 fusion.67
  47.5 4.6 fusion.68
  52.1 4.6 fusion.69
  56.7 4.6 fusion.70
  61.3 4.7 fusion.71
  66.0 4.6 fusion.72
  70.6 4.6 fusion.73
  75.2 4.7 fusion.74
  79.9 4.6 fusion.75
  84.5 0.0 collective-permute-done.2
  84.5 0.0 collective-permute-done.3
  84.5 0.0 copy-done.3
  84.5 0.1 fusion.53
  84.6 0.0 collective-permute-start.4
  84.6 5.0 collective-permute-start.5
  89.6 4.7 fusion.76
  94.3 2.7 convert_element_type.28
  97.0 0.0 collective-permute-done.4
  97.0 0.0 collective-permute-done.5
  97.0 0.2 convolution_multiply_fusion
  97.2 0.1 copy.31
  97.3 0.3 multiply_bitcast_fusion
  97.6 1.7 broadcast_in_dim.4
  99.3 8.0 %scatter_fusion = f32[32,144,128]{2,0,1:T(8,128)} fusion(f32[32,144,128]{2,0,1:T(8,128)} %broadcast_in_dim.4, s32[64]{0:T(128)S(1)} %compare_select_fusion, f32[64,32,128]{2,1,0:T(8,128)S(1)} %multiply_bitcast_fusion), kind=kCustom, calls=%fused_computation.1 | custom fusion | flops 262144 | bytes 3145984 | tf_op jit(solution)/shard_map/scatter-add | solution.py:91
  107.4 4.5 copy.32
  111.8 4.5 reshape.35
  116.4 0.0 collective-permute-done
  116.4 0.0 collective-permute-done.1
  116.4 8.1 %maximum_convert_fusion = f32[32,18,48,64]{3,2,1,0:T(8,128)} fusion(bf16[32,6,48,64]{3,2,1,0:T(8,128)(2,1)} %collective-permute-done.1, bf16[32,6,48,64]{3,2,1,0:T(8,128)(2,1)S(1)} %copy-done, bf16[32,6,48,64]{3,2,1,0:T(8,128)(2,1)} %collective-permute-done), kind=kLoop, calls=%fused_computation.14 | loop fusion | flops 5308416 | bytes 10616832 | tf_op jit(solution)/shard_map/convert_element_type | solution.py:57
  124.5 0.0 copy-done.1
  124.5 75.7 %fusion.21 = (f32[32]{0:T(128)S(1)}, f32[32]{0:T(128)S(1)}, f32[32,6,48,64]{3,2,1,0:T(8,128)}) fusion(bf16[32,6,48,64]{3,2,1,0:T(8,128)(2,1)S(1)} %copy-done, f32[32,6,48,64]{3,2,1,0:T(8,128)} %reshape.35, f32[6,48,64]{2,1,0:T(8,128)S(1)} %copy-done.1, f32[32,6,48,6]{3,2,1,0:T(8,128)} %get-tuple-element.36, f32[32,6,48,58]{3,2,1,0:T(8,128)} %get-tuple-element.38, ...), kind=kLoop, calls=%fused_computation.41 | loop fusion | flops 44826560 | bytes 64954624 | tf_op jit(solution)/shard_map/reduce_sum | solution.py:94
  200.2 56.2 %all-reduce.1 = (f32[32]{0:T(128)S(1)}, f32[32]{0:T(128)S(1)}) all-reduce(f32[32]{0:T(128)S(1)} %get-tuple-element.11, f32[32]{0:T(128)S(1)} %get-tuple-element.10), channel_id=1, replica_groups=mesh['band'=8,'dom'=32] {'dom'}, use_global_device_ids=true, to_apply=%region_3.4 | all-reduce | flops 64 | bytes 512 | tf_op jit(solution)/shard_map/psum | solution.py:93
  256.4 4.6 fusion.23
  261.0 7.8 %copy.45 = bf16[32,6,48,64]{0,1,3,2:T(8,128)(2,1)} copy(bf16[32,6,48,64]{3,2,1,0:T(8,128)(2,1)} %fusion.23) | data formatting | bytes 2359296 | tf_op jit(solution)/shard_map/reshape | solution.py:99
  268.8 8.6 %reshape.59 = bf16[8,2,36864]{2,1,0:T(2,128)(2,1)} reshape(bf16[3072,6,32]{2,1,0:T(8,128)(2,1)} %bitcast.23) | data formatting | bytes 2359296
  277.4 20.0 %all-to-all-start = ((bf16[8,2,36864]{2,1,0:T(2,128)(2,1)}), bf16[8,2,36864]{2,1,0:T(2,128)(2,1)S(1)}, u32[]{:S(2)}, u32[]{:S(2)}) async-start(bf16[8,2,36864]{2,1,0:T(2,128)(2,1)} %reshape.59), calls=%async_computation | async-start | bytes 2359296 | tf_op jit(solution)/shard_map/all_to_all | solution.py:100
  297.4 12.5 %copy.37 = bf16[2048,6,384]{0,2,1:T(8,128)(2,1)} copy(bf16[2048,6,384]{2,0,1:T(8,128)(2,1)} %param.15) | data formatting | bytes 18874368 | tf_op args[7]
  309.9 4.0 all-to-all-done
  313.9 6.2 %reshape.60 = bf16[3072,6,32]{2,1,0:T(8,128)(2,1)} reshape(bf16[8,2,36864]{2,1,0:T(2,128)(2,1)S(1)} %all-to-all-done) | data formatting | bytes 2359296
  320.1 6.5 %copy.36 = bf16[8,32,6,384]{3,2,1,0:T(8,128)(2,1)S(1)} copy(bf16[8,32,6,384]{1,2,3,0:T(8,128)(2,1)} %bitcast.24) | data formatting | bytes 2359296 | tf_op jit(solution)/shard_map/all_to_all | solution.py:100
  326.6 0.2 copy.46
  326.8 7.7 %convolution_bitcast_fusion = f32[2048,256]{0,1:T(8,128)} fusion(bf16[256,2304]{1,0:T(8,128)(2,1)S(1)} %bitcast.29, bf16[2048,2304]{0,1:T(8,128)(2,1)} %bitcast.25), kind=kOutput, calls=%fused_computation.82 | convolution fusion | flops 2415919104 | bytes 12713984 | tf_op jit(solution)/shard_map/dot_general | solution.py:107
  334.5 0.0 all-reduce.4.cloned.1.call-update
  334.6 257.0 %all-reduce.4.cloned.1.call-done = f32[2048,256]{0,1:T(8,128)} async-done(((f32[2048,256]{0,1:T(8,128)}), f32[2048,256]{0,1:T(8,128)}) %all-reduce.4.cloned.1.call-update) | async-done | bytes 2097168 | tf_op jit(solution)/shard_map/psum | solution.py:106
  591.6 7.0 %fusion.48 = bf16[256,2304]{1,0:T(8,128)(2,1)S(1)} fusion(bf16[2048,2304]{0,1:T(8,128)(2,1)} %bitcast.26, bf16[256,2304]{1,0:T(8,128)(2,1)S(1)} %bitcast.30, f32[2048,256]{0,1:T(8,128)} %all-reduce.4.cloned.1.call-done), kind=kOutput, calls=%fused_computation.81 | convolution fusion | flops 2418212864 | bytes 13893632 | tf_op jit(solution)/shard_map/dot_general | solution.py:116
  598.6 0.6 copy.38
  599.2 1.4 copy.39
  600.6 1.0 constant_dynamic-slice_fusion
  601.6 0.7 copy.40
  (13 shorter events, 0.1 us)
Async XLA Ops:
  7.2 13.4 %copy-start.4 = (s32[64]{0:T(128)S(1)}, s32[64]{0:T(128)}, u32[]{:S(2)}) copy-start(s32[64]{0:T(128)} %param.12) | copy-start | bytes 772
  7.2 109.2 %collective-permute-start = (bf16[32,6,48,64]{3,2,1,0:T(8,128)(2,1)}, bf16[32,6,48,64]{3,2,1,0:T(8,128)(2,1)}, u32[]{:S(2)}, u32[]{:S(2)}) collective-permute-start(bf16[32,6,48,64]{3,2,1,0:T(8,128)(2,1)} %param.8), channel_id=1, source_target_pairs={{0,1},{1,2},{2,3},{3,4},{4,5},{5,6},{6,7},{7,8},{8,9},{9,10},{10,1... | collective-permute-start | bytes 3538952 | tf_op jit(solution)/shard_map/ppermute | solution.py:28
  9.4 107.0 %collective-permute-start.1 = (bf16[32,6,48,64]{3,2,1,0:T(8,128)(2,1)}, bf16[32,6,48,64]{3,2,1,0:T(8,128)(2,1)}, u32[]{:S(2)}, u32[]{:S(2)}) collective-permute-start(bf16[32,6,48,64]{3,2,1,0:T(8,128)(2,1)} %param.8), channel_id=1, source_target_pairs={{1,0},{2,1},{3,2},{4,3},{5,4},{6,5},{7,6},{8,7},{9,8},{10,9},{11,1... | collective-permute-start | bytes 3538952 | tf_op jit(solution)/shard_map/ppermute | solution.py:29
  16.2 9.1 %copy-start.5 = (s32[64]{0:T(128)S(1)}, s32[64]{0:T(128)}, u32[]{:S(2)}) copy-start(s32[64]{0:T(128)} %param.13) | copy-start | bytes 772
  16.2 11.4 %copy-start.2 = (f32[64,128]{1,0:T(8,128)S(1)}, f32[64,128]{1,0:T(8,128)}, u32[]{:S(2)}) copy-start(f32[64,128]{1,0:T(8,128)} %param.10) | copy-start | bytes 98308
  20.6 13.0 %copy-start = (bf16[32,6,48,64]{3,2,1,0:T(8,128)(2,1)S(1)}, bf16[32,6,48,64]{3,2,1,0:T(8,128)(2,1)}, u32[]{:S(2)}) copy-start(bf16[32,6,48,64]{3,2,1,0:T(8,128)(2,1)} %param.8) | copy-start | bytes 3538948
  28.3 56.2 %collective-permute-start.2 = (f32[32,32]{1,0:T(8,128)S(1)}, f32[32,32]{1,0:T(8,128)S(1)}, u32[]{:S(2)}, u32[]{:S(2)}) collective-permute-start(f32[32,32]{1,0:T(8,128)S(1)} %get-tuple-element.39), channel_id=1, source_target_pairs={{0,1},{1,2},{2,3},{3,4},{4,5},{5,6},{6,7},{7,8},{8,9},{9,10},{10,1... | collective-permute-start | bytes 12296 | tf_op jit(solution)/shard_map/ppermute | solution.py:28
  28.3 56.2 %collective-permute-start.3 = (f32[32,32]{1,0:T(8,128)S(1)}, f32[32,32]{1,0:T(8,128)S(1)}, u32[]{:S(2)}, u32[]{:S(2)}) collective-permute-start(f32[32,32]{1,0:T(8,128)S(1)} %get-tuple-element.40), channel_id=1, source_target_pairs={{1,0},{2,1},{3,2},{4,3},{5,4},{6,5},{7,6},{8,7},{9,8},{10,9},{11,1... | collective-permute-start | bytes 12296 | tf_op jit(solution)/shard_map/ppermute | solution.py:29
  79.9 4.7 copy-start.3
  84.6 12.4 %collective-permute-start.4 = (f32[32,32]{1,0:T(8,128)S(1)}, f32[32,32]{1,0:T(8,128)S(1)}, u32[]{:S(2)}, u32[]{:S(2)}) collective-permute-start(f32[32,32]{1,0:T(8,128)S(1)} %fusion.53), channel_id=1, source_target_pairs={{0,1},{1,2},{2,3},{3,4},{4,5},{5,6},{6,7},{7,8},{8,9},{9,10},{10,1... | collective-permute-start | bytes 12296 | tf_op jit(solution)/shard_map/ppermute | solution.py:28
  84.6 12.3 %collective-permute-start.5 = (f32[32,32]{1,0:T(8,128)S(1)}, f32[32,32]{1,0:T(8,128)S(1)}, u32[]{:S(2)}, u32[]{:S(2)}) collective-permute-start(f32[32,32]{1,0:T(8,128)S(1)} %fusion.53), channel_id=1, source_target_pairs={{1,0},{2,1},{3,2},{4,3},{5,4},{6,5},{7,6},{8,7},{9,8},{10,9},{11,1... | collective-permute-start | bytes 12296 | tf_op jit(solution)/shard_map/ppermute | solution.py:29
  116.4 8.1 %copy-start.1 = (f32[6,48,64]{2,1,0:T(8,128)S(1)}, f32[6,48,64]{2,1,0:T(8,128)}, u32[]{:S(2)}) copy-start(f32[6,48,64]{2,1,0:T(8,128)} %param.9) | copy-start | bytes 221188
  277.4 36.5 %all-to-all-start = ((bf16[8,2,36864]{2,1,0:T(2,128)(2,1)}), bf16[8,2,36864]{2,1,0:T(2,128)(2,1)S(1)}, u32[]{:S(2)}, u32[]{:S(2)}) async-start(bf16[8,2,36864]{2,1,0:T(2,128)(2,1)} %reshape.59), calls=%async_computation | async-start | bytes 2359296 | tf_op jit(solution)/shard_map/all_to_all | solution.py:100
  297.4 294.2 %all-reduce.4.cloned.1.call-start = ((), (), s32[]{:S(2)}) async-start(), calls=%async_computation.1 | async-start | bytes 4194304 | tf_op jit(solution)/shard_map/psum | solution.py:106
Sparse Core Ops, SparseCore 0:
  334.7 256.8 all-reduce.3
where the time goes:
time: 616 us; the launch traced here: 609 us
  waiting for transfers between devices  261 us (42%)
  local copies, waits for them, and re-layouts  123 us (20%)
  other arithmetic  99.9 us (16%)
  blocking collectives  56.2 us (9%)
  starting transfers between devices  39.3 us (6%)
  matrix products  15.2 us (2%)
  between operations  15.1 us (2%)
    psum x1, waiting for transfers between devices, per_device(): lax.psum(lax.dot_general(locked_flat, residual_flat, contract_cells, pref...  257 us
    reduce_sum x1, other arithmetic, per_device(): jnp.sum(orbital * orbital, axis=(1, 2, 3))  75.7 us
    psum x1, blocking collectives, per_device(): lax.psum((jnp.sum(orbital * hamilton, axis=(1, 2, 3)), jnp.sum(orbital *...  56.2 us
    slice x12, local copies, waits for them, and re-layouts, laplacian(): jnp.roll(orbital, offset, 3) + jnp.roll(orbital, -offset, 3)  55.6 us
    unnamed x18, local copies, waits for them, and re-layouts  29.6 us
    all_to_all x1, starting transfers between devices, per_device(): lax.all_to_all(residual, 'band', split_axis=2, concat_axis=0, tiled=True)  20 us
    ppermute x3, starting transfers between devices, with_halo(): after = lax.ppermute(initial, axis, down)  17 us
  transfers between devices with their start and end apart: 8, of which 2 were waited for; matrix products, arithmetic and copies ran while one was open for 17% of the time, Pallas kernels for 0%

commit v1 on v0

v1 whole, which is shorter than its diff:
```python
import functools

import jax
import jax.numpy as jnp
import numpy as np
from jax import lax
from jax.experimental import pallas as pl
from jax.experimental.pallas import tpu as pltpu
from jax.sharding import Mesh
from jax.sharding import PartitionSpec as P

BS = 128
CHUNKS = 1

COEFFS = (
    -5369.0 / 1800.0,
    12.0 / 7.0,
    -15.0 / 56.0,
    10.0 / 189.0,
    -1.0 / 112.0,
    2.0 / 825.0,
    -1.0 / 5544.0,
)
HALF = tuple(-0.5 * c for c in COEFFS)
WIDTH = 6
DOM = ("z", "y")
BAND = ("x", "core")
F32 = jnp.float32
BF16 = jnp.bfloat16
VMEM = pl.BlockSpec(memory_space=pltpu.VMEM)
SMEM = pl.BlockSpec(memory_space=pltpu.SMEM)


def params(mib):
    return pltpu.CompilerParams(vmem_limit_bytes=mib * 1024 * 1024)


@functools.lru_cache
def plane_weights(width_y):
    src = np.arange(1024)
    dst = np.arange(256)
    dz = np.abs((src // width_y - 2 * (384 // (2 * width_y)))[:, None] - (dst // width_y)[None])
    dy = np.abs((src % width_y)[:, None] - (dst % width_y)[None])
    dy = np.minimum(dy, width_y - dy)
    table = np.zeros(2048)
    table[1 : WIDTH + 1] = HALF[1:]
    full = np.where(dy == 0, table[dz], 0.0) + np.where(dz == 0, table[dy], 0.0)
    terms = []
    for _ in range(3):
        term = full.astype(np.float32).astype(BF16)
        terms.append(term)
        full = full - term.astype(np.float64)
    return np.stack(terms)


def inner_kernel(block_ref, x_ref, proj_ref, onehot_ref, out_ref):
    rows = x_ref.shape[0]
    slots = proj_ref.shape[0]
    lane = lax.broadcasted_iota(jnp.int32, (rows, BS), 1)

    def body(s, acc):
        start = pl.multiple_of(block_ref[s] * BS, BS)
        cells = x_ref[:, pl.ds(start, BS)].astype(F32)
        total = jnp.sum(cells * proj_ref[pl.ds(s, 1), :], axis=1, keepdims=True)
        return jnp.where(lane == s, total, acc)

    acc = lax.fori_loop(0, slots, body, jnp.zeros((rows, BS), F32), unroll=8)
    out_ref[...] = jnp.dot(
        acc, onehot_ref[...], precision=lax.Precision.HIGHEST, preferred_element_type=F32
    )


def local_kernel(planes, x_ref, pot_ref, w_ref, out_ref, pad_ref):
    rows = x_ref.shape[0]
    plane = x_ref.shape[1] // planes
    zeros = jnp.zeros((planes * rows, 384), BF16)
    pad_ref[:, :384] = zeros
    pad_ref[:, 384 + plane :] = zeros
    for p in range(planes):
        pad_ref[p * rows : (p + 1) * rows, 384 : 384 + plane] = x_ref[:, p * plane : (p + 1) * plane]

    def body(step, carry):
        start = pl.multiple_of(step * 256, 256)
        window = pad_ref[:, pl.ds(start, 1024)]
        acc = jnp.dot(window, w_ref[0], preferred_element_type=F32)
        acc += jnp.dot(window, w_ref[1], preferred_element_type=F32)
        acc += jnp.dot(window, w_ref[2], preferred_element_type=F32)
        mid = [window[p * rows : (p + 1) * rows, 384:640].astype(F32) for p in range(planes)]
        for p in range(planes):
            where = pl.multiple_of(p * plane + start, 256)
            value = acc[p * rows : (p + 1) * rows]
            value += (pot_ref[:, pl.ds(where, 256)] + 3.0 * HALF[0]) * mid[p]
            for q in range(planes):
                if q != p and abs(q - p) <= WIDTH:
                    value += HALF[abs(q - p)] * mid[q]
            out_ref[:, pl.ds(where, 256)] = value
        return carry

    lax.fori_loop(0, plane // 256, body, 0)


def hamilton_kernel(
    planes, block_ref, h0_ref, x_ref, left_ref, right_ref, sv_ref, proj_ref, h_ref, nd_ref
):
    rows, cells = x_ref.shape
    plane = cells // planes
    slots = proj_ref.shape[0]

    def halo(step, carry):
        for top in range(0, rows, 16):
            pick = slice(top, top + 16)
            before = []
            after = []
            for p in range(planes):
                where = pl.ds(pl.multiple_of(p * plane + step * BS, BS), BS)
                before.append(left_ref[pick, where].astype(F32))
                after.append(right_ref[pick, where].astype(F32))
            for p in range(planes):
                where = pl.ds(pl.multiple_of(p * plane + step * BS, BS), BS)
                value = h0_ref[pick, where]
                for j in range(p, planes):
                    value += HALF[planes + p - j] * before[j]
                for j in range(p + 1):
                    value += HALF[planes + j - p] * after[j]
                h_ref[pick, where] = value
        return carry

    lax.fori_loop(0, plane // BS, halo, 0)

    for s in range(slots):
        where = pl.ds(pl.multiple_of(block_ref[s] * BS, BS), BS)
        h_ref[:, where] += sv_ref[:, s : s + 1] * proj_ref[s : s + 1, :]

    def energy(step, carry):
        num, den = carry
        where = pl.ds(pl.multiple_of(step * BS, BS), BS)
        x = x_ref[:, where].astype(F32)
        return num + x * h_ref[:, where], den + x * x

    zero = jnp.zeros((rows, BS), F32)
    num, den = lax.fori_loop(0, cells // BS, energy, (zero, zero), unroll=4)
    lane = lax.broadcasted_iota(jnp.int32, (rows, BS), 1)
    num = jnp.sum(num, axis=1, keepdims=True)
    den = jnp.sum(den, axis=1, keepdims=True)
    nd_ref[...] = jnp.where(lane == 0, num, jnp.where(lane == 1, den, 0.0))


def residual_kernel(planes, h_ref, x_ref, e_ref, r_ref):
    parts, rows, width = r_ref.shape
    plane = x_ref.shape[1] // planes
    part = plane // parts
    energy = jnp.broadcast_to(e_ref[...], (rows, BS))
    for c in range(parts):
        for p in range(planes):
            for j in range(part // BS):
                src = p * plane + c * part + j * BS
                dst = p * part + j * BS
                value = h_ref[:, src : src + BS] - energy * x_ref[:, src : src + BS].astype(F32)
                r_ref[c, :, dst : dst + BS] = value.astype(BF16)


def ring(size):
    up = [(i, (i + 1) % size) for i in range(size)]
    return up, [(j, i) for i, j in up]


def spread(value, axis):
    size = lax.axis_size(axis)
    return lax.all_to_all(
        jnp.broadcast_to(value[None], (size,) + value.shape), axis, 0, 0, tiled=True
    )


def per_device(
    orbitals, potential, projectors, coupling, slot_block, slot_projector, slot_count, locked
):
    bands, planes, depth_z, width_y = orbitals.shape
    plane = depth_z * width_y
    cells = planes * plane
    domains = lax.axis_size(DOM)
    groups = lax.axis_size(BAND)
    n_x = lax.axis_size("x")
    core = lax.axis_index("core")
    here = lax.axis_index(DOM)
    slots = slot_block.shape[0]
    owned_count = coupling.shape[0]
    part = plane // groups
    n_locked = locked.shape[0]
    up, down = ring(domains)
    swap = [(0, 1), (1, 0)]

    flat = orbitals.reshape(bands, cells)
    pot = potential.reshape(1, cells)
    weights = jnp.asarray(plane_weights(width_y))

    active = jnp.arange(slots, dtype=jnp.int32) < slot_count[0]
    relative = (slot_projector // owned_count - here + domains) % domains
    section = jnp.where(relative == 0, 1, jnp.where(relative == 1, 2, 0))
    column = section * owned_count + slot_projector % owned_count
    onehot = (
        (column[:, None] == jnp.arange(BS, dtype=jnp.int32)[None, :]) & active[:, None]
    ).astype(F32)
    onehot_rows = jnp.pad(onehot, ((0, BS - slots), (0, 0)))
    locked_flat = locked.reshape(n_locked, planes * part)

    rows = bands // CHUNKS
    outs = []
    for k in range(CHUNKS):
        x = flat[k * rows : (k + 1) * rows]
        left = lax.ppermute(x, DOM, up)
        right = lax.ppermute(x, DOM, down)

        shares = pl.pallas_call(
            inner_kernel,
            out_shape=jax.ShapeDtypeStruct((rows, BS), F32),
            in_specs=[SMEM, VMEM, VMEM, VMEM],
            out_specs=VMEM,
            compiler_params=params(8),
            name="inner",
        )(slot_block, x, projectors, onehot_rows)
        n = owned_count
        to_down, mine, to_up = shares[:, :n], shares[:, n : 2 * n], shares[:, 2 * n : 3 * n]
        total = mine + lax.ppermute(to_up, DOM, up) + lax.ppermute(to_down, DOM, down)
        total = total * coupling[None]
        table = jnp.concatenate(
            [lax.ppermute(total, DOM, up), total, lax.ppermute(total, DOM, down)], axis=1
        )
        slot_value = jnp.dot(
            table, onehot[:, : 3 * n].T, precision=lax.Precision.HIGHEST
        )

        h0 = pl.pallas_call(
            functools.partial(local_kernel, planes),
            out_shape=jax.ShapeDtypeStruct((rows, cells), F32),
            in_specs=[VMEM, VMEM, VMEM],
            out_specs=VMEM,
            scratch_shapes=[pltpu.VMEM((planes * rows, plane + 768), BF16)],
            compiler_params=params(24),
            name="local",
        )(x, pot, weights)

        hamilton, sums = pl.pallas_call(
            functools.partial(hamilton_kernel, planes),
            out_shape=(
                jax.ShapeDtypeStruct((rows, cells), F32),
                jax.ShapeDtypeStruct((rows, BS), F32),
            ),
            in_specs=[SMEM] + [VMEM] * 6,
            out_specs=(VMEM, VMEM),
            compiler_params=params(24),
            name="hamilton",
        )(slot_block, h0, x, left, right, slot_value, projectors)
        sums = jnp.sum(spread(sums[:, :2].T[None], DOM), axis=0)
        sums = sums.reshape(2, rows)
        energy = (sums[0] / sums[1])[:, None]

        residual = pl.pallas_call(
            functools.partial(residual_kernel, planes),
            out_shape=jax.ShapeDtypeStruct((groups, rows, planes * part), BF16),
            in_specs=[VMEM] * 3,
            out_specs=VMEM,
            compiler_params=params(24),
            name="residual",
        )(hamilton, x, energy)
        moved = lax.all_to_all(residual, BAND, 0, 0, tiled=True)
        moved = moved.reshape(groups * rows, planes * part)

        partial = lax.dot_general(
            locked_flat, moved, (((1,), (1,)), ((), ())), preferred_element_type=F32
        )
        partial = partial.reshape(n_x, 2, n_locked // groups, groups * rows)
        kept = lax.dynamic_index_in_dim(partial, core, 1, keepdims=False)
        given = lax.dynamic_index_in_dim(partial, 1 - core, 1, keepdims=False)
        pair = kept + lax.ppermute(given, "core", swap)
        share = jnp.sum(lax.all_to_all(pair, "x", 0, 0, tiled=True), axis=0)
        share = share.reshape(domains, -1, groups * rows)
        margins = jnp.sum(lax.all_to_all(share, DOM, 0, 0, tiled=True), axis=0)

        coeffs = margins.astype(BF16)
        coeffs = spread(coeffs, DOM).reshape(n_locked // groups, groups * rows)
        coeffs = spread(coeffs, "x")
        coeffs = coeffs.reshape(n_x, n_locked // groups, groups * rows)
        other = lax.ppermute(coeffs, "core", swap)
        first = jnp.where(core == 0, coeffs, other)
        second = jnp.where(core == 0, other, coeffs)
        coeffs = jnp.stack([first, second], axis=1).reshape(n_locked, groups * rows)
        correction = lax.dot_general(
            coeffs, locked_flat, (((0,), (0,)), ((), ())), preferred_element_type=F32
        )
        orthogonal = (moved.astype(F32) - correction).astype(BF16)
        outs.append((orthogonal, margins))

    orthogonal = jnp.stack([o.reshape(groups, rows, planes, part) for o, _ in outs], axis=1)
    margins = jnp.stack([m.reshape(-1, groups, rows) for _, m in outs], axis=2)
    return (
        orthogonal.reshape(groups * bands, planes, part),
        margins.reshape(margins.shape[0], groups * bands),
    )


def solution(mesh):
    n_band, n_dom = mesh.devices.shape
    n_y = 4 if n_dom % 4 == 0 else 2
    fine = Mesh(
        mesh.devices.reshape(n_band // 2, 2, n_dom // n_y, n_y), ("x", "core", "z", "y")
    )
    in_specs = (
        P(BAND, DOM, None, None),
        P(DOM, None, None),
        P(DOM, None),
        P(DOM),
        P(DOM),
        P(DOM),
        P(DOM),
        P(None, DOM, BAND),
    )
    out_specs = (P(None, DOM, BAND), P(BAND + DOM, None))
    return jax.shard_map(
        per_device, mesh=fine, in_specs=in_specs, out_specs=out_specs, check_vma=False
    )
```

time: 616 us -> 187 us (0.30); the launches traced: 609 us -> 187 us
  waiting for transfers between devices: 261 us -> 30.8 us
  other arithmetic: 99.9 us -> 2.05 us
  local copies, waits for them, and re-layouts: 123 us -> 26.2 us
  Pallas kernels: 0 us -> 14.1 us
  between operations: 15.1 us -> 1.59 us
  blocking collectives: 56.2 us -> 68.4 us
  starting transfers between devices: 39.3 us -> 28.3 us
    psum x1 -> x0, waiting for transfers between devices: 257 us -> none  [per_device(): lax.psum(lax.dot_general(locked_flat, residual_flat, contract_cells, pref...]
    reduce_sum x2 -> x3, other arithmetic: 76.1 us -> 0.92 us  [the longest x1 0.8 us: per_device(): sums = jnp.sum(spread(sums[:, :2].T[None], DOM), axis=0)]
    all_to_all x0 -> x5, blocking collectives: none -> 68.4 us  [the longest x3 37.5 us: spread(): lax.all_to_all(jnp.broadcast_to(value[None], (size,) + value.shape), axis...]
    psum x1 -> x0, blocking collectives: 56.2 us -> none  [per_device(): lax.psum((jnp.sum(orbital * hamilton, axis=(1, 2, 3)), jnp.sum(orbital *...]
    slice x13 -> x1, local copies, waits for them, and re-layouts: 55.7 us -> 0.08 us  [per_device(): shares[:, 2 * n:3 * n]]
    ppermute x6 -> x8, waiting for transfers between devices: 0.02 us -> 26.8 us  [the longest x1 22.9 us: per_device(): lax.ppermute(to_up, DOM, up)]
    unnamed x18, local copies, waits for them, and re-layouts: 29.6 us -> 14 us
    convert_element_type x4 -> x1, other arithmetic: 15.3 us -> 0.01 us  [per_device(): coeffs = margins.astype(BF16)]
  transfers between devices with their start and end apart: 8 -> 9, of which waited for: 2 -> 4; matrix products, arithmetic and copies ran while one was open for 17% -> 7% of each run, Pallas kernels for 0% -> 4%
where the time goes in v1:
time: 187 us
  blocking collectives  68.4 us (37%)
  waiting for transfers between devices  30.8 us (16%)
  starting transfers between devices  28.3 us (15%)
  local copies, waits for them, and re-layouts  26.2 us (14%)
  matrix products  15.2 us (8%)
  Pallas kernels  14.1 us (8%)
  other arithmetic  2.05 us (1%)
    all_to_all x3, blocking collectives, spread(): lax.all_to_all(jnp.broadcast_to(value[None], (size,) + value.shape), axis...  37.5 us
    ppermute x1, waiting for transfers between devices, per_device(): lax.ppermute(to_up, DOM, up)  22.9 us
    all_to_all x1, blocking collectives, per_device(): share = jnp.sum(lax.all_to_all(pair, 'x', 0, 0, tiled=True), axis=0)  17.3 us
    unnamed x18, local copies, waits for them, and re-layouts  14 us
    all_to_all x1, blocking collectives, per_device(): margins = jnp.sum(lax.all_to_all(share, DOM, 0, 0, tiled=True), axis=0)  13.6 us
    ppermute x1, starting transfers between devices, per_device(): right = lax.ppermute(x, DOM, down)  8.93 us
    all_to_all x1, starting transfers between devices, per_device(): moved = lax.all_to_all(residual, BAND, 0, 0, tiled=True)  7.73 us
    dot_general x1, matrix products, per_device(): lax.dot_general(locked_flat, moved, (((1,), (1,)), ((), ())), preferred_e...  7.59 us
  transfers between devices with their start and end apart: 9, of which 4 were waited for; matrix products, arithmetic and copies ran while one was open for 7% of the time, Pallas kernels for 4%

profile of v1, /device:TPU:1, one launch (start us, length us, event | category | flops | bytes accessed | tf_op | source)
XLA Modules:
  0.0 186.6 jit_solution(17188565382636420619)
XLA Ops:
  0.6 0.0 copy-start
  0.6 0.0 copy-start.7
  0.7 0.0 copy-start.3
  0.7 0.0 copy-start.1
  0.7 0.0 copy-start.6
  0.7 0.0 copy-start.4
  0.7 3.2 %reshape.62.x_ref = bf16[32,18432]{1,0:T(8,128)(2,1)S(1)} reshape(bf16[32,6,48,64]{3,2,1,0:T(8,128)(2,1)} %param.9) | data formatting | bytes 2359296 | tf_op jit(solution)/shard_map/reshape | solution.py:192
  3.9 8.9 %collective-permute-start.1 = (bf16[32,18432]{1,0:T(8,128)(2,1)S(1)}, bf16[32,18432]{1,0:T(8,128)(2,1)}, u32[]{:S(2)}, u32[]{:S(2)}) collective-permute-start(bf16[32,18432]{1,0:T(8,128)(2,1)S(1)} %reshape.62.x_ref), channel_id=1, source_target_pairs={{1,0},{2,1},{3,2},{4,3},{5,4},{6,5},{7,6},{8,7},{9,8},{10,9},{11,1... | collective-permute-start | bytes 3538952 | tf_op jit(solution)/shard_map/ppermute | solution.py:211
  12.8 0.0 collective-permute-start
  12.8 0.0 copy-done.7
  13.5 0.1 fusion.1
  13.6 0.0 copy-done.3
  13.6 0.0 copy-done.1
  13.6 1.6 inner.1
  15.2 0.1 fusion.16
  15.3 0.0 collective-permute-start.2
  15.4 4.9 %collective-permute-start.3 = (f32[32,32]{1,0:T(8,128)S(1)}, f32[32,32]{1,0:T(8,128)S(1)}, u32[]{:S(2)}, u32[]{:S(2)}) collective-permute-start(f32[32,32]{1,0:T(8,128)S(1)} %get-tuple-element.23), channel_id=1, source_target_pairs={{1,0},{2,1},{3,2},{4,3},{5,4},{6,5},{7,6},{8,7},{9,8},{10,9},{11,1... | collective-permute-start | bytes 12296 | tf_op jit(solution)/shard_map/ppermute | solution.py:223
  20.2 22.9 %collective-permute-done.2 = f32[32,32]{1,0:T(8,128)S(1)} collective-permute-done((f32[32,32]{1,0:T(8,128)S(1)}, f32[32,32]{1,0:T(8,128)S(1)}, u32[]{:S(2)}, u32[]{:S(2)}) %collective-permute-start.2) | collective-permute-done | bytes 4128 | tf_op jit(solution)/shard_map/ppermute | solution.py:223
  43.1 0.0 collective-permute-done.3
  43.1 0.0 copy-done.6
  43.1 0.1 fusion.5
  43.2 0.3 collective-permute-start.5
  43.5 1.2 collective-permute-start.4
  44.7 0.1 reshape.63.pot_ref
  44.8 0.0 copy-done
  44.8 0.0 copy-start.2
  44.8 6.3 %local.1.h0_ref = f32[32,18432]{1,0:T(8,128)S(1)} custom-call(bf16[32,18432]{1,0:T(8,128)(2,1)S(1)} %reshape.62.x_ref, f32[1,18432]{1,0:T(1,128)S(1)} %reshape.63.pot_ref, bf16[3,1024,256]{2,1,0:T(8,128)(2,1)S(1)} %copy-done), custom_call_target="tpu_custom_call" | custom-call | tf_op jit(solution)/shard_map/local/pallas_call | solution.py:232
  51.1 0.0 collective-permute-done.5
  51.1 0.0 collective-permute-done.4
  51.2 0.2 fusion.2.sv_ref
  51.3 0.0 collective-permute-done.1.right_ref
  51.4 0.0 collective-permute-done.left_ref
  51.4 4.8 %hamilton.1 = (f32[32,18432]{1,0:T(8,128)S(1)}, f32[32,128]{1,0:T(8,128)S(1)}) custom-call(s32[64]{0:T(128)S(1)} %copy-done.3, f32[32,18432]{1,0:T(8,128)S(1)} %local.1.h0_ref, bf16[32,18432]{1,0:T(8,128)(2,1)S(1)} %reshape.62.x_ref, bf16[32,18432]{1,0:T(8,128)(2,1)} %collective-permute-done.left_ref, bf16[32,18432]{1,0:T(8,128)(2,1)} %collective-permute-done.1.right_ref, ...), custom_call_target="tpu_custom_call" | custom-call | tf_op jit(solution)/shard_map/hamilton/pallas_call | solution.py:242
  56.2 0.6 copy.49
  56.8 0.7 broadcast_in_dim.17
  57.5 13.9 %all_to_all.30 = f32[32,1,2,32]{3,2,1,0:T(2,128)} all-to-all(f32[32,1,2,32]{3,2,1,0:T(2,128)S(1)} %broadcast_in_dim.17), channel_id=1, replica_groups=mesh['x'=4,'core'=2,'z'=8,'y'=4] {'z','y'}, dimensions={0} | all-to-all | bytes 16384 | tf_op jit(solution)/shard_map/all_to_all | solution.py:169
  71.4 0.8 reduce_sum.29
  72.2 0.5 fusion.14
  72.7 0.7 copy.51.e_ref
  73.5 1.4 residual.1
  74.9 7.7 %all-to-all-start.1 = ((bf16[8,32,2304]{2,1,0:T(8,128)(2,1)}), bf16[8,32,2304]{2,1,0:T(8,128)(2,1)S(1)}, u32[]{:S(2)}, u32[]{:S(2)}) async-start(bf16[8,32,2304]{2,1,0:T(8,128)(2,1)} %residual.1), calls=%async_computation.1 | async-start | bytes 2359296 | tf_op jit(solution)/shard_map/all_to_all | solution.py:265
  82.6 12.5 %copy.52 = bf16[2048,6,384]{0,2,1:T(8,128)(2,1)} copy(bf16[2048,6,384]{2,0,1:T(8,128)(2,1)} %param.16) | data formatting | bytes 18874368 | tf_op args[7]
  95.1 4.0 %all-to-all-done.1 = bf16[8,32,2304]{2,1,0:T(8,128)(2,1)S(1)} async-done(((bf16[8,32,2304]{2,1,0:T(8,128)(2,1)}), bf16[8,32,2304]{2,1,0:T(8,128)(2,1)S(1)}, u32[]{:S(2)}, u32[]{:S(2)}) %all-to-all-start.1) | async-done | bytes 1179680 | tf_op jit(solution)/shard_map/all_to_all | solution.py:265
  99.1 7.6 %convolution_bitcast_fusion = f32[2048,256]{0,1:T(8,128)} fusion(bf16[256,2304]{1,0:T(8,128)(2,1)S(1)} %bitcast.37, bf16[2048,2304]{0,1:T(8,128)(2,1)} %bitcast.34), kind=kOutput, calls=%fused_computation.2 | convolution fusion | flops 2415919104 | bytes 12713984 | tf_op jit(solution)/shard_map/dot_general | solution.py:268
  106.7 3.0 %reshape.66 = f32[4,2,256,256]{2,1,0,3:T(2,128)S(1)} reshape(f32[2048,256]{0,1:T(8,128)} %convolution_bitcast_fusion) | data formatting | bytes 4194304 | tf_op jit(solution)/shard_map/reshape | solution.py:271
  109.7 1.8 constant_dynamic-slice_fusion.1
  111.5 0.2 copy.64
  111.7 1.0 collective-permute-start.6
  112.7 2.3 %collective-permute-done.6 = f32[4,256,256]{1,2,0:T(8,128)S(1)} collective-permute-done((f32[4,256,256]{1,2,0:T(8,128)S(1)}, f32[4,256,256]{1,2,0:T(8,128)S(1)}, u32[]{:S(2)}, u32[]{:S(2)}) %collective-permute-start.6) | collective-permute-done | bytes 1048608 | tf_op jit(solution)/shard_map/ppermute | solution.py:274
  115.0 0.2 bitcast_add_fusion
  115.2 17.3 %all_to_all.31 = f32[4,256,256]{1,2,0:T(8,128)S(1)} all-to-all(f32[4,256,256]{1,2,0:T(8,128)S(1)} %bitcast_add_fusion), channel_id=1, replica_groups=mesh['x'=4,'core'=2,'z'=8,'y'=4] {'x'}, dimensions={0} | all-to-all | bytes 2097152 | tf_op jit(solution)/shard_map/all_to_all | solution.py:275
  132.5 0.1 reduce_sum.31
  132.6 0.1 copy.56
  132.7 13.6 %all_to_all.32 = f32[32,8,256]{2,1,0:T(8,128)S(1)} all-to-all(f32[32,8,256]{2,1,0:T(8,128)S(1)} %bitcast.41), channel_id=1, replica_groups=mesh['x'=4,'core'=2,'z'=8,'y'=4] {'z','y'}, dimensions={0} | all-to-all | bytes 524288 | tf_op jit(solution)/shard_map/all_to_all | solution.py:277
  146.3 0.0 copy-start.5
  146.4 14.3 %all_to_all.33 = bf16[32,8,256]{2,1,0:T(8,128)(2,1)S(1)} all-to-all(bf16[32,8,256]{2,1,0:T(8,128)(2,1)S(1)} %broadcast_in_dim.18), channel_id=1, replica_groups=mesh['x'=4,'core'=2,'z'=8,'y'=4] {'z','y'}, dimensions={0} | all-to-all | bytes 262144 | tf_op jit(solution)/shard_map/all_to_all | solution.py:169
  160.7 9.3 %all_to_all.34 = bf16[4,256,256]{2,1,0:T(8,128)(2,1)S(1)} all-to-all(bf16[4,256,256]{2,1,0:T(8,128)(2,1)S(1)} %broadcast_in_dim.20), channel_id=1, replica_groups=mesh['x'=4,'core'=2,'z'=8,'y'=4] {'x'}, dimensions={0} | all-to-all | bytes 1048576 | tf_op jit(solution)/shard_map/all_to_all | solution.py:169
  170.1 4.4 %collective-permute-start.7 = (bf16[4,256,256]{2,1,0:T(8,128)(2,1)S(1)}, bf16[4,256,256]{2,1,0:T(8,128)(2,1)S(1)}, u32[]{:S(2)}, u32[]{:S(2)}) collective-permute-start(bf16[4,256,256]{2,1,0:T(8,128)(2,1)S(1)} %all_to_all.34), channel_id=1, source_target_pairs={{0,32},{32,0},{1,33},{33,1},{2,34},{34,2},{3,35},{35,3},{4,36},{36... | collective-permute-start | bytes 1572872 | tf_op jit(solution)/shard_map/ppermute | solution.py:283
  174.4 1.5 collective-permute-done.7
  176.0 0.1 select_bitcast_fusion.1
  176.1 0.1 pad_maximum_fusion
  176.2 7.4 %fusion = bf16[256,2304]{1,0:T(8,128)(2,1)} fusion(bf16[2048,256]{1,0:T(8,128)(2,1)S(1)} %bitcast.40, bf16[2048,2304]{0,1:T(8,128)(2,1)} %bitcast.35, bf16[256,2304]{1,0:T(8,128)(2,1)S(1)} %bitcast.38), kind=kOutput, calls=%fused_computation.1 | convolution fusion | flops 2417688576 | bytes 12845056 | tf_op jit(solution)/shard_map/dot_general | solution.py:287
  183.6 1.6 copy.58
  185.2 1.4 copy.59
  (11 shorter events, 0.1 us)
Async XLA Ops:
  0.6 44.2 %copy-start = (bf16[3,1024,256]{2,1,0:T(8,128)(2,1)S(1)}, bf16[3,1024,256]{2,1,0:T(8,128)(2,1)}, u32[]{:S(2)}) copy-start(bf16[3,1024,256]{2,1,0:T(8,128)(2,1)} %constant.72.clone.w_ref) | copy-start | bytes 4718596
  0.6 12.2 %copy-start.7 = (s32[64]{0:T(128)S(1)}, s32[64]{0:T(128)}, u32[]{:S(2)}) copy-start(s32[64]{0:T(128)} %param.14) | copy-start | bytes 772
  0.7 13.0 %copy-start.3 = (s32[64]{0:T(128)S(1)}, s32[64]{0:T(128)}, u32[]{:S(2)}) copy-start(s32[64]{0:T(128)} %block_ref.3) | copy-start | bytes 772
  0.7 13.0 %copy-start.1 = (f32[64,128]{1,0:T(8,128)S(1)}, f32[64,128]{1,0:T(8,128)}, u32[]{:S(2)}) copy-start(f32[64,128]{1,0:T(8,128)} %proj_ref.3) | copy-start | bytes 98308
  0.7 42.4 %copy-start.6 = (f32[32]{0:T(128)S(1)}, f32[32]{0:T(128)}, u32[]{:S(2)}) copy-start(f32[32]{0:T(128)} %param.12) | copy-start | bytes 388
  0.7 44.0 %copy-start.4 = (f32[6,48,64]{2,1,0:T(8,128)S(1)}, f32[6,48,64]{2,1,0:T(8,128)}, u32[]{:S(2)}) copy-start(f32[6,48,64]{2,1,0:T(8,128)} %param.10) | copy-start | bytes 221188
  3.9 47.5 %collective-permute-start.1 = (bf16[32,18432]{1,0:T(8,128)(2,1)S(1)}, bf16[32,18432]{1,0:T(8,128)(2,1)}, u32[]{:S(2)}, u32[]{:S(2)}) collective-permute-start(bf16[32,18432]{1,0:T(8,128)(2,1)S(1)} %reshape.62.x_ref), channel_id=1, source_target_pairs={{1,0},{2,1},{3,2},{4,3},{5,4},{6,5},{7,6},{8,7},{9,8},{10,9},{11,1... | collective-permute-start | bytes 3538952 | tf_op jit(solution)/shard_map/ppermute | solution.py:211
  12.8 38.6 %collective-permute-start = (bf16[32,18432]{1,0:T(8,128)(2,1)S(1)}, bf16[32,18432]{1,0:T(8,128)(2,1)}, u32[]{:S(2)}, u32[]{:S(2)}) collective-permute-start(bf16[32,18432]{1,0:T(8,128)(2,1)S(1)} %reshape.62.x_ref), channel_id=1, source_target_pairs={{0,1},{1,2},{2,3},{3,4},{4,5},{5,6},{6,7},{7,8},{8,9},{9,10},{10,1... | collective-permute-start | bytes 3538952 | tf_op jit(solution)/shard_map/ppermute | solution.py:210
  15.3 27.8 %collective-permute-start.2 = (f32[32,32]{1,0:T(8,128)S(1)}, f32[32,32]{1,0:T(8,128)S(1)}, u32[]{:S(2)}, u32[]{:S(2)}) collective-permute-start(f32[32,32]{1,0:T(8,128)S(1)} %get-tuple-element.22), channel_id=1, source_target_pairs={{0,1},{1,2},{2,3},{3,4},{4,5},{5,6},{6,7},{7,8},{8,9},{9,10},{10,1... | collective-permute-start | bytes 12296 | tf_op jit(solution)/shard_map/ppermute | solution.py:223
  15.4 27.8 %collective-permute-start.3 = (f32[32,32]{1,0:T(8,128)S(1)}, f32[32,32]{1,0:T(8,128)S(1)}, u32[]{:S(2)}, u32[]{:S(2)}) collective-permute-start(f32[32,32]{1,0:T(8,128)S(1)} %get-tuple-element.23), channel_id=1, source_target_pairs={{1,0},{2,1},{3,2},{4,3},{5,4},{6,5},{7,6},{8,7},{9,8},{10,9},{11,1... | collective-permute-start | bytes 12296 | tf_op jit(solution)/shard_map/ppermute | solution.py:223
  43.2 7.9 %collective-permute-start.5 = (f32[32,32]{1,0:T(8,128)S(1)}, f32[32,32]{1,0:T(8,128)S(1)}, u32[]{:S(2)}, u32[]{:S(2)}) collective-permute-start(f32[32,32]{1,0:T(8,128)S(1)} %fusion.5), channel_id=1, source_target_pairs={{1,0},{2,1},{3,2},{4,3},{5,4},{6,5},{7,6},{8,7},{9,8},{10,9},{11,1... | collective-permute-start | bytes 12296 | tf_op jit(solution)/shard_map/ppermute | solution.py:226
  43.5 7.6 %collective-permute-start.4 = (f32[32,32]{1,0:T(8,128)S(1)}, f32[32,32]{1,0:T(8,128)S(1)}, u32[]{:S(2)}, u32[]{:S(2)}) collective-permute-start(f32[32,32]{1,0:T(8,128)S(1)} %fusion.5), channel_id=1, source_target_pairs={{0,1},{1,2},{2,3},{3,4},{4,5},{5,6},{6,7},{7,8},{8,9},{9,10},{10,1... | collective-permute-start | bytes 12296 | tf_op jit(solution)/shard_map/ppermute | solution.py:226
  44.8 6.6 %copy-start.2 = (f32[64,128]{1,0:T(8,128)S(1)}, f32[64,128]{1,0:T(8,128)}, u32[]{:S(2)}) copy-start(f32[64,128]{1,0:T(8,128)} %proj_ref.3) | copy-start | bytes 98308
  74.9 24.2 %all-to-all-start.1 = ((bf16[8,32,2304]{2,1,0:T(8,128)(2,1)}), bf16[8,32,2304]{2,1,0:T(8,128)(2,1)S(1)}, u32[]{:S(2)}, u32[]{:S(2)}) async-start(bf16[8,32,2304]{2,1,0:T(8,128)(2,1)} %residual.1), calls=%async_computation.1 | async-start | bytes 2359296 | tf_op jit(solution)/shard_map/all_to_all | solution.py:265
  111.7 3.2 %collective-permute-start.6 = (f32[4,256,256]{1,2,0:T(8,128)S(1)}, f32[4,256,256]{1,2,0:T(8,128)S(1)}, u32[]{:S(2)}, u32[]{:S(2)}) collective-permute-start(f32[4,256,256]{1,2,0:T(8,128)S(1)} %bitcast.39), channel_id=1, source_target_pairs={{0,32},{32,0},{1,33},{33,1},{2,34},{34,2},{3,35},{35,3},{4,36},{36... | collective-permute-start | bytes 3145736 | tf_op jit(solution)/shard_map/ppermute | solution.py:274
  146.3 29.7 %copy-start.5 = (f32[8,256]{1,0:T(8,128)}, f32[8,256]{1,0:T(8,128)S(1)}, u32[]{:S(2)}) copy-start(f32[8,256]{1,0:T(8,128)S(1)} %reduce_sum.32) | copy-start | bytes 24580
  170.1 5.9 %collective-permute-start.7 = (bf16[4,256,256]{2,1,0:T(8,128)(2,1)S(1)}, bf16[4,256,256]{2,1,0:T(8,128)(2,1)S(1)}, u32[]{:S(2)}, u32[]{:S(2)}) collective-permute-start(bf16[4,256,256]{2,1,0:T(8,128)(2,1)S(1)} %all_to_all.34), channel_id=1, source_target_pairs={{0,32},{32,0},{1,33},{33,1},{2,34},{34,2},{3,35},{35,3},{4,36},{36... | collective-permute-start | bytes 1572872 | tf_op jit(solution)/shard_map/ppermute | solution.py:283

commit v2 on v1

v2 whole, which is shorter than its diff:
```python
import functools

import jax
import jax.numpy as jnp
import numpy as np
from jax import lax
from jax.experimental import pallas as pl
from jax.experimental.pallas import tpu as pltpu
from jax.sharding import Mesh
from jax.sharding import PartitionSpec as P

BS = 128

COEFFS = (
    -5369.0 / 1800.0,
    12.0 / 7.0,
    -15.0 / 56.0,
    10.0 / 189.0,
    -1.0 / 112.0,
    2.0 / 825.0,
    -1.0 / 5544.0,
)
HALF = tuple(-0.5 * c for c in COEFFS)
WIDTH = 6
DOM = ("z", "y")
BAND = ("x", "core")
F32 = jnp.float32
BF16 = jnp.bfloat16
VMEM = pl.BlockSpec(memory_space=pltpu.VMEM)
SMEM = pl.BlockSpec(memory_space=pltpu.SMEM)


def params(mib):
    return pltpu.CompilerParams(vmem_limit_bytes=mib * 1024 * 1024)


def cost(microseconds):
    return pl.CostEstimate(
        flops=0, transcendentals=0, bytes_accessed=int(microseconds * 3_000_000)
    )


@functools.lru_cache
def plane_weights(width_y):
    src = np.arange(1024)
    dst = np.arange(256)
    dz = np.abs((src // width_y - 2 * (384 // (2 * width_y)))[:, None] - (dst // width_y)[None])
    dy = np.abs((src % width_y)[:, None] - (dst % width_y)[None])
    dy = np.minimum(dy, width_y - dy)
    table = np.zeros(2048)
    table[1 : WIDTH + 1] = HALF[1:]
    full = np.where(dy == 0, table[dz], 0.0) + np.where(dz == 0, table[dy], 0.0)
    terms = []
    for _ in range(3):
        term = full.astype(np.float32).astype(BF16)
        terms.append(term)
        full = full - term.astype(np.float64)
    return np.stack(terms)


def inner_kernel(
    planes, block_ref, x_ref, proj_ref, onehot_ref, coupling_ref, share_ref, raw_ref, pack_ref
):
    rows = x_ref.shape[0]
    slots = proj_ref.shape[0]
    lane = lax.broadcasted_iota(jnp.int32, (rows, BS), 1)

    def body(s, acc):
        start = pl.multiple_of(block_ref[s] * BS, BS)
        cells = x_ref[:, pl.ds(start, BS)].astype(F32)
        total = jnp.sum(cells * proj_ref[pl.ds(s, 1), :], axis=1, keepdims=True)
        return jnp.where(lane == s, total, acc)

    acc = lax.fori_loop(0, slots, body, jnp.zeros((rows, BS), F32), unroll=8)
    raw_ref[...] = acc
    share_ref[:rows] = jnp.dot(
        acc, onehot_ref[...], precision=lax.Precision.HIGHEST, preferred_element_type=F32
    )
    share_ref[rows:] = coupling_ref[...]

    parts, _, width = pack_ref.shape
    plane = x_ref.shape[1] // planes
    part = plane // parts
    for c in range(parts):
        for p in range(planes):
            src = p * plane + c * part
            pack_ref[c, :, p * part : (p + 1) * part] = x_ref[:, src : src + part]


def local_kernel(planes, x_ref, pot_ref, w_ref, out_ref, den_ref, pad_ref):
    rows = x_ref.shape[0]
    plane = x_ref.shape[1] // planes
    zeros = jnp.zeros((planes * rows, 384), BF16)
    pad_ref[:, :384] = zeros
    pad_ref[:, 384 + plane :] = zeros
    for p in range(planes):
        pad_ref[p * rows : (p + 1) * rows, 384 : 384 + plane] = x_ref[:, p * plane : (p + 1) * plane]

    def body(step, den):
        start = pl.multiple_of(step * 256, 256)
        window = pad_ref[:, pl.ds(start, 1024)]
        acc = jnp.dot(window, w_ref[0], preferred_element_type=F32)
        acc += jnp.dot(window, w_ref[1], preferred_element_type=F32)
        acc += jnp.dot(window, w_ref[2], preferred_element_type=F32)
        mid = [window[p * rows : (p + 1) * rows, 384:640].astype(F32) for p in range(planes)]
        for p in range(planes):
            where = pl.multiple_of(p * plane + start, 256)
            value = acc[p * rows : (p + 1) * rows]
            value += (pot_ref[:, pl.ds(where, 256)] + 3.0 * HALF[0]) * mid[p]
            for q in range(planes):
                if q != p and abs(q - p) <= WIDTH:
                    value += HALF[abs(q - p)] * mid[q]
            out_ref[:, pl.ds(where, 256)] = value
            square = mid[p] * mid[p]
            den += square[:, :BS] + square[:, BS:]
        return den

    den_ref[...] = lax.fori_loop(0, plane // 256, body, jnp.zeros((rows, BS), F32))


def hamilton_kernel(
    planes,
    block_ref,
    group_ref,
    h0_ref,
    x_ref,
    left_ref,
    right_ref,
    proj_ref,
    onehot_ref,
    den_ref,
    raw_ref,
    mine_ref,
    left1_ref,
    left2_ref,
    right1_ref,
    right2_ref,
    r_ref,
    nd_ref,
    h_ref,
):
    rows, cells = x_ref.shape
    plane = cells // planes
    slots = proj_ref.shape[0]
    n = BS // 4

    def halo(step, carry):
        sums = []
        for top in range(0, rows, 16):
            pick = slice(top, top + 16)
            before = []
            after = []
            num = carry[top // 16]
            for p in range(planes):
                where = pl.ds(pl.multiple_of(p * plane + step * BS, BS), BS)
                before.append(left_ref[pick, where].astype(F32))
                after.append(right_ref[pick, where].astype(F32))
            for p in range(planes):
                where = pl.ds(pl.multiple_of(p * plane + step * BS, BS), BS)
                value = h0_ref[pick, where]
                for j in range(p, planes):
                    value += HALF[planes + p - j] * before[j]
                for j in range(p + 1):
                    value += HALF[planes + j - p] * after[j]
                h_ref[pick, where] = value
                num += value * x_ref[pick, where].astype(F32)
            sums.append(num)
        return tuple(sums)

    zero = jnp.zeros((16, BS), F32)
    num = lax.fori_loop(0, plane // BS, halo, (zero,) * (rows // 16))
    num = jnp.concatenate(num, axis=0)

    shape = mine_ref.shape
    at = lax.broadcasted_iota(jnp.int32, shape, 1)
    total = mine_ref[...]
    total += jnp.where(at < 2 * n, pltpu.roll(left1_ref[...], 3 * n, 1), 0.0)
    total += jnp.where(at < n, pltpu.roll(left2_ref[...], 2 * n, 1), 0.0)
    total += jnp.where((at >= n) & (at < 3 * n), pltpu.roll(right1_ref[...], n, 1), 0.0)
    total += jnp.where((at >= 2 * n) & (at < 3 * n), pltpu.roll(right2_ref[...], 2 * n, 1), 0.0)
    table = total[:rows] * total[rows : rows + 1]
    value = lax.dot_general(
        table,
        onehot_ref[...],
        (((1,), (1,)), ((), ())),
        precision=lax.Precision.HIGHEST,
        preferred_element_type=F32,
    )
    for s in range(slots):
        where = pl.ds(pl.multiple_of(block_ref[s] * BS, BS), BS)
        h_ref[:, where] += value[:, s : s + 1] * proj_ref[s : s + 1, :]

    num = jnp.sum(num + value * raw_ref[...], axis=1, keepdims=True)
    den = jnp.sum(den_ref[...], axis=1, keepdims=True)
    parts, _, width = r_ref.shape
    part = plane // parts
    energy = jnp.broadcast_to(jnp.where(den > 0.0, num / den, 0.0), (rows, BS))
    for c in range(parts):
        for p in range(planes):
            for j in range(part // BS):
                src = p * plane + c * part + j * BS
                dst = p * part + j * BS
                left = h_ref[:, src : src + BS] - energy * x_ref[:, src : src + BS].astype(F32)
                r_ref[c, :, dst : dst + BS] = left.astype(BF16)

    bands = nd_ref.shape[2]
    lane = lax.broadcasted_iota(jnp.int32, (rows, bands), 1)
    band = lax.broadcasted_iota(jnp.int32, (rows, bands), 0) + group_ref[0] * rows
    for i, column in enumerate((num, den)):
        line = jnp.sum(jnp.where(lane == band, column, 0.0), axis=0, keepdims=True)
        nd_ref[:, i : i + 1, :] = jnp.broadcast_to(line[None], (nd_ref.shape[0], 1, bands))


def margin_kernel(planes, fix, core_ref, locked_ref, *refs):
    if fix:
        h_ref, x_ref, sums_ref, out_ref, r_ref = refs

        @pl.when(pl.program_id(0) == 0)
        def _():
            bands = h_ref.shape[0]
            sums = jnp.sum(sums_ref[...], axis=0)
            own = jnp.where(sums[3:4] > 0.0, sums[2:3] / sums[3:4], 0.0)
            shift = sums[0:1] / sums[1:2] - own
            eye = lax.broadcasted_iota(jnp.int32, (bands, bands), 0) == lax.broadcasted_iota(
                jnp.int32, (bands, bands), 1
            )
            shift = jnp.sum(jnp.where(eye, shift, 0.0), axis=1, keepdims=True)
            for j in range(0, h_ref.shape[1], BS):
                where = slice(j, j + BS)
                value = h_ref[:, where].astype(F32) - shift * x_ref[:, where].astype(F32)
                r_ref[:, where] = value.astype(BF16)

    else:
        r_ref, out_ref = refs
    part = r_ref.shape[1] // planes
    acc = None
    for p in range(planes):
        term = lax.dot_general(
            locked_ref[p, 0, 0],
            r_ref[:, p * part : (p + 1) * part],
            (((1,), (1,)), ((), ())),
            preferred_element_type=F32,
        )
        acc = term if acc is None else acc + term
    out_ref[0] = acc


def clean_kernel(core_ref, locked_ref, mine_ref, other_ref, r_ref, out_ref, turned_ref):
    n_x = mine_ref.shape[0]
    core = core_ref[0]

    @pl.when(pl.program_id(0) == 0)
    def _():
        for i in range(n_x):
            turned_ref[0, i] = mine_ref[i].T
            turned_ref[1, i] = other_ref[i].T

    acc = None
    for side in range(2):
        for i in range(n_x):
            term = jnp.dot(
                turned_ref[side, i],
                locked_ref[0, i, jnp.where(side == 0, core, 1 - core)],
                preferred_element_type=F32,
            )
            acc = term if acc is None else acc + term
    out_ref[0] = (r_ref[...].astype(F32) - acc).astype(BF16)


def ring(size):
    up = [(i, (i + 1) % size) for i in range(size)]
    return up, [(j, i) for i, j in up]


def spread(value, axis):
    size = lax.axis_size(axis)
    return lax.all_to_all(
        jnp.broadcast_to(value[None], (size,) + value.shape), axis, 0, 0, tiled=True
    )


def per_device(
    orbitals, potential, projectors, coupling, slot_block, slot_projector, slot_count, locked
):
    rows, planes, depth_z, width_y = orbitals.shape
    plane = depth_z * width_y
    cells = planes * plane
    domains = lax.axis_size(DOM)
    groups = lax.axis_size(BAND)
    n_x = lax.axis_size("x")
    core = lax.axis_index("core").astype(jnp.int32)
    here = lax.axis_index(DOM)
    group = lax.axis_index(BAND).astype(jnp.int32)
    slots = slot_block.shape[0]
    n = coupling.shape[0]
    part = plane // groups
    width = planes * part
    n_locked = locked.shape[0]
    bands = groups * rows
    share_rows = n_locked // groups
    up, down = ring(domains)
    up2 = [(i, (i + 2) % domains) for i in range(domains)]
    down2 = [(j, i) for i, j in up2]
    swap = [(0, 1), (1, 0)]

    x = orbitals.reshape(rows, cells)
    left = lax.ppermute(x, DOM, up)
    right = lax.ppermute(x, DOM, down)

    pot = potential.reshape(1, cells)
    weights = jnp.asarray(plane_weights(width_y))
    active = jnp.arange(slots, dtype=jnp.int32) < slot_count[0]
    relative = (slot_projector // n - here + domains) % domains
    section = jnp.where(relative == 0, 1, jnp.where(relative == 1, 2, 0))
    column = section * n + slot_projector % n
    column = jnp.where(active, column, BS)
    column = jnp.pad(column, (0, BS - slots), constant_values=BS)
    onehot = (column[:, None] == jnp.arange(BS, dtype=jnp.int32)[None, :]).astype(F32)
    coupling_rows = jnp.pad(coupling[None], ((0, 7), (n, BS - 2 * n)))

    shares, raw, packed = pl.pallas_call(
        functools.partial(inner_kernel, planes),
        out_shape=(
            jax.ShapeDtypeStruct((rows + 8, BS), F32),
            jax.ShapeDtypeStruct((rows, BS), F32),
            jax.ShapeDtypeStruct((groups, rows, width), BF16),
        ),
        in_specs=[SMEM, VMEM, VMEM, VMEM, VMEM],
        out_specs=(VMEM, VMEM, VMEM),
        compiler_params=params(8),
        cost_estimate=cost(3),
        name="inner",
    )(slot_block, x, projectors, onehot, coupling_rows)
    left1 = lax.ppermute(shares, DOM, up)
    left2 = lax.ppermute(shares, DOM, up2)
    right1 = lax.ppermute(shares, DOM, down)
    right2 = lax.ppermute(shares, DOM, down2)
    x_moved = lax.all_to_all(packed, BAND, 0, 0, tiled=True).reshape(bands, width)

    h0, den = pl.pallas_call(
        functools.partial(local_kernel, planes),
        out_shape=(
            jax.ShapeDtypeStruct((rows, cells), F32),
            jax.ShapeDtypeStruct((rows, BS), F32),
        ),
        in_specs=[VMEM, VMEM, VMEM],
        out_specs=(VMEM, VMEM),
        scratch_shapes=[pltpu.VMEM((planes * rows, plane + 768), BF16)],
        compiler_params=params(24),
        cost_estimate=cost(7),
        name="local",
    )(x, pot, weights)

    sent, sums = pl.pallas_call(
        functools.partial(hamilton_kernel, planes),
        out_shape=(
            jax.ShapeDtypeStruct((groups, rows, width), BF16),
            jax.ShapeDtypeStruct((domains, 2, bands), F32),
        ),
        in_specs=[SMEM, SMEM] + [VMEM] * 13,
        out_specs=(VMEM, VMEM),
        scratch_shapes=[pltpu.VMEM((rows, cells), F32)],
        compiler_params=params(24),
        cost_estimate=cost(5),
        name="hamilton",
    )(
        slot_block,
        group.reshape(1),
        h0,
        x,
        left,
        right,
        projectors,
        onehot,
        den,
        raw,
        shares,
        left1,
        left2,
        right1,
        right2,
    )
    moved = lax.all_to_all(sent, BAND, 0, 0, tiled=True).reshape(bands, width)
    whole = jnp.sum(lax.all_to_all(sums, DOM, 0, 0, tiled=True), axis=0)
    sums = spread(jnp.concatenate([whole, sums[0]], axis=0), BAND)
    sums = sums.reshape(groups, 4, bands)

    by_plane = locked.transpose(1, 0, 2).reshape(planes, n_x, 2, share_rows, part)

    def margin_call(fix, side, *operands):
        full = pl.BlockSpec((bands, width), lambda i, c: (0, 0))
        out_spec = pl.BlockSpec((1, share_rows, bands), lambda i, c: (i, 0, 0))
        out_shape = jax.ShapeDtypeStruct((n_x, share_rows, bands), F32)
        extra = [pl.BlockSpec((groups, 4, bands), lambda i, c: (0, 0, 0))]
        return pl.pallas_call(
            functools.partial(margin_kernel, planes, fix),
            out_shape=(out_shape, jax.ShapeDtypeStruct((bands, width), BF16)) if fix else out_shape,
            grid_spec=pltpu.PrefetchScalarGridSpec(
                num_scalar_prefetch=1,
                grid=(n_x,),
                in_specs=[
                    pl.BlockSpec((planes, 1, 1, share_rows, part), lambda i, c: (0, i, c[0], 0, 0))
                ]
                + ([full, full] + extra if fix else [full]),
                out_specs=(out_spec, full) if fix else out_spec,
            ),
            compiler_params=params(24),
            cost_estimate=cost(3),
            name="margin",
        )(side.reshape(1), by_plane, *operands)

    given, residual = margin_call(True, 1 - core, moved, x_moved, sums)
    given = lax.ppermute(given, "core", swap)
    kept = margin_call(False, core, residual)
    pair = kept + given
    share = jnp.sum(lax.all_to_all(pair, "x", 0, 0, tiled=True), axis=0)
    share = share.reshape(domains, -1, bands)
    margins = jnp.sum(lax.all_to_all(share, DOM, 0, 0, tiled=True), axis=0)

    coeffs = spread(margins.astype(BF16), DOM).reshape(share_rows, bands)
    coeffs = spread(coeffs, "x").reshape(n_x, share_rows, bands)
    other = lax.ppermute(coeffs, "core", swap)
    whole_block = pl.BlockSpec((n_x, share_rows, bands), lambda p, c: (0, 0, 0))
    orthogonal = pl.pallas_call(
        clean_kernel,
        out_shape=jax.ShapeDtypeStruct((planes, bands, part), BF16),
        grid_spec=pltpu.PrefetchScalarGridSpec(
            num_scalar_prefetch=1,
            grid=(planes,),
            in_specs=[
                pl.BlockSpec((1, n_x, 2, share_rows, part), lambda p, c: (p, 0, 0, 0, 0)),
                whole_block,
                whole_block,
                pl.BlockSpec((bands, part), lambda p, c: (0, p)),
            ],
            out_specs=pl.BlockSpec((1, bands, part), lambda p, c: (p, 0, 0)),
            scratch_shapes=[pltpu.VMEM((2, n_x, bands, share_rows), BF16)],
        ),
        compiler_params=params(24),
        cost_estimate=cost(5),
        name="clean",
    )(core.reshape(1), by_plane, coeffs, other, residual)
    return orthogonal.transpose(1, 0, 2), margins


def solution(mesh):
    n_band, n_dom = mesh.devices.shape
    n_y = 4 if n_dom % 4 == 0 else 2
    fine = Mesh(
        mesh.devices.reshape(n_band // 2, 2, n_dom // n_y, n_y), ("x", "core", "z", "y")
    )
    in_specs = (
        P(BAND, DOM, None, None),
        P(DOM, None, None),
        P(DOM, None),
        P(DOM),
        P(DOM),
        P(DOM),
        P(DOM),
        P(None, DOM, BAND),
    )
    out_specs = (P(None, DOM, BAND), P(BAND + DOM, None))
    return jax.shard_map(
        per_device, mesh=fine, in_specs=in_specs, out_specs=out_specs, check_vma=False
    )
```

time: 187 us -> 208 us (1.11)
  waiting for transfers between devices: 30.8 us -> 52.8 us
  matrix products: 15.2 us -> 0 us
  Pallas kernels: 14.1 us -> 26.6 us
  local copies, waits for them, and re-layouts: 26.2 us -> 15.2 us
  blocking collectives: 68.4 us -> 78.4 us
  starting transfers between devices: 28.3 us -> 32.1 us
    all_to_all x1 -> x2, waiting for transfers between devices: 3.99 us -> 33 us  [the longest x1 16.5 us: per_device(): moved = lax.all_to_all(sent, BAND, 0, 0, tiled=True).reshape(bands, width)]
    all_to_all x0 -> x1, blocking collectives: none -> 15.3 us  [per_device(): whole = jnp.sum(lax.all_to_all(sums, DOM, 0, 0, tiled=True), axis=0)]
    dot_general x3 -> x0, matrix products: 15.2 us -> none  [the longest x1 7.59 us: per_device(): lax.dot_general(locked_flat, moved, (((1,), (1,)), ((), ())), preferred_e...]
    pallas_call x3 -> x5, Pallas kernels: 9.28 us -> 20.7 us  [the longest x1 6.29 us: per_device(): pl.pallas_call(functools.partial(local_kernel, planes), out_shape=(jax.Sh...]
    ppermute x5, waiting for transfers between devices: 25.2 us -> 18.3 us  [the longest x1 18.3 us: per_device(): left1 = lax.ppermute(shares, DOM, up)]
    all_to_all x3, blocking collectives: 37.5 us -> 32.2 us  [spread(): lax.all_to_all(jnp.broadcast_to(value[None], (size,) + value.shape), axis...]
    all_to_all x1 -> x2, starting transfers between devices: 7.73 us -> 11.8 us  [the longest x1 7.59 us: per_device(): lax.all_to_all(packed, BAND, 0, 0, tiled=True).reshape(bands, width)]
    reshape x2 -> x1, local copies, waits for them, and re-layouts: 6.21 us -> 3.14 us  [per_device(): x = orbitals.reshape(rows, cells)]
  transfers between devices with their start and end apart: 9 -> 10, of which waited for: 4 -> 4; matrix products, arithmetic and copies ran while one was open for 7% -> 0% of each run, Pallas kernels for 4% -> 6%
where the time goes in v2:
time: 208 us; the launch traced here: 207 us
  blocking collectives  78.4 us (38%)
  waiting for transfers between devices  52.8 us (25%)
  starting transfers between devices  32.1 us (15%)
  Pallas kernels  26.6 us (13%)
  local copies, waits for them, and re-layouts  15.2 us (7%)
    all_to_all x3, blocking collectives, spread(): lax.all_to_all(jnp.broadcast_to(value[None], (size,) + value.shape), axis...  32.2 us
    ppermute x1, waiting for transfers between devices, per_device(): left1 = lax.ppermute(shares, DOM, up)  18.3 us
    all_to_all x1, blocking collectives, per_device(): share = jnp.sum(lax.all_to_all(pair, 'x', 0, 0, tiled=True), axis=0)  17.4 us
    all_to_all x1, waiting for transfers between devices, per_device(): moved = lax.all_to_all(sent, BAND, 0, 0, tiled=True).reshape(bands, width)  16.5 us
    all_to_all x1, waiting for transfers between devices, per_device(): lax.all_to_all(packed, BAND, 0, 0, tiled=True).reshape(bands, width)  16.4 us
    all_to_all x1, blocking collectives, per_device(): whole = jnp.sum(lax.all_to_all(sums, DOM, 0, 0, tiled=True), axis=0)  15.3 us
    all_to_all x1, blocking collectives, per_device(): margins = jnp.sum(lax.all_to_all(share, DOM, 0, 0, tiled=True), axis=0)  13.6 us
    unnamed x22, local copies, waits for them, and re-layouts  11.8 us
  transfers between devices with their start and end apart: 10, of which 4 were waited for; matrix products, arithmetic and copies ran while one was open for 0% of the time, Pallas kernels for 6%

profile of v2, /device:TPU:1, one launch (start us, length us, event | category | flops | bytes accessed | tf_op | source)
XLA Modules:
  0.0 207.1 jit_solution(1541222777924375169)
XLA Ops:
  0.6 0.0 copy-start.10
  0.6 0.0 copy-start.9
  0.7 0.0 copy-start.4
  0.7 0.0 copy-start.6
  0.7 0.0 copy-start.7
  0.7 3.1 %reshape.42.x_ref = bf16[32,18432]{1,0:T(8,128)(2,1)S(1)} reshape(bf16[32,6,48,64]{3,2,1,0:T(8,128)(2,1)} %param.9) | data formatting | bytes 2359296 | tf_op jit(solution)/shard_map/reshape | solution.py:306
  3.8 0.0 copy-start.3
  3.8 2.2 %collective-permute-start = (bf16[32,18432]{1,0:T(8,128)(2,1)S(1)}, bf16[32,18432]{1,0:T(8,128)(2,1)}, u32[]{:S(2)}, u32[]{:S(2)}) collective-permute-start(bf16[32,18432]{1,0:T(8,128)(2,1)S(1)} %reshape.42.x_ref), channel_id=1, source_target_pairs={{0,1},{1,2},{2,3},{3,4},{4,5},{5,6},{6,7},{7,8},{8,9},{9,10},{10,1... | collective-permute-start | bytes 3538952 | tf_op jit(solution)/shard_map/ppermute | solution.py:307
  6.0 6.8 %collective-permute-start.1 = (bf16[32,18432]{1,0:T(8,128)(2,1)S(1)}, bf16[32,18432]{1,0:T(8,128)(2,1)}, u32[]{:S(2)}, u32[]{:S(2)}) collective-permute-start(bf16[32,18432]{1,0:T(8,128)(2,1)S(1)} %reshape.42.x_ref), channel_id=1, source_target_pairs={{1,0},{2,1},{3,2},{4,3},{5,4},{6,5},{7,6},{8,7},{9,8},{10,9},{11,1... | collective-permute-start | bytes 3538952 | tf_op jit(solution)/shard_map/ppermute | solution.py:308
  13.5 0.0 copy-done.10
  13.6 0.0 copy-done.9
  13.6 0.1 pad.9.coupling_ref
  13.7 0.1 fusion.onehot_ref
  13.7 0.0 copy-done.4
  13.7 0.0 copy-done.6
  13.8 2.6 %inner.1 = (f32[40,128]{1,0:T(8,128)S(1)}, f32[32,128]{1,0:T(8,128)S(1)}, bf16[8,32,2304]{2,1,0:T(8,128)(2,1)}) custom-call(s32[64]{0:T(128)S(1)} %copy-done.6, bf16[32,18432]{1,0:T(8,128)(2,1)S(1)} %reshape.42.x_ref, f32[64,128]{1,0:T(8,128)S(1)} %copy-done.4, f32[128,128]{1,0:T(8,128)S(1)} %fusion.onehot_ref, f32[8,128]{1,0:T(8,128)S(1)} %pad.9.coupling_ref), custom_call_target="tpu_custom_call" | custom-call | bytes 9000000 | tf_op jit(solution)/shard_map/inner/pallas_call | solution.py:321
  16.3 0.0 collective-permute-start.2
  16.3 0.0 collective-permute-start.3
  16.3 4.8 %collective-permute-start.4 = (f32[40,128]{1,0:T(8,128)S(1)}, f32[40,128]{1,0:T(8,128)S(1)}, u32[]{:S(2)}, u32[]{:S(2)}) collective-permute-start(f32[40,128]{1,0:T(8,128)S(1)} %get-tuple-element.14.mine_ref), channel_id=1, source_target_pairs={{1,0},{2,1},{3,2},{4,3},{5,4},{6,5},{7,6},{8,7},{9,8},{10,9},{11,1... | collective-permute-start | bytes 61448 | tf_op jit(solution)/shard_map/ppermute | solution.py:336
  21.1 18.3 %collective-permute-done.2.left1_ref = f32[40,128]{1,0:T(8,128)S(1)} collective-permute-done((f32[40,128]{1,0:T(8,128)S(1)}, f32[40,128]{1,0:T(8,128)S(1)}, u32[]{:S(2)}, u32[]{:S(2)}) %collective-permute-start.2) | collective-permute-done | bytes 20512 | tf_op jit(solution)/shard_map/ppermute | solution.py:334
  39.4 1.0 collective-permute-start.5
  40.4 0.0 copy-done.7
  40.4 0.1 reshape.43.pot_ref
  40.6 0.0 copy-done.3
  40.6 6.3 %local.1 = (f32[32,18432]{1,0:T(8,128)S(1)}, f32[32,128]{1,0:T(8,128)S(1)}) custom-call(bf16[32,18432]{1,0:T(8,128)(2,1)S(1)} %reshape.42.x_ref, f32[1,18432]{1,0:T(1,128)S(1)} %reshape.43.pot_ref, bf16[3,1024,256]{2,1,0:T(8,128)(2,1)S(1)} %copy-done.3), custom_call_target="tpu_custom_call" | custom-call | bytes 21000000 | tf_op jit(solution)/shard_map/local/pallas_call | solution.py:340
  46.9 0.0 collective-permute-done.3.left2_ref
  46.9 0.0 collective-permute-done.4.right1_ref
  46.9 0.0 collective-permute-done.5.right2_ref
  46.9 0.0 collective-permute-done.left_ref
  46.9 0.0 collective-permute-done.1.right_ref
  47.0 6.0 %hamilton.1 = (bf16[8,32,2304]{2,1,0:T(8,128)(2,1)}, f32[32,2,256]{2,1,0:T(2,128)S(1)}) custom-call(s32[64]{0:T(128)S(1)} %copy-done.6, s32[1]{0:T(128)} %bitcast.5.group_ref, f32[32,18432]{1,0:T(8,128)S(1)} %get-tuple-element.11.h0_ref, bf16[32,18432]{1,0:T(8,128)(2,1)S(1)} %reshape.42.x_ref, bf16[32,18432]{1,0:T(8,128)(2,1)} %collective-permute-done.left_ref, ...), custom_call_target="tpu_custom_call" | custom-call | bytes 15000000 | tf_op jit(solution)/shard_map/hamilton/pallas_call | solution.py:354
  52.9 15.3 %all_to_all.40 = f32[32,2,256]{2,1,0:T(2,128)S(1)} all-to-all(f32[32,2,256]{2,1,0:T(2,128)S(1)} %get-tuple-element.17), channel_id=1, replica_groups=mesh['x'=4,'core'=2,'z'=8,'y'=4] {'z','y'}, dimensions={0} | all-to-all | bytes 131072 | tf_op jit(solution)/shard_map/all_to_all | solution.py:384
  68.3 7.6 %all-to-all-start.1 = ((bf16[8,32,2304]{2,1,0:T(8,128)(2,1)}), bf16[8,32,2304]{2,1,0:T(8,128)(2,1)S(1)}, u32[]{:S(2)}, u32[]{:S(2)}) async-start(bf16[8,32,2304]{2,1,0:T(8,128)(2,1)} %get-tuple-element.16), calls=%async_computation.1 | async-start | bytes 2359296 | tf_op jit(solution)/shard_map/all_to_all | solution.py:338
  75.9 16.4 %all-to-all-done.1 = bf16[8,32,2304]{2,1,0:T(8,128)(2,1)S(1)} async-done(((bf16[8,32,2304]{2,1,0:T(8,128)(2,1)}), bf16[8,32,2304]{2,1,0:T(8,128)(2,1)S(1)}, u32[]{:S(2)}, u32[]{:S(2)}) %all-to-all-start.1) | async-done | bytes 1179680 | tf_op jit(solution)/shard_map/all_to_all | solution.py:338
  92.4 8.6 %all_to_all.41.refs_2_ = f32[8,4,256]{2,1,0:T(4,128)} all-to-all(f32[8,4,256]{2,1,0:T(4,128)S(1)} %broadcast_in_dim.39), channel_id=1, replica_groups=mesh['x'=4,'core'=2,'z'=8,'y'=4] {'x','core'}, dimensions={0} | all-to-all | bytes 65536 | tf_op jit(solution)/shard_map/all_to_all | solution.py:277
  101.0 4.2 %all-to-all-start = ((bf16[8,32,2304]{2,1,0:T(8,128)(2,1)}), bf16[8,32,2304]{2,1,0:T(8,128)(2,1)S(1)}, u32[]{:S(2)}, u32[]{:S(2)}) async-start(bf16[8,32,2304]{2,1,0:T(8,128)(2,1)} %get-tuple-element.15), calls=%async_computation | async-start | bytes 2359296 | tf_op jit(solution)/shard_map/all_to_all | solution.py:383
  105.2 16.5 %all-to-all-done = bf16[8,32,2304]{2,1,0:T(8,128)(2,1)S(1)} async-done(((bf16[8,32,2304]{2,1,0:T(8,128)(2,1)}), bf16[8,32,2304]{2,1,0:T(8,128)(2,1)S(1)}, u32[]{:S(2)}, u32[]{:S(2)}) %all-to-all-start) | async-done | bytes 1179680 | tf_op jit(solution)/shard_map/all_to_all | solution.py:383
  121.7 0.0 copy-start
  121.7 3.7 %copy-done = bf16[2048,6,384]{2,0,1:T(8,128)(2,1)S(1)} copy-done((bf16[2048,6,384]{2,0,1:T(8,128)(2,1)S(1)}, bf16[2048,6,384]{2,0,1:T(8,128)(2,1)}, u32[]{:S(2)}) %copy-start) | copy-done | bytes 9437208
  125.4 0.0 copy-start.5
  125.4 0.8 copy-done.5
  126.1 3.4 %margin.2 = (f32[4,256,256]{2,1,0:T(8,128)S(1)}, bf16[256,2304]{1,0:T(8,128)(2,1)S(1)}) custom-call(s32[1]{0:T(128)} %bitcast.4.core_ref, bf16[6,4,2,256,384]{4,3,2,1,0:T(8,128)(2,1)S(1)} %bitcast.18, bf16[256,2304]{1,0:T(8,128)(2,1)S(1)} %bitcast.22, bf16[256,2304]{1,0:T(8,128)(2,1)S(1)} %bitcast.21, f32[8,4,256]{2,1,0:T(4,128)S(1)} %copy-done.5), custom_call_target="tpu_custom_call" | custom-call | bytes 9000000 | tf_op jit(solution)/shard_map/margin/pallas_call | solution.py:395
  129.6 1.0 collective-permute-start.6
  130.5 0.0 copy-start.1
  130.5 3.7 %copy-done.1 = bf16[2048,6,384]{2,0,1:T(8,128)(2,1)S(1)} copy-done((bf16[2048,6,384]{2,0,1:T(8,128)(2,1)S(1)}, bf16[2048,6,384]{2,0,1:T(8,128)(2,1)}, u32[]{:S(2)}) %copy-start.1) | copy-done | bytes 9437208
  134.2 2.8 %margin.3 = f32[4,256,256]{2,1,0:T(8,128)S(1)} custom-call(s32[1]{0:T(128)} %bitcast.core_ref, bf16[6,4,2,256,384]{4,3,2,1,0:T(8,128)(2,1)S(1)} %bitcast.19, bf16[256,2304]{1,0:T(8,128)(2,1)S(1)} %get-tuple-element.18.refs_0_.r_ref), custom_call_target="tpu_custom_call" | custom-call | bytes 9000000 | tf_op jit(solution)/shard_map/margin/pallas_call | solution.py:395
  137.1 0.0 collective-permute-done.6
  137.1 0.1 add.36
  137.2 17.4 %all_to_all.42 = f32[4,256,256]{2,1,0:T(8,128)S(1)} all-to-all(f32[4,256,256]{2,1,0:T(8,128)S(1)} %add.36), channel_id=1, replica_groups=mesh['x'=4,'core'=2,'z'=8,'y'=4] {'x'}, dimensions={0} | all-to-all | bytes 2097152 | tf_op jit(solution)/shard_map/all_to_all | solution.py:416
  154.6 0.1 reduce_sum.28
  154.7 13.6 %all_to_all.43 = f32[32,8,256]{2,1,0:T(8,128)S(1)} all-to-all(f32[32,8,256]{2,1,0:T(8,128)S(1)} %bitcast.24), channel_id=1, replica_groups=mesh['x'=4,'core'=2,'z'=8,'y'=4] {'z','y'}, dimensions={0} | all-to-all | bytes 524288 | tf_op jit(solution)/shard_map/all_to_all | solution.py:418
  168.3 0.0 copy-start.8
  168.3 14.3 %all_to_all.44 = bf16[32,8,256]{2,1,0:T(8,128)(2,1)S(1)} all-to-all(bf16[32,8,256]{2,1,0:T(8,128)(2,1)S(1)} %broadcast_in_dim.40), channel_id=1, replica_groups=mesh['x'=4,'core'=2,'z'=8,'y'=4] {'z','y'}, dimensions={0} | all-to-all | bytes 262144 | tf_op jit(solution)/shard_map/all_to_all | solution.py:277
  182.6 9.3 %all_to_all.45.mine_ref = bf16[4,256,256]{2,1,0:T(8,128)(2,1)S(1)} all-to-all(bf16[4,256,256]{2,1,0:T(8,128)(2,1)S(1)} %broadcast_in_dim.42), channel_id=1, replica_groups=mesh['x'=4,'core'=2,'z'=8,'y'=4] {'x'}, dimensions={0} | all-to-all | bytes 1048576 | tf_op jit(solution)/shard_map/all_to_all | solution.py:277
  191.9 4.5 %collective-permute-start.7 = (bf16[4,256,256]{2,1,0:T(8,128)(2,1)S(1)}, bf16[4,256,256]{2,1,0:T(8,128)(2,1)S(1)}, u32[]{:S(2)}, u32[]{:S(2)}) collective-permute-start(bf16[4,256,256]{2,1,0:T(8,128)(2,1)S(1)} %all_to_all.45.mine_ref), channel_id=1, source_target_pairs={{0,32},{32,0},{1,33},{33,1},{2,34},{34,2},{3,35},{35,3},{4,36},{36... | collective-permute-start | bytes 1572872 | tf_op jit(solution)/shard_map/ppermute | solution.py:422
  196.4 1.5 collective-permute-done.7.other_ref
  198.0 0.0 copy-start.2
  198.0 3.7 %copy-done.2 = bf16[2048,6,384]{2,0,1:T(8,128)(2,1)S(1)} copy-done((bf16[2048,6,384]{2,0,1:T(8,128)(2,1)S(1)}, bf16[2048,6,384]{2,0,1:T(8,128)(2,1)}, u32[]{:S(2)}) %copy-start.2) | copy-done | bytes 9437208
  201.6 5.5 %clean.1 = bf16[6,256,384]{2,1,0:T(8,128)(2,1)} custom-call(s32[1]{0:T(128)} %bitcast.core_ref, bf16[6,4,2,256,384]{4,3,2,1,0:T(8,128)(2,1)S(1)} %bitcast.20, bf16[4,256,256]{2,1,0:T(8,128)(2,1)S(1)} %all_to_all.45.mine_ref, bf16[4,256,256]{2,1,0:T(8,128)(2,1)S(1)} %collective-permute-done.7.other_ref, bf16[256,2304]{1,0:T(8,128)(2,1)S(1)} %get-tuple-element.18.refs_0_.r_ref), custom_call_target="tpu_custom_call" | custom-call | bytes 15000000 | tf_op jit(solution)/shard_map/clean/pallas_call | solution.py:424
  207.1 0.0 copy-done.8
  (10 shorter events, 0.2 us)
Async XLA Ops:
  0.6 12.9 %copy-start.10 = (s32[64]{0:T(128)S(1)}, s32[64]{0:T(128)}, u32[]{:S(2)}) copy-start(s32[64]{0:T(128)} %param.14) | copy-start | bytes 772
  0.6 12.9 %copy-start.9 = (f32[32]{0:T(128)S(1)}, f32[32]{0:T(128)}, u32[]{:S(2)}) copy-start(f32[32]{0:T(128)} %param.12) | copy-start | bytes 388
  0.7 13.1 %copy-start.4 = (f32[64,128]{1,0:T(8,128)S(1)}, f32[64,128]{1,0:T(8,128)}, u32[]{:S(2)}) copy-start(f32[64,128]{1,0:T(8,128)} %proj_ref.3) | copy-start | bytes 98308
  0.7 13.1 %copy-start.6 = (s32[64]{0:T(128)S(1)}, s32[64]{0:T(128)}, u32[]{:S(2)}) copy-start(s32[64]{0:T(128)} %block_ref.3) | copy-start | bytes 772
  0.7 39.8 %copy-start.7 = (f32[6,48,64]{2,1,0:T(8,128)S(1)}, f32[6,48,64]{2,1,0:T(8,128)}, u32[]{:S(2)}) copy-start(f32[6,48,64]{2,1,0:T(8,128)} %param.10) | copy-start | bytes 221188
  3.8 36.8 %copy-start.3 = (bf16[3,1024,256]{2,1,0:T(8,128)(2,1)S(1)}, bf16[3,1024,256]{2,1,0:T(8,128)(2,1)}, u32[]{:S(2)}) copy-start(bf16[3,1024,256]{2,1,0:T(8,128)(2,1)} %constant.68.clone.w_ref) | copy-start | bytes 4718596
  3.8 43.1 %collective-permute-start = (bf16[32,18432]{1,0:T(8,128)(2,1)S(1)}, bf16[32,18432]{1,0:T(8,128)(2,1)}, u32[]{:S(2)}, u32[]{:S(2)}) collective-permute-start(bf16[32,18432]{1,0:T(8,128)(2,1)S(1)} %reshape.42.x_ref), channel_id=1, source_target_pairs={{0,1},{1,2},{2,3},{3,4},{4,5},{5,6},{6,7},{7,8},{8,9},{9,10},{10,1... | collective-permute-start | bytes 3538952 | tf_op jit(solution)/shard_map/ppermute | solution.py:307
  6.0 40.9 %collective-permute-start.1 = (bf16[32,18432]{1,0:T(8,128)(2,1)S(1)}, bf16[32,18432]{1,0:T(8,128)(2,1)}, u32[]{:S(2)}, u32[]{:S(2)}) collective-permute-start(bf16[32,18432]{1,0:T(8,128)(2,1)S(1)} %reshape.42.x_ref), channel_id=1, source_target_pairs={{1,0},{2,1},{3,2},{4,3},{5,4},{6,5},{7,6},{8,7},{9,8},{10,9},{11,1... | collective-permute-start | bytes 3538952 | tf_op jit(solution)/shard_map/ppermute | solution.py:308
  16.3 23.1 %collective-permute-start.2 = (f32[40,128]{1,0:T(8,128)S(1)}, f32[40,128]{1,0:T(8,128)S(1)}, u32[]{:S(2)}, u32[]{:S(2)}) collective-permute-start(f32[40,128]{1,0:T(8,128)S(1)} %get-tuple-element.14.mine_ref), channel_id=1, source_target_pairs={{0,1},{1,2},{2,3},{3,4},{4,5},{5,6},{6,7},{7,8},{8,9},{9,10},{10,1... | collective-permute-start | bytes 61448 | tf_op jit(solution)/shard_map/ppermute | solution.py:334
  16.3 30.6 %collective-permute-start.3 = (f32[40,128]{1,0:T(8,128)S(1)}, f32[40,128]{1,0:T(8,128)S(1)}, u32[]{:S(2)}, u32[]{:S(2)}) collective-permute-start(f32[40,128]{1,0:T(8,128)S(1)} %get-tuple-element.14.mine_ref), channel_id=1, source_target_pairs={{0,2},{1,3},{2,4},{3,5},{4,6},{5,7},{6,8},{7,9},{8,10},{9,11},{10,... | collective-permute-start | bytes 61448 | tf_op jit(solution)/shard_map/ppermute | solution.py:335
  16.3 30.6 %collective-permute-start.4 = (f32[40,128]{1,0:T(8,128)S(1)}, f32[40,128]{1,0:T(8,128)S(1)}, u32[]{:S(2)}, u32[]{:S(2)}) collective-permute-start(f32[40,128]{1,0:T(8,128)S(1)} %get-tuple-element.14.mine_ref), channel_id=1, source_target_pairs={{1,0},{2,1},{3,2},{4,3},{5,4},{6,5},{7,6},{8,7},{9,8},{10,9},{11,1... | collective-permute-start | bytes 61448 | tf_op jit(solution)/shard_map/ppermute | solution.py:336
  39.4 7.5 %collective-permute-start.5 = (f32[40,128]{1,0:T(8,128)S(1)}, f32[40,128]{1,0:T(8,128)S(1)}, u32[]{:S(2)}, u32[]{:S(2)}) collective-permute-start(f32[40,128]{1,0:T(8,128)S(1)} %get-tuple-element.14.mine_ref), channel_id=1, source_target_pairs={{2,0},{3,1},{4,2},{5,3},{6,4},{7,5},{8,6},{9,7},{10,8},{11,9},{12,... | collective-permute-start | bytes 61448 | tf_op jit(solution)/shard_map/ppermute | solution.py:337
  68.3 24.1 %all-to-all-start.1 = ((bf16[8,32,2304]{2,1,0:T(8,128)(2,1)}), bf16[8,32,2304]{2,1,0:T(8,128)(2,1)S(1)}, u32[]{:S(2)}, u32[]{:S(2)}) async-start(bf16[8,32,2304]{2,1,0:T(8,128)(2,1)} %get-tuple-element.16), calls=%async_computation.1 | async-start | bytes 2359296 | tf_op jit(solution)/shard_map/all_to_all | solution.py:338
  101.0 20.7 %all-to-all-start = ((bf16[8,32,2304]{2,1,0:T(8,128)(2,1)}), bf16[8,32,2304]{2,1,0:T(8,128)(2,1)S(1)}, u32[]{:S(2)}, u32[]{:S(2)}) async-start(bf16[8,32,2304]{2,1,0:T(8,128)(2,1)} %get-tuple-element.15), calls=%async_computation | async-start | bytes 2359296 | tf_op jit(solution)/shard_map/all_to_all | solution.py:383
  121.7 3.7 %copy-start = (bf16[2048,6,384]{2,0,1:T(8,128)(2,1)S(1)}, bf16[2048,6,384]{2,0,1:T(8,128)(2,1)}, u32[]{:S(2)}) copy-start(bf16[2048,6,384]{2,0,1:T(8,128)(2,1)} %param.16) | copy-start | bytes 28311556
  125.4 0.8 copy-start.5
  129.6 7.5 %collective-permute-start.6 = (f32[4,256,256]{2,1,0:T(8,128)S(1)}, f32[4,256,256]{2,1,0:T(8,128)S(1)}, u32[]{:S(2)}, u32[]{:S(2)}) collective-permute-start(f32[4,256,256]{2,1,0:T(8,128)S(1)} %get-tuple-element.19), channel_id=1, source_target_pairs={{0,32},{32,0},{1,33},{33,1},{2,34},{34,2},{3,35},{35,3},{4,36},{36... | collective-permute-start | bytes 3145736 | tf_op jit(solution)/shard_map/ppermute | solution.py:413
  130.5 3.7 %copy-start.1 = (bf16[2048,6,384]{2,0,1:T(8,128)(2,1)S(1)}, bf16[2048,6,384]{2,0,1:T(8,128)(2,1)}, u32[]{:S(2)}) copy-start(bf16[2048,6,384]{2,0,1:T(8,128)(2,1)} %param.16) | copy-start | bytes 28311556
  168.3 38.9 %copy-start.8 = (f32[8,256]{1,0:T(8,128)}, f32[8,256]{1,0:T(8,128)S(1)}, u32[]{:S(2)}) copy-start(f32[8,256]{1,0:T(8,128)S(1)} %reduce_sum.29) | copy-start | bytes 24580
  191.9 6.0 %collective-permute-start.7 = (bf16[4,256,256]{2,1,0:T(8,128)(2,1)S(1)}, bf16[4,256,256]{2,1,0:T(8,128)(2,1)S(1)}, u32[]{:S(2)}, u32[]{:S(2)}) collective-permute-start(bf16[4,256,256]{2,1,0:T(8,128)(2,1)S(1)} %all_to_all.45.mine_ref), channel_id=1, source_target_pairs={{0,32},{32,0},{1,33},{33,1},{2,34},{34,2},{3,35},{35,3},{4,36},{36... | collective-permute-start | bytes 1572872 | tf_op jit(solution)/shard_map/ppermute | solution.py:422
  198.0 3.7 %copy-start.2 = (bf16[2048,6,384]{2,0,1:T(8,128)(2,1)S(1)}, bf16[2048,6,384]{2,0,1:T(8,128)(2,1)}, u32[]{:S(2)}) copy-start(bf16[2048,6,384]{2,0,1:T(8,128)(2,1)} %param.16) | copy-start | bytes 28311556

commit v3 on v2

--- a/solution.py
+++ b/solution.py
@@ -24,6 +24,7 @@
 WIDTH = 6
 DOM = ("z", "y")
 BAND = ("x", "core")
+EACH = ("x", "z", "y")
 F32 = jnp.float32
 BF16 = jnp.bfloat16
 VMEM = pl.BlockSpec(memory_space=pltpu.VMEM)
@@ -58,9 +59,7 @@
     return np.stack(terms)
 
 
-def inner_kernel(
-    planes, block_ref, x_ref, proj_ref, onehot_ref, coupling_ref, share_ref, raw_ref, pack_ref
-):
+def inner_kernel(block_ref, x_ref, proj_ref, onehot_ref, share_ref):
     rows = x_ref.shape[0]
     slots = proj_ref.shape[0]
     lane = lax.broadcasted_iota(jnp.int32, (rows, BS), 1)
@@ -72,19 +71,9 @@
         return jnp.where(lane == s, total, acc)
 
     acc = lax.fori_loop(0, slots, body, jnp.zeros((rows, BS), F32), unroll=8)
-    raw_ref[...] = acc
-    share_ref[:rows] = jnp.dot(
+    share_ref[...] = jnp.dot(
         acc, onehot_ref[...], precision=lax.Precision.HIGHEST, preferred_element_type=F32
     )
-    share_ref[rows:] = coupling_ref[...]
-
-    parts, _, width = pack_ref.shape
-    plane = x_ref.shape[1] // planes
-    part = plane // parts
-    for c in range(parts):
-        for p in range(planes):
-            src = p * plane + c * part
-            pack_ref[c, :, p * part : (p + 1) * part] = x_ref[:, src : src + part]
 
 
 def local_kernel(planes, x_ref, pot_ref, w_ref, out_ref, den_ref, pad_ref):
@@ -120,28 +109,21 @@
 
 def hamilton_kernel(
     planes,
-    block_ref,
-    group_ref,
     h0_ref,
     x_ref,
     left_ref,
     right_ref,
-    proj_ref,
-    onehot_ref,
     den_ref,
-    raw_ref,
     mine_ref,
-    left1_ref,
-    left2_ref,
-    right1_ref,
-    right2_ref,
-    r_ref,
+    below_ref,
+    above_ref,
+    coupling_ref,
+    h_ref,
+    table_ref,
     nd_ref,
-    h_ref,
 ):
     rows, cells = x_ref.shape
     plane = cells // planes
-    slots = proj_ref.shape[0]
     n = BS // 4
 
     def halo(step, carry):
@@ -171,14 +153,40 @@
     num = lax.fori_loop(0, plane // BS, halo, (zero,) * (rows // 16))
     num = jnp.concatenate(num, axis=0)
 
-    shape = mine_ref.shape
-    at = lax.broadcasted_iota(jnp.int32, shape, 1)
+    lane = lax.broadcasted_iota(jnp.int32, (rows, BS), 1)
+    row = lax.broadcasted_iota(jnp.int32, (rows, BS), 0)
     total = mine_ref[...]
-    total += jnp.where(at < 2 * n, pltpu.roll(left1_ref[...], 3 * n, 1), 0.0)
-    total += jnp.where(at < n, pltpu.roll(left2_ref[...], 2 * n, 1), 0.0)
-    total += jnp.where((at >= n) & (at < 3 * n), pltpu.roll(right1_ref[...], n, 1), 0.0)
-    total += jnp.where((at >= 2 * n) & (at < 3 * n), pltpu.roll(right2_ref[...], 2 * n, 1), 0.0)
-    table = total[:rows] * total[rows : rows + 1]
+    total += pltpu.roll(below_ref[...], 3 * n, 1)
+    total += pltpu.roll(above_ref[...], n, 1)
+    table = total * coupling_ref[...]
+    table_ref[...] = table
+    num = jnp.sum(num + table * total, axis=1, keepdims=True)
+    den = jnp.sum(den_ref[...], axis=1, keepdims=True)
+    line = jnp.where(lane == row, num, 0.0) + jnp.where(lane == row + rows, den, 0.0)
+    line = jnp.sum(line, axis=0, keepdims=True)
+    nd_ref[...] = jnp.broadcast_to(line[None], nd_ref.shape)
+
+
+def residual_kernel(
+    planes,
+    block_ref,
+    h_ref,
+    x_ref,
+    nd_ref,
+    proj_ref,
+    onehot_ref,
+    mine_ref,
+    below_ref,
+    above_ref,
+    r_ref,
+    full_ref,
+):
+    rows, cells = x_ref.shape
+    plane = cells // planes
+    slots = proj_ref.shape[0]
+    n = BS // 4
+    table = mine_ref[...] + pltpu.roll(below_ref[...], 3 * n, 1)
+    table += pltpu.roll(above_ref[...], n, 1)
     value = lax.dot_general(
         table,
         onehot_ref[...],
@@ -186,52 +194,29 @@
         precision=lax.Precision.HIGHEST,
         preferred_element_type=F32,
     )
+    lane = lax.broadcasted_iota(jnp.int32, (rows, BS), 1)
+    row = lax.broadcasted_iota(jnp.int32, (rows, BS), 0)
+    sums = jnp.sum(nd_ref[...], axis=0)
+    num = jnp.sum(jnp.where(lane == row, sums, 0.0), axis=1, keepdims=True)
+    den = jnp.sum(jnp.where(lane == row + rows, sums, 0.0), axis=1, keepdims=True)
+    energy = jnp.broadcast_to(num / den, (rows, BS))
+    for at in range(0, cells, BS):
+        where = slice(at, at + BS)
+        full_ref[:, where] = h_ref[:, where] - energy * x_ref[:, where].astype(F32)
+
     for s in range(slots):
         where = pl.ds(pl.multiple_of(block_ref[s] * BS, BS), BS)
-        h_ref[:, where] += value[:, s : s + 1] * proj_ref[s : s + 1, :]
-
-    num = jnp.sum(num + value * raw_ref[...], axis=1, keepdims=True)
-    den = jnp.sum(den_ref[...], axis=1, keepdims=True)
-    parts, _, width = r_ref.shape
+        full_ref[:, where] += value[:, s : s + 1] * proj_ref[s : s + 1, :]
+
+    parts = r_ref.shape[0]
     part = plane // parts
-    energy = jnp.broadcast_to(jnp.where(den > 0.0, num / den, 0.0), (rows, BS))
     for c in range(parts):
         for p in range(planes):
-            for j in range(part // BS):
-                src = p * plane + c * part + j * BS
-                dst = p * part + j * BS
-                left = h_ref[:, src : src + BS] - energy * x_ref[:, src : src + BS].astype(F32)
-                r_ref[c, :, dst : dst + BS] = left.astype(BF16)
-
-    bands = nd_ref.shape[2]
-    lane = lax.broadcasted_iota(jnp.int32, (rows, bands), 1)
-    band = lax.broadcasted_iota(jnp.int32, (rows, bands), 0) + group_ref[0] * rows
-    for i, column in enumerate((num, den)):
-        line = jnp.sum(jnp.where(lane == band, column, 0.0), axis=0, keepdims=True)
-        nd_ref[:, i : i + 1, :] = jnp.broadcast_to(line[None], (nd_ref.shape[0], 1, bands))
-
-
-def margin_kernel(planes, fix, core_ref, locked_ref, *refs):
-    if fix:
-        h_ref, x_ref, sums_ref, out_ref, r_ref = refs
-
-        @pl.when(pl.program_id(0) == 0)
-        def _():
-            bands = h_ref.shape[0]
-            sums = jnp.sum(sums_ref[...], axis=0)
-            own = jnp.where(sums[3:4] > 0.0, sums[2:3] / sums[3:4], 0.0)
-            shift = sums[0:1] / sums[1:2] - own
-            eye = lax.broadcasted_iota(jnp.int32, (bands, bands), 0) == lax.broadcasted_iota(
-                jnp.int32, (bands, bands), 1
-            )
-            shift = jnp.sum(jnp.where(eye, shift, 0.0), axis=1, keepdims=True)
-            for j in range(0, h_ref.shape[1], BS):
-                where = slice(j, j + BS)
-                value = h_ref[:, where].astype(F32) - shift * x_ref[:, where].astype(F32)
-                r_ref[:, where] = value.astype(BF16)
-
-    else:
-        r_ref, out_ref = refs
+            src = p * plane + c * part
+            r_ref[c, :, p * part : (p + 1) * part] = full_ref[:, src : src + part].astype(BF16)
+
+
+def margin_kernel(planes, core_ref, locked_ref, r_ref, out_ref):
     part = r_ref.shape[1] // planes
     acc = None
     for p in range(planes):
@@ -290,7 +275,6 @@
     n_x = lax.axis_size("x")
     core = lax.axis_index("core").astype(jnp.int32)
     here = lax.axis_index(DOM)
-    group = lax.axis_index(BAND).astype(jnp.int32)
     slots = slot_block.shape[0]
     n = coupling.shape[0]
     part = plane // groups
@@ -299,8 +283,6 @@
     bands = groups * rows
     share_rows = n_locked // groups
     up, down = ring(domains)
-    up2 = [(i, (i + 2) % domains) for i in range(domains)]
-    down2 = [(j, i) for i, j in up2]
     swap = [(0, 1), (1, 0)]
 
     x = orbitals.reshape(rows, cells)
@@ -316,26 +298,19 @@
     column = jnp.where(active, column, BS)
     column = jnp.pad(column, (0, BS - slots), constant_values=BS)
     onehot = (column[:, None] == jnp.arange(BS, dtype=jnp.int32)[None, :]).astype(F32)
-    coupling_rows = jnp.pad(coupling[None], ((0, 7), (n, BS - 2 * n)))
-
-    shares, raw, packed = pl.pallas_call(
-        functools.partial(inner_kernel, planes),
-        out_shape=(
-            jax.ShapeDtypeStruct((rows + 8, BS), F32),
-            jax.ShapeDtypeStruct((rows, BS), F32),
-            jax.ShapeDtypeStruct((groups, rows, width), BF16),
-        ),
-        in_specs=[SMEM, VMEM, VMEM, VMEM, VMEM],
-        out_specs=(VMEM, VMEM, VMEM),
+    coupling_row = jnp.pad(coupling[None], ((0, 0), (n, BS - 2 * n)))
+
+    shares = pl.pallas_call(
+        inner_kernel,
+        out_shape=jax.ShapeDtypeStruct((rows, BS), F32),
+        in_specs=[SMEM, VMEM, VMEM, VMEM],
+        out_specs=VMEM,
         compiler_params=params(8),
-        cost_estimate=cost(3),
+        cost_estimate=cost(2),
         name="inner",
-    )(slot_block, x, projectors, onehot, coupling_rows)
-    left1 = lax.ppermute(shares, DOM, up)
-    left2 = lax.ppermute(shares, DOM, up2)
-    right1 = lax.ppermute(shares, DOM, down)
-    right2 = lax.ppermute(shares, DOM, down2)
-    x_moved = lax.all_to_all(packed, BAND, 0, 0, tiled=True).reshape(bands, width)
+    )(slot_block, x, projectors, onehot)
+    below = lax.ppermute(shares, DOM, up)
+    above = lax.ppermute(shares, DOM, down)
 
     h0, den = pl.pallas_call(
         functools.partial(local_kernel, planes),
@@ -351,74 +326,72 @@
         name="local",
     )(x, pot, weights)
 
-    sent, sums = pl.pallas_call(
+    hamilton, table, sums = pl.pallas_call(
         functools.partial(hamilton_kernel, planes),
         out_shape=(
-            jax.ShapeDtypeStruct((groups, rows, width), BF16),
-            jax.ShapeDtypeStruct((domains, 2, bands), F32),
+            jax.ShapeDtypeStruct((rows, cells), F32),
+            jax.ShapeDtypeStruct((rows, BS), F32),
+            jax.ShapeDtypeStruct((domains, 1, BS), F32),
         ),
-        in_specs=[SMEM, SMEM] + [VMEM] * 13,
-        out_specs=(VMEM, VMEM),
-        scratch_shapes=[pltpu.VMEM((rows, cells), F32)],
+        in_specs=[VMEM] * 9,
+        out_specs=(VMEM, VMEM, VMEM),
         compiler_params=params(24),
         cost_estimate=cost(5),
         name="hamilton",
+    )(h0, x, left, right, den, shares, below, above, coupling_row)
+    table_below = lax.ppermute(table, DOM, up)
+    table_above = lax.ppermute(table, DOM, down)
+    sums = lax.all_to_all(sums, DOM, 0, 0, tiled=True)
+
+    residual = pl.pallas_call(
+        functools.partial(residual_kernel, planes),
+        out_shape=jax.ShapeDtypeStruct((groups, rows, width), BF16),
+        in_specs=[SMEM] + [VMEM] * 8,
+        out_specs=VMEM,
+        scratch_shapes=[pltpu.VMEM((rows, cells), F32)],
+        compiler_params=params(24),
+        cost_estimate=cost(2),
+        name="residual",
     )(
         slot_block,
-        group.reshape(1),
-        h0,
+        hamilton,
         x,
-        left,
-        right,
+        sums,
         projectors,
         onehot,
-        den,
-        raw,
-        shares,
-        left1,
-        left2,
-        right1,
-        right2,
-    )
-    moved = lax.all_to_all(sent, BAND, 0, 0, tiled=True).reshape(bands, width)
-    whole = jnp.sum(lax.all_to_all(sums, DOM, 0, 0, tiled=True), axis=0)
-    sums = spread(jnp.concatenate([whole, sums[0]], axis=0), BAND)
-    sums = sums.reshape(groups, 4, bands)
+        table,
+        table_below,
+        table_above,
+    )
+    residual = lax.all_to_all(residual, BAND, 0, 0, tiled=True).reshape(bands, width)
 
     by_plane = locked.transpose(1, 0, 2).reshape(planes, n_x, 2, share_rows, part)
-
-    def margin_call(fix, side, *operands):
-        full = pl.BlockSpec((bands, width), lambda i, c: (0, 0))
-        out_spec = pl.BlockSpec((1, share_rows, bands), lambda i, c: (i, 0, 0))
-        out_shape = jax.ShapeDtypeStruct((n_x, share_rows, bands), F32)
-        extra = [pl.BlockSpec((groups, 4, bands), lambda i, c: (0, 0, 0))]
+    by_plane = pltpu.with_memory_space_constraint(by_plane, pltpu.HBM)
+
+    def margin_call(side):
         return pl.pallas_call(
-            functools.partial(margin_kernel, planes, fix),
-            out_shape=(out_shape, jax.ShapeDtypeStruct((bands, width), BF16)) if fix else out_shape,
+            functools.partial(margin_kernel, planes),
+            out_shape=jax.ShapeDtypeStruct((n_x, share_rows, bands), F32),
             grid_spec=pltpu.PrefetchScalarGridSpec(
                 num_scalar_prefetch=1,
                 grid=(n_x,),
                 in_specs=[
-                    pl.BlockSpec((planes, 1, 1, share_rows, part), lambda i, c: (0, i, c[0], 0, 0))
-                ]
-                + ([full, full] + extra if fix else [full]),
-                out_specs=(out_spec, full) if fix else out_spec,
+                    pl.BlockSpec((planes, 1, 1, share_rows, part), lambda i, c: (0, i, c[0], 0, 0)),
+                    pl.BlockSpec((bands, width), lambda i, c: (0, 0)),
+                ],
+                out_specs=pl.BlockSpec((1, share_rows, bands), lambda i, c: (i, 0, 0)),
             ),
             compiler_params=params(24),
             cost_estimate=cost(3),
             name="margin",
-        )(side.reshape(1), by_plane, *operands)
-
-    given, residual = margin_call(True, 1 - core, moved, x_moved, sums)
-    given = lax.ppermute(given, "core", swap)
-    kept = margin_call(False, core, residual)
-    pair = kept + given
-    share = jnp.sum(lax.all_to_all(pair, "x", 0, 0, tiled=True), axis=0)
-    share = share.reshape(domains, -1, bands)
-    margins = jnp.sum(lax.all_to_all(share, DOM, 0, 0, tiled=True), axis=0)
-
-    coeffs = spread(margins.astype(BF16), DOM).reshape(share_rows, bands)
-    coeffs = spread(coeffs, "x").reshape(n_x, share_rows, bands)
+        )(side.reshape(1), by_plane, residual)
+
+    given = lax.ppermute(margin_call(1 - core), "core", swap)
+    pair = margin_call(core) + given
+    share = pair.reshape(n_x * domains, -1, bands)
+    margins = jnp.sum(lax.all_to_all(share, EACH, 0, 0, tiled=True), axis=0)
+
+    coeffs = spread(margins.astype(BF16), EACH).reshape(n_x, share_rows, bands)
     other = lax.ppermute(coeffs, "core", swap)
     whole_block = pl.BlockSpec((n_x, share_rows, bands), lambda p, c: (0, 0, 0))
     orthogonal = pl.pallas_call(

time: 208 us -> 181 us (0.87)
  waiting for transfers between devices: 52.8 us -> 32.3 us
  blocking collectives: 78.4 us -> 64.1 us
  Pallas kernels: 26.6 us -> 31.7 us
  starting transfers between devices: 32.1 us -> 36.8 us
    all_to_all x2, waiting for transfers between devices: 33 us -> 17.7 us  [the longest x1 16.5 us: per_device(): lax.all_to_all(residual, BAND, 0, 0, tiled=True).reshape(bands, width)]
    all_to_all x3 -> x1, blocking collectives: 46.2 us -> 38.7 us  [per_device(): margins = jnp.sum(lax.all_to_all(share, EACH, 0, 0, tiled=True), axis=0)]
    all_to_all x3 -> x1, blocking collectives: 32.2 us -> 25.4 us  [spread(): lax.all_to_all(jnp.broadcast_to(value[None], (size,) + value.shape), axis...]
    ppermute x5, waiting for transfers between devices: 18.3 us -> 13 us  [the longest x1 11.7 us: per_device(): below = lax.ppermute(shares, DOM, up)]
    pallas_call x3 -> x4, Pallas kernels: 8.86 us -> 13 us  [the longest x2 8.81 us: margin_call(): pl.pallas_call(functools.partial(margin_kernel, planes), out_shape=jax.Sh...]
    ppermute x5, starting transfers between devices: 6.79 us -> 10.6 us  [the longest x1 4.78 us: per_device(): above = lax.ppermute(shares, DOM, down)]
    pallas_call x1, Pallas kernels: 5.5 us -> 8.51 us  [per_device(): pl.pallas_call(clean_kernel, out_shape=jax.ShapeDtypeStruct((planes, band...]
    pallas_call x1, Pallas kernels: 5.99 us -> 3.88 us  [per_device(): pl.pallas_call(functools.partial(hamilton_kernel, planes), out_shape=(jax...]
  transfers between devices with their start and end apart: 10 -> 10, of which waited for: 4 -> 5; matrix products, arithmetic and copies ran while one was open for 0% -> 0% of each run, Pallas kernels for 6% -> 7%
where the time goes in v3:
time: 181 us; the launch traced here: 180 us
  blocking collectives  64.1 us (35%)
  starting transfers between devices  36.8 us (20%)
  waiting for transfers between devices  32.3 us (18%)
  Pallas kernels  31.7 us (18%)
  local copies, waits for them, and re-layouts  13.5 us (7%)
    all_to_all x1, blocking collectives, per_device(): margins = jnp.sum(lax.all_to_all(share, EACH, 0, 0, tiled=True), axis=0)  38.7 us
    all_to_all x1, blocking collectives, spread(): lax.all_to_all(jnp.broadcast_to(value[None], (size,) + value.shape), axis...  25.4 us
    all_to_all x1, waiting for transfers between devices, per_device(): lax.all_to_all(residual, BAND, 0, 0, tiled=True).reshape(bands, width)  16.5 us
    ppermute x1, waiting for transfers between devices, per_device(): below = lax.ppermute(shares, DOM, up)  11.7 us
    unnamed x44, local copies, waits for them, and re-layouts  10.1 us
    pallas_call x2, Pallas kernels, margin_call(): pl.pallas_call(functools.partial(margin_kernel, planes), out_shape=jax.Sh...  8.81 us
    pallas_call x1, Pallas kernels, per_device(): pl.pallas_call(clean_kernel, out_shape=jax.ShapeDtypeStruct((planes, band...  8.51 us
    all_to_all x1, starting transfers between devices, per_device(): lax.all_to_all(residual, BAND, 0, 0, tiled=True).reshape(bands, width)  7.32 us
  transfers between devices with their start and end apart: 10, of which 5 were waited for; matrix products, arithmetic and copies ran while one was open for 0% of the time, Pallas kernels for 7%

profile of v3, /device:TPU:1, one launch (start us, length us, event | category | flops | bytes accessed | tf_op | source)
XLA Modules:
  0.0 180.3 jit_solution(14209743120170328036)
XLA Ops:
  0.6 0.0 copy-start.20
  0.6 0.0 copy-start.3
  0.7 0.0 copy-start.16
  0.7 0.0 copy-start.18
  0.7 3.1 %reshape.35.x_ref = bf16[32,18432]{1,0:T(8,128)(2,1)S(1)} reshape(bf16[32,6,48,64]{3,2,1,0:T(8,128)(2,1)} %param.9) | data formatting | bytes 2359296 | tf_op jit(solution)/shard_map/reshape | solution.py:288
  3.8 0.0 copy-start
  3.8 2.2 %collective-permute-start = (bf16[32,18432]{1,0:T(8,128)(2,1)S(1)}, bf16[32,18432]{1,0:T(8,128)(2,1)}, u32[]{:S(2)}, u32[]{:S(2)}) collective-permute-start(bf16[32,18432]{1,0:T(8,128)(2,1)S(1)} %reshape.35.x_ref), channel_id=1, source_target_pairs={{0,1},{1,2},{2,3},{3,4},{4,5},{5,6},{6,7},{7,8},{8,9},{9,10},{10,1... | collective-permute-start | bytes 3538952 | tf_op jit(solution)/shard_map/ppermute | solution.py:289
  6.0 6.8 %collective-permute-start.1 = (bf16[32,18432]{1,0:T(8,128)(2,1)S(1)}, bf16[32,18432]{1,0:T(8,128)(2,1)}, u32[]{:S(2)}, u32[]{:S(2)}) collective-permute-start(bf16[32,18432]{1,0:T(8,128)(2,1)S(1)} %reshape.35.x_ref), channel_id=1, source_target_pairs={{1,0},{2,1},{3,2},{4,3},{5,4},{6,5},{7,6},{8,7},{9,8},{10,9},{11,1... | collective-permute-start | bytes 3538952 | tf_op jit(solution)/shard_map/ppermute | solution.py:290
  13.5 0.0 copy-done.20
  13.5 0.1 fusion.onehot_ref
  13.6 0.0 copy-done.3
  13.6 0.0 copy-done.16
  13.6 1.6 inner.1.mine_ref
  15.2 0.6 copy-done.1
  15.9 0.0 collective-permute-start.2
  15.9 4.8 %collective-permute-start.3 = (f32[32,128]{1,0:T(8,128)S(1)}, f32[32,128]{1,0:T(8,128)S(1)}, u32[]{:S(2)}, u32[]{:S(2)}) collective-permute-start(f32[32,128]{1,0:T(8,128)S(1)} %inner.1.mine_ref), channel_id=1, source_target_pairs={{1,0},{2,1},{3,2},{4,3},{5,4},{6,5},{7,6},{8,7},{9,8},{10,9},{11,1... | collective-permute-start | bytes 49160 | tf_op jit(solution)/shard_map/ppermute | solution.py:313
  20.7 0.0 copy-done.18
  20.7 0.1 reshape.36.pot_ref
  20.8 0.0 copy-done
  20.8 0.0 copy-start.21
  20.8 6.3 %local.1 = (f32[32,18432]{1,0:T(8,128)S(1)}, f32[32,128]{1,0:T(8,128)S(1)}) custom-call(bf16[32,18432]{1,0:T(8,128)(2,1)S(1)} %reshape.35.x_ref, f32[1,18432]{1,0:T(1,128)S(1)} %reshape.36.pot_ref, bf16[3,1024,256]{2,1,0:T(8,128)(2,1)S(1)} %copy-done), custom_call_target="tpu_custom_call" | custom-call | bytes 21000000 | tf_op jit(solution)/shard_map/local/pallas_call | solution.py:315
  27.1 0.0 copy-done.21
  27.1 0.1 pad.9.coupling_ref
  27.2 11.7 %collective-permute-done.2.below_ref = f32[32,128]{1,0:T(8,128)S(1)} collective-permute-done((f32[32,128]{1,0:T(8,128)S(1)}, f32[32,128]{1,0:T(8,128)S(1)}, u32[]{:S(2)}, u32[]{:S(2)}) %collective-permute-start.2) | collective-permute-done | bytes 16416 | tf_op jit(solution)/shard_map/ppermute | solution.py:312
  38.9 0.6 copy-done.7
  39.5 0.0 collective-permute-done.3.above_ref
  39.5 0.6 copy-done.9
  40.1 0.0 collective-permute-done.left_ref
  40.1 0.0 collective-permute-done.1.right_ref
  40.1 0.7 copy-done.8
  40.8 0.7 copy-done.10
  41.5 3.9 %hamilton.1 = (f32[32,18432]{1,0:T(8,128)S(1)}, f32[32,128]{1,0:T(8,128)S(1)}, f32[32,1,128]{2,1,0:T(1,128)S(1)}) custom-call(f32[32,18432]{1,0:T(8,128)S(1)} %get-tuple-element.7.h0_ref, bf16[32,18432]{1,0:T(8,128)(2,1)S(1)} %reshape.35.x_ref, bf16[32,18432]{1,0:T(8,128)(2,1)} %collective-permute-done.left_ref, ...), custom_call_target="tpu_custom_call" | custom-call | bytes 15000000 | tf_op jit(solution)/shard_map/hamilton/pallas_call | solution.py:329
  45.4 0.0 copy-start.5
  45.4 0.6 copy-done.5
  46.0 0.6 copy-done.15
  46.6 6.5 %all-to-all-start = ((f32[32,1,128]{2,1,0:T(1,128)}), f32[32,1,128]{2,1,0:T(1,128)S(1)}, u32[]{:S(2)}, u32[]{:S(2)}) async-start(f32[32,1,128]{2,1,0:T(1,128)} %copy-done.15), calls=%async_computation | async-start | bytes 32768 | tf_op jit(solution)/shard_map/all_to_all | solution.py:344
  53.1 1.3 collective-permute-start.4
  54.4 3.6 %collective-permute-start.5 = (f32[32,128]{1,0:T(8,128)}, f32[32,128]{1,0:T(8,128)S(1)}, u32[]{:S(2)}, u32[]{:S(2)}) collective-permute-start(f32[32,128]{1,0:T(8,128)} %copy-done.5), channel_id=1, source_target_pairs={{1,0},{2,1},{3,2},{4,3},{5,4},{6,5},{7,6},{8,7},{9,8},{10,9},{11,1... | collective-permute-start | bytes 49160 | tf_op jit(solution)/shard_map/ppermute | solution.py:343
  58.0 1.3 collective-permute-done.4.below_ref
  59.3 0.6 copy-done.11
  59.9 0.0 collective-permute-done.5.above_ref
  59.9 0.6 copy-done.13
  60.5 1.2 all-to-all-done.nd_ref
  61.7 0.8 copy-done.2
  62.6 0.8 copy-done.4
  63.3 0.7 copy-done.6
  64.0 0.7 copy-done.12
  64.8 0.7 copy-done.14
  65.5 0.7 copy-done.17
  66.1 2.6 %residual.1 = bf16[8,32,2304]{2,1,0:T(8,128)(2,1)} custom-call(s32[64]{0:T(128)S(1)} %copy-done.17, f32[32,18432]{1,0:T(8,128)S(1)} %get-tuple-element.9.h_ref, bf16[32,18432]{1,0:T(8,128)(2,1)S(1)} %reshape.35.x_ref, f32[32,1,128]{2,1,0:T(1,128)S(1)} %all-to-all-done.nd_ref, f32[64,128]{1,0:T(8,128)S(1)} %copy-done.4, f32[128,128]{1,0:T(8,128)S(1)} %copy-done.2, ...), custom_call_target="tpu_custom_call" | custom-call | bytes 6000000 | tf_op jit(solution)/shard_map/residual/pallas_call | solution.py:346
  68.7 7.3 %all-to-all-start.1 = ((bf16[8,32,2304]{2,1,0:T(8,128)(2,1)}), bf16[8,32,2304]{2,1,0:T(8,128)(2,1)S(1)}, u32[]{:S(2)}, u32[]{:S(2)}) async-start(bf16[8,32,2304]{2,1,0:T(8,128)(2,1)} %residual.1), calls=%async_computation.1 | async-start | bytes 2359296 | tf_op jit(solution)/shard_map/all_to_all | solution.py:366
  76.0 16.5 %all-to-all-done.1 = bf16[8,32,2304]{2,1,0:T(8,128)(2,1)S(1)} async-done(((bf16[8,32,2304]{2,1,0:T(8,128)(2,1)}), bf16[8,32,2304]{2,1,0:T(8,128)(2,1)S(1)}, u32[]{:S(2)}, u32[]{:S(2)}) %all-to-all-start.1) | async-done | bytes 1179680 | tf_op jit(solution)/shard_map/all_to_all | solution.py:366
  92.5 4.4 %margin.3 = f32[4,256,256]{2,1,0:T(8,128)S(1)} custom-call(s32[1]{0:T(128)} %bitcast.7.core_ref, bf16[6,4,2,256,384]{4,3,2,1,0:T(8,128)(2,1)} %bitcast.19, bf16[256,2304]{1,0:T(8,128)(2,1)S(1)} %bitcast.14), custom_call_target="tpu_custom_call" | custom-call | bytes 9000000 | tf_op jit(solution)/shard_map/margin/pallas_call | solution.py:372
  96.9 1.0 collective-permute-start.6
  97.9 4.4 %margin.2 = f32[4,256,256]{2,1,0:T(8,128)S(1)} custom-call(s32[1]{0:T(128)} %bitcast.core_ref, bf16[6,4,2,256,384]{4,3,2,1,0:T(8,128)(2,1)} %bitcast.20, bf16[256,2304]{1,0:T(8,128)(2,1)S(1)} %bitcast.15), custom_call_target="tpu_custom_call" | custom-call | bytes 9000000 | tf_op jit(solution)/shard_map/margin/pallas_call | solution.py:372
  102.3 0.0 collective-permute-done.6
  102.3 0.1 add.32
  102.5 38.7 %all_to_all.20 = f32[128,8,256]{2,1,0:T(8,128)S(1)} all-to-all(f32[128,8,256]{2,1,0:T(8,128)S(1)} %bitcast.22), channel_id=1, replica_groups=mesh['x'=4,'core'=2,'z'=8,'y'=4] {'x','z','y'}, dimensions={0} | all-to-all | bytes 2097152 | tf_op jit(solution)/shard_map/all_to_all | solution.py:392
  141.2 0.1 reduce_sum.9
  141.3 0.0 copy-start.19
  141.4 25.4 %all_to_all.21 = bf16[128,8,256]{2,1,0:T(8,128)(2,1)S(1)} all-to-all(bf16[128,8,256]{2,1,0:T(8,128)(2,1)S(1)} %broadcast_in_dim.26), channel_id=1, replica_groups=mesh['x'=4,'core'=2,'z'=8,'y'=4] {'x','z','y'}, dimensions={0} | all-to-all | bytes 1048576 | tf_op jit(solution)/shard_map/all_to_all | solution.py:262
  166.8 3.4 %collective-permute-start.7 = (bf16[4,256,256]{2,1,0:T(8,128)(2,1)S(1)}, bf16[4,256,256]{2,1,0:T(8,128)(2,1)S(1)}, u32[]{:S(2)}, u32[]{:S(2)}) collective-permute-start(bf16[4,256,256]{2,1,0:T(8,128)(2,1)S(1)} %bitcast.17), channel_id=1, source_target_pairs={{0,32},{32,0},{1,33},{33,1},{2,34},{34,2},{3,35},{35,3},{4,36},{36... | collective-permute-start | bytes 1572872 | tf_op jit(solution)/shard_map/ppermute | solution.py:395
  170.2 1.5 collective-permute-done.7.other_ref
  171.7 8.5 %clean.1 = bf16[6,256,384]{2,1,0:T(8,128)(2,1)} custom-call(s32[1]{0:T(128)} %bitcast.core_ref, bf16[6,4,2,256,384]{4,3,2,1,0:T(8,128)(2,1)} %bitcast.21, bf16[4,256,256]{2,1,0:T(8,128)(2,1)S(1)} %bitcast.18, bf16[4,256,256]{2,1,0:T(8,128)(2,1)S(1)} %collective-permute-done.7.other_ref, bf16[256,2304]{1,0:T(8,128)(2,1)S(1)} %bitcast.16), custom_call_target="tpu_custom_call" | custom-call | bytes 15000000 | tf_op jit(solution)/shard_map/clean/pallas_call | solution.py:397
  (19 shorter events, 0.1 us)
Async XLA Ops:
  0.6 12.8 %copy-start.20 = (s32[64]{0:T(128)S(1)}, s32[64]{0:T(128)}, u32[]{:S(2)}) copy-start(s32[64]{0:T(128)} %param.14) | copy-start | bytes 772
  0.6 13.0 %copy-start.3 = (f32[64,128]{1,0:T(8,128)S(1)}, f32[64,128]{1,0:T(8,128)}, u32[]{:S(2)}) copy-start(f32[64,128]{1,0:T(8,128)} %proj_ref.3) | copy-start | bytes 98308
  0.7 13.0 %copy-start.16 = (s32[64]{0:T(128)S(1)}, s32[64]{0:T(128)}, u32[]{:S(2)}) copy-start(s32[64]{0:T(128)} %block_ref.3) | copy-start | bytes 772
  0.7 20.0 %copy-start.18 = (f32[6,48,64]{2,1,0:T(8,128)S(1)}, f32[6,48,64]{2,1,0:T(8,128)}, u32[]{:S(2)}) copy-start(f32[6,48,64]{2,1,0:T(8,128)} %param.10) | copy-start | bytes 221188
  3.8 17.0 %copy-start = (bf16[3,1024,256]{2,1,0:T(8,128)(2,1)S(1)}, bf16[3,1024,256]{2,1,0:T(8,128)(2,1)}, u32[]{:S(2)}) copy-start(bf16[3,1024,256]{2,1,0:T(8,128)(2,1)} %constant.64.clone.w_ref) | copy-start | bytes 4718596
  3.8 36.3 %collective-permute-start = (bf16[32,18432]{1,0:T(8,128)(2,1)S(1)}, bf16[32,18432]{1,0:T(8,128)(2,1)}, u32[]{:S(2)}, u32[]{:S(2)}) collective-permute-start(bf16[32,18432]{1,0:T(8,128)(2,1)S(1)} %reshape.35.x_ref), channel_id=1, source_target_pairs={{0,1},{1,2},{2,3},{3,4},{4,5},{5,6},{6,7},{7,8},{8,9},{9,10},{10,1... | collective-permute-start | bytes 3538952 | tf_op jit(solution)/shard_map/ppermute | solution.py:289
  6.0 34.1 %collective-permute-start.1 = (bf16[32,18432]{1,0:T(8,128)(2,1)S(1)}, bf16[32,18432]{1,0:T(8,128)(2,1)}, u32[]{:S(2)}, u32[]{:S(2)}) collective-permute-start(bf16[32,18432]{1,0:T(8,128)(2,1)S(1)} %reshape.35.x_ref), channel_id=1, source_target_pairs={{1,0},{2,1},{3,2},{4,3},{5,4},{6,5},{7,6},{8,7},{9,8},{10,9},{11,1... | collective-permute-start | bytes 3538952 | tf_op jit(solution)/shard_map/ppermute | solution.py:290
  15.2 0.6 copy-start.1
  15.9 23.0 %collective-permute-start.2 = (f32[32,128]{1,0:T(8,128)S(1)}, f32[32,128]{1,0:T(8,128)S(1)}, u32[]{:S(2)}, u32[]{:S(2)}) collective-permute-start(f32[32,128]{1,0:T(8,128)S(1)} %inner.1.mine_ref), channel_id=1, source_target_pairs={{0,1},{1,2},{2,3},{3,4},{4,5},{5,6},{6,7},{7,8},{8,9},{9,10},{10,1... | collective-permute-start | bytes 49160 | tf_op jit(solution)/shard_map/ppermute | solution.py:312
  15.9 23.6 %collective-permute-start.3 = (f32[32,128]{1,0:T(8,128)S(1)}, f32[32,128]{1,0:T(8,128)S(1)}, u32[]{:S(2)}, u32[]{:S(2)}) collective-permute-start(f32[32,128]{1,0:T(8,128)S(1)} %inner.1.mine_ref), channel_id=1, source_target_pairs={{1,0},{2,1},{3,2},{4,3},{5,4},{6,5},{7,6},{8,7},{9,8},{10,9},{11,1... | collective-permute-start | bytes 49160 | tf_op jit(solution)/shard_map/ppermute | solution.py:313
  20.8 6.3 %copy-start.21 = (f32[32]{0:T(128)S(1)}, f32[32]{0:T(128)}, u32[]{:S(2)}) copy-start(f32[32]{0:T(128)} %param.12) | copy-start | bytes 388
  38.9 0.6 copy-start.7
  39.5 0.6 copy-start.9
  40.1 0.7 copy-start.8
  40.8 0.7 copy-start.10
  45.4 0.6 copy-start.5
  46.0 0.6 copy-start.15
  46.6 15.1 %all-to-all-start = ((f32[32,1,128]{2,1,0:T(1,128)}), f32[32,1,128]{2,1,0:T(1,128)S(1)}, u32[]{:S(2)}, u32[]{:S(2)}) async-start(f32[32,1,128]{2,1,0:T(1,128)} %copy-done.15), calls=%async_computation | async-start | bytes 32768 | tf_op jit(solution)/shard_map/all_to_all | solution.py:344
  53.1 6.2 %collective-permute-start.4 = (f32[32,128]{1,0:T(8,128)}, f32[32,128]{1,0:T(8,128)S(1)}, u32[]{:S(2)}, u32[]{:S(2)}) collective-permute-start(f32[32,128]{1,0:T(8,128)} %copy-done.5), channel_id=1, source_target_pairs={{0,1},{1,2},{2,3},{3,4},{4,5},{5,6},{6,7},{7,8},{8,9},{9,10},{10,1... | collective-permute-start | bytes 49160 | tf_op jit(solution)/shard_map/ppermute | solution.py:342
  54.4 5.5 %collective-permute-start.5 = (f32[32,128]{1,0:T(8,128)}, f32[32,128]{1,0:T(8,128)S(1)}, u32[]{:S(2)}, u32[]{:S(2)}) collective-permute-start(f32[32,128]{1,0:T(8,128)} %copy-done.5), channel_id=1, source_target_pairs={{1,0},{2,1},{3,2},{4,3},{5,4},{6,5},{7,6},{8,7},{9,8},{10,9},{11,1... | collective-permute-start | bytes 49160 | tf_op jit(solution)/shard_map/ppermute | solution.py:343
  59.3 0.6 copy-start.11
  59.9 0.6 copy-start.13
  61.7 0.8 copy-start.2
  62.6 0.8 copy-start.4
  63.3 0.7 copy-start.6
  64.0 0.7 copy-start.12
  64.7 0.7 copy-start.14
  65.5 0.7 copy-start.17
  68.7 23.8 %all-to-all-start.1 = ((bf16[8,32,2304]{2,1,0:T(8,128)(2,1)}), bf16[8,32,2304]{2,1,0:T(8,128)(2,1)S(1)}, u32[]{:S(2)}, u32[]{:S(2)}) async-start(bf16[8,32,2304]{2,1,0:T(8,128)(2,1)} %residual.1), calls=%async_computation.1 | async-start | bytes 2359296 | tf_op jit(solution)/shard_map/all_to_all | solution.py:366
  96.9 5.4 %collective-permute-start.6 = (f32[4,256,256]{2,1,0:T(8,128)S(1)}, f32[4,256,256]{2,1,0:T(8,128)S(1)}, u32[]{:S(2)}, u32[]{:S(2)}) collective-permute-start(f32[4,256,256]{2,1,0:T(8,128)S(1)} %margin.3), channel_id=1, source_target_pairs={{0,32},{32,0},{1,33},{33,1},{2,34},{34,2},{3,35},{35,3},{4,36},{36... | collective-permute-start | bytes 3145736 | tf_op jit(solution)/shard_map/ppermute | solution.py:389
  141.3 39.0 %copy-start.19 = (f32[8,256]{1,0:T(8,128)}, f32[8,256]{1,0:T(8,128)S(1)}, u32[]{:S(2)}) copy-start(f32[8,256]{1,0:T(8,128)S(1)} %reduce_sum.9) | copy-start | bytes 24580
  166.8 5.0 %collective-permute-start.7 = (bf16[4,256,256]{2,1,0:T(8,128)(2,1)S(1)}, bf16[4,256,256]{2,1,0:T(8,128)(2,1)S(1)}, u32[]{:S(2)}, u32[]{:S(2)}) collective-permute-start(bf16[4,256,256]{2,1,0:T(8,128)(2,1)S(1)} %bitcast.17), channel_id=1, source_target_pairs={{0,32},{32,0},{1,33},{33,1},{2,34},{34,2},{3,35},{35,3},{4,36},{36... | collective-permute-start | bytes 1572872 | tf_op jit(solution)/shard_map/ppermute | solution.py:395

commit v4 on v3

--- a/solution.py
+++ b/solution.py
@@ -24,11 +24,12 @@
 WIDTH = 6
 DOM = ("z", "y")
 BAND = ("x", "core")
-EACH = ("x", "z", "y")
+SHORT = ("x", "y")
 F32 = jnp.float32
 BF16 = jnp.bfloat16
 VMEM = pl.BlockSpec(memory_space=pltpu.VMEM)
 SMEM = pl.BlockSpec(memory_space=pltpu.SMEM)
+ANY = pl.BlockSpec(memory_space=pl.ANY)
 
 
 def params(mib):
@@ -115,13 +116,21 @@
     right_ref,
     den_ref,
     mine_ref,
+    coupling_ref,
+    below_hbm,
+    above_hbm,
+    h_ref,
+    pay_ref,
     below_ref,
     above_ref,
-    coupling_ref,
-    h_ref,
-    table_ref,
-    nd_ref,
+    sems,
 ):
+    late = [
+        pltpu.make_async_copy(below_hbm, below_ref, sems.at[0]),
+        pltpu.make_async_copy(above_hbm, above_ref, sems.at[1]),
+    ]
+    for copy in late:
+        copy.start()
     rows, cells = x_ref.shape
     plane = cells // planes
     n = BS // 4
@@ -153,40 +162,79 @@
     num = lax.fori_loop(0, plane // BS, halo, (zero,) * (rows // 16))
     num = jnp.concatenate(num, axis=0)
 
+    for copy in late:
+        copy.wait()
     lane = lax.broadcasted_iota(jnp.int32, (rows, BS), 1)
     row = lax.broadcasted_iota(jnp.int32, (rows, BS), 0)
     total = mine_ref[...]
     total += pltpu.roll(below_ref[...], 3 * n, 1)
     total += pltpu.roll(above_ref[...], n, 1)
     table = total * coupling_ref[...]
-    table_ref[...] = table
     num = jnp.sum(num + table * total, axis=1, keepdims=True)
     den = jnp.sum(den_ref[...], axis=1, keepdims=True)
     line = jnp.where(lane == row, num, 0.0) + jnp.where(lane == row + rows, den, 0.0)
     line = jnp.sum(line, axis=0, keepdims=True)
-    nd_ref[...] = jnp.broadcast_to(line[None], nd_ref.shape)
+
+    short = rows // 4
+    packed = None
+    for g in range(4):
+        piece = table[g * short : (g + 1) * short]
+        piece = piece if g == 1 else pltpu.roll(piece, (g + 3) % 4 * n, 1)
+        packed = piece if packed is None else packed + piece
+    for r in range(short):
+        pay_ref[:, r] = jnp.broadcast_to(packed[r : r + 1][None], (pay_ref.shape[0], 1, BS))
+    pay_ref[:, short] = jnp.broadcast_to(line[None], (pay_ref.shape[0], 1, BS))
 
 
 def residual_kernel(
     planes,
     block_ref,
+    near_ref,
     h_ref,
     x_ref,
-    nd_ref,
+    pay_ref,
+    proj_hbm,
+    onehot_hbm,
+    r_ref,
+    full_ref,
     proj_ref,
     onehot_ref,
-    mine_ref,
-    below_ref,
-    above_ref,
-    r_ref,
-    full_ref,
+    sems,
 ):
+    late = [
+        pltpu.make_async_copy(proj_hbm, proj_ref, sems.at[0]),
+        pltpu.make_async_copy(onehot_hbm, onehot_ref, sems.at[1]),
+    ]
+    for copy in late:
+        copy.start()
     rows, cells = x_ref.shape
     plane = cells // planes
     slots = proj_ref.shape[0]
     n = BS // 4
-    table = mine_ref[...] + pltpu.roll(below_ref[...], 3 * n, 1)
-    table += pltpu.roll(above_ref[...], n, 1)
+    short = rows // 4
+    lane = lax.broadcasted_iota(jnp.int32, (rows, BS), 1)
+    row = lax.broadcasted_iota(jnp.int32, (rows, BS), 0)
+    sums = jnp.sum(pay_ref[:, short], axis=0)
+    num = jnp.sum(jnp.where(lane == row, sums, 0.0), axis=1, keepdims=True)
+    den = jnp.sum(jnp.where(lane == row + rows, sums, 0.0), axis=1, keepdims=True)
+    energy = jnp.broadcast_to(num / den, (rows, BS))
+    for at in range(0, cells, BS):
+        where = slice(at, at + BS)
+        full_ref[:, where] = h_ref[:, where] - energy * x_ref[:, where].astype(F32)
+
+    table = jnp.zeros((rows, BS), F32)
+    for section in range(3):
+        packed = jnp.concatenate(
+            [pay_ref[near_ref[section], r] for r in range(short)], axis=0
+        )
+        pieces = [
+            packed if g == section else pltpu.roll(packed, (section - g) % 4 * n, 1)
+            for g in range(4)
+        ]
+        whole = jnp.concatenate(pieces, axis=0)
+        table += jnp.where((lane >= section * n) & (lane < (section + 1) * n), whole, 0.0)
+    for copy in late:
+        copy.wait()
     value = lax.dot_general(
         table,
         onehot_ref[...],
@@ -194,16 +242,6 @@
         precision=lax.Precision.HIGHEST,
         preferred_element_type=F32,
     )
-    lane = lax.broadcasted_iota(jnp.int32, (rows, BS), 1)
-    row = lax.broadcasted_iota(jnp.int32, (rows, BS), 0)
-    sums = jnp.sum(nd_ref[...], axis=0)
-    num = jnp.sum(jnp.where(lane == row, sums, 0.0), axis=1, keepdims=True)
-    den = jnp.sum(jnp.where(lane == row + rows, sums, 0.0), axis=1, keepdims=True)
-    energy = jnp.broadcast_to(num / den, (rows, BS))
-    for at in range(0, cells, BS):
-        where = slice(at, at + BS)
-        full_ref[:, where] = h_ref[:, where] - energy * x_ref[:, where].astype(F32)
-
     for s in range(slots):
         where = pl.ds(pl.multiple_of(block_ref[s] * BS, BS), BS)
         full_ref[:, where] += value[:, s : s + 1] * proj_ref[s : s + 1, :]
@@ -216,12 +254,13 @@
             r_ref[c, :, p * part : (p + 1) * part] = full_ref[:, src : src + part].astype(BF16)
 
 
-def margin_kernel(planes, core_ref, locked_ref, r_ref, out_ref):
+def margin_kernel(planes, core_ref, *refs):
+    *locked_refs, r_ref, out_ref = refs
     part = r_ref.shape[1] // planes
     acc = None
     for p in range(planes):
         term = lax.dot_general(
-            locked_ref[p, 0, 0],
+            locked_refs[p][0, 0, 0],
             r_ref[:, p * part : (p + 1) * part],
             (((1,), (1,)), ((), ())),
             preferred_element_type=F32,
@@ -230,7 +269,8 @@
     out_ref[0] = acc
 
 
-def clean_kernel(core_ref, locked_ref, mine_ref, other_ref, r_ref, out_ref, turned_ref):
+def clean_kernel(core_ref, *refs):
+    *locked_refs, mine_ref, other_ref, r_ref, out_ref, turned_ref = refs
     n_x = mine_ref.shape[0]
     core = core_ref[0]
 
@@ -245,7 +285,7 @@
         for i in range(n_x):
             term = jnp.dot(
                 turned_ref[side, i],
-                locked_ref[0, i, jnp.where(side == 0, core, 1 - core)],
+                locked_refs[i][0, 0, jnp.where(side == 0, core, 1 - core)],
                 preferred_element_type=F32,
             )
             acc = term if acc is None else acc + term
@@ -273,6 +313,8 @@
     domains = lax.axis_size(DOM)
     groups = lax.axis_size(BAND)
     n_x = lax.axis_size("x")
+    n_z = lax.axis_size("z")
+    n_y = lax.axis_size("y")
     core = lax.axis_index("core").astype(jnp.int32)
     here = lax.axis_index(DOM)
     slots = slot_block.shape[0]
@@ -326,43 +368,41 @@
         name="local",
     )(x, pot, weights)
 
-    hamilton, table, sums = pl.pallas_call(
+    hamilton, pay = pl.pallas_call(
         functools.partial(hamilton_kernel, planes),
         out_shape=(
             jax.ShapeDtypeStruct((rows, cells), F32),
-            jax.ShapeDtypeStruct((rows, BS), F32),
-            jax.ShapeDtypeStruct((domains, 1, BS), F32),
+            jax.ShapeDtypeStruct((domains, rows // 4 + 1, 1, BS), F32),
         ),
-        in_specs=[VMEM] * 9,
-        out_specs=(VMEM, VMEM, VMEM),
+        in_specs=[VMEM] * 7 + [ANY] * 2,
+        out_specs=(VMEM, VMEM),
+        scratch_shapes=[
+            pltpu.VMEM((rows, BS), F32),
+            pltpu.VMEM((rows, BS), F32),
+            pltpu.SemaphoreType.DMA((2,)),
+        ],
         compiler_params=params(24),
         cost_estimate=cost(5),
         name="hamilton",
-    )(h0, x, left, right, den, shares, below, above, coupling_row)
-    table_below = lax.ppermute(table, DOM, up)
-    table_above = lax.ppermute(table, DOM, down)
-    sums = lax.all_to_all(sums, DOM, 0, 0, tiled=True)
+    )(h0, x, left, right, den, shares, coupling_row, below, above)
+    pay = lax.all_to_all(pay, DOM, 0, 0, tiled=True)
+    near = (here + domains + jnp.arange(-1, 2, dtype=jnp.int32)) % domains
 
     residual = pl.pallas_call(
         functools.partial(residual_kernel, planes),
         out_shape=jax.ShapeDtypeStruct((groups, rows, width), BF16),
-        in_specs=[SMEM] + [VMEM] * 8,
+        in_specs=[SMEM, SMEM] + [VMEM] * 3 + [ANY] * 2,
         out_specs=VMEM,
-        scratch_shapes=[pltpu.VMEM((rows, cells), F32)],
+        scratch_shapes=[
+            pltpu.VMEM((rows, cells), F32),
+            pltpu.VMEM((slots, BS), F32),
+            pltpu.VMEM((BS, BS), F32),
+            pltpu.SemaphoreType.DMA((2,)),
+        ],
         compiler_params=params(24),
         cost_estimate=cost(2),
         name="residual",
-    )(
-        slot_block,
-        hamilton,
-        x,
-        sums,
-        projectors,
-        onehot,
-        table,
-        table_below,
-        table_above,
-    )
+    )(slot_block, near.astype(jnp.int32), hamilton, x, pay, projectors, onehot)
     residual = lax.all_to_all(residual, BAND, 0, 0, tiled=True).reshape(bands, width)
 
     by_plane = locked.transpose(1, 0, 2).reshape(planes, n_x, 2, share_rows, part)
@@ -376,22 +416,30 @@
                 num_scalar_prefetch=1,
                 grid=(n_x,),
                 in_specs=[
-                    pl.BlockSpec((planes, 1, 1, share_rows, part), lambda i, c: (0, i, c[0], 0, 0)),
-                    pl.BlockSpec((bands, width), lambda i, c: (0, 0)),
-                ],
+                    pl.BlockSpec(
+                        (1, 1, 1, share_rows, part), lambda i, c, p=p: (p, i, c[0], 0, 0)
+                    )
+                    for p in range(planes)
+                ]
+                + [pl.BlockSpec((bands, width), lambda i, c: (0, 0))],
                 out_specs=pl.BlockSpec((1, share_rows, bands), lambda i, c: (i, 0, 0)),
             ),
             compiler_params=params(24),
             cost_estimate=cost(3),
             name="margin",
-        )(side.reshape(1), by_plane, residual)
+        )(side.reshape(1), *[by_plane] * planes, residual)
 
     given = lax.ppermute(margin_call(1 - core), "core", swap)
     pair = margin_call(core) + given
-    share = pair.reshape(n_x * domains, -1, bands)
-    margins = jnp.sum(lax.all_to_all(share, EACH, 0, 0, tiled=True), axis=0)
-
-    coeffs = spread(margins.astype(BF16), EACH).reshape(n_x, share_rows, bands)
+    share = pair.reshape(n_x, n_z, n_y, -1, bands).transpose(0, 2, 1, 3, 4)
+    share = share.reshape(n_x * n_y, -1, bands)
+    share = jnp.sum(lax.all_to_all(share, SHORT, 0, 0, tiled=True), axis=0)
+    share = share.reshape(n_z, -1, bands)
+    margins = jnp.sum(lax.all_to_all(share, "z", 0, 0, tiled=True), axis=0)
+
+    coeffs = spread(margins.astype(BF16), "z").reshape(-1, bands)
+    coeffs = spread(coeffs, SHORT).reshape(n_x, n_y, n_z, -1, bands)
+    coeffs = coeffs.transpose(0, 2, 1, 3, 4).reshape(n_x, share_rows, bands)
     other = lax.ppermute(coeffs, "core", swap)
     whole_block = pl.BlockSpec((n_x, share_rows, bands), lambda p, c: (0, 0, 0))
     orthogonal = pl.pallas_call(
@@ -401,7 +449,10 @@
             num_scalar_prefetch=1,
             grid=(planes,),
             in_specs=[
-                pl.BlockSpec((1, n_x, 2, share_rows, part), lambda p, c: (p, 0, 0, 0, 0)),
+                pl.BlockSpec((1, 1, 2, share_rows, part), lambda p, c, i=i: (p, i, 0, 0, 0))
+                for i in range(n_x)
+            ]
+            + [
                 whole_block,
                 whole_block,
                 pl.BlockSpec((bands, part), lambda p, c: (0, p)),
@@ -412,7 +463,7 @@
         compiler_params=params(24),
         cost_estimate=cost(5),
         name="clean",
-    )(core.reshape(1), by_plane, coeffs, other, residual)
+    )(core.reshape(1), *[by_plane] * n_x, coeffs, other, residual)
     return orthogonal.transpose(1, 0, 2), margins
 
 

time: 181 us -> 169 us (0.934)
  blocking collectives: 64.1 us -> 50.5 us
  waiting for transfers between devices: 32.3 us -> 39.2 us
  local copies, waits for them, and re-layouts: 13.5 us -> 9.75 us
  starting transfers between devices: 36.8 us -> 34 us
    all_to_all x1 -> x2, blocking collectives: 38.7 us -> 28.1 us  [the longest x1 18.5 us: per_device(): share = jnp.sum(lax.all_to_all(share, SHORT, 0, 0, tiled=True), axis=0)]
    all_to_all x1, waiting for transfers between devices: 1.19 us -> 9.48 us  [per_device(): pay = lax.all_to_all(pay, DOM, 0, 0, tiled=True)]
    ppermute x2 -> x0, starting transfers between devices: 4.86 us -> none  [the longest x1 3.56 us: per_device(): table_above = lax.ppermute(table, DOM, down)]
    unnamed x44 -> x32, local copies, waits for them, and re-layouts: 10.1 us -> 6.22 us
    all_to_all x1 -> x2, blocking collectives: 25.4 us -> 22.3 us  [spread(): lax.all_to_all(jnp.broadcast_to(value[None], (size,) + value.shape), axis...]
  transfers between devices with their start and end apart: 10 -> 8, of which waited for: 5 -> 4; matrix products, arithmetic and copies ran while one was open for 0% -> 0% of each run, Pallas kernels for 7% -> 7%
where the time goes in v4:
time: 169 us; the launch traced here: 168 us
  blocking collectives  50.5 us (30%)
  waiting for transfers between devices  39.2 us (23%)
  starting transfers between devices  34 us (20%)
  Pallas kernels  32.6 us (19%)
  local copies, waits for them, and re-layouts  9.75 us (6%)
    all_to_all x2, blocking collectives, spread(): lax.all_to_all(jnp.broadcast_to(value[None], (size,) + value.shape), axis...  22.3 us
    all_to_all x1, blocking collectives, per_device(): share = jnp.sum(lax.all_to_all(share, SHORT, 0, 0, tiled=True), axis=0)  18.5 us
    all_to_all x1, waiting for transfers between devices, per_device(): lax.all_to_all(residual, BAND, 0, 0, tiled=True).reshape(bands, width)  16.5 us
    ppermute x1, waiting for transfers between devices, per_device(): below = lax.ppermute(shares, DOM, up)  11.7 us
    all_to_all x1, blocking collectives, per_device(): margins = jnp.sum(lax.all_to_all(share, 'z', 0, 0, tiled=True), axis=0)  9.6 us
    all_to_all x1, waiting for transfers between devices, per_device(): pay = lax.all_to_all(pay, DOM, 0, 0, tiled=True)  9.48 us
    pallas_call x2, Pallas kernels, margin_call(): pl.pallas_call(functools.partial(margin_kernel, planes), out_shape=jax.Sh...  9.11 us
    pallas_call x1, Pallas kernels, per_device(): pl.pallas_call(clean_kernel, out_shape=jax.ShapeDtypeStruct((planes, band...  8.37 us
  transfers between devices with their start and end apart: 8, of which 4 were waited for; matrix products, arithmetic and copies ran while one was open for 0% of the time, Pallas kernels for 7%

profile of v4, /device:TPU:1, one launch (start us, length us, event | category | flops | bytes accessed | tf_op | source)
XLA Modules:
  0.0 167.9 jit_solution(10445900842782020811)
XLA Ops:
  0.6 0.0 copy-start.14
  0.6 0.0 copy-start.4
  0.7 0.0 copy-start.10
  0.7 0.0 copy-start.12
  0.7 3.1 %reshape.45.x_ref = bf16[32,18432]{1,0:T(8,128)(2,1)S(1)} reshape(bf16[32,6,48,64]{3,2,1,0:T(8,128)(2,1)} %param.9) | data formatting | bytes 2359296 | tf_op jit(solution)/shard_map/reshape | solution.py:330
  3.8 0.0 copy-start
  3.8 2.2 %collective-permute-start = (bf16[32,18432]{1,0:T(8,128)(2,1)S(1)}, bf16[32,18432]{1,0:T(8,128)(2,1)}, u32[]{:S(2)}, u32[]{:S(2)}) collective-permute-start(bf16[32,18432]{1,0:T(8,128)(2,1)S(1)} %reshape.45.x_ref), channel_id=1, source_target_pairs={{0,1},{1,2},{2,3},{3,4},{4,5},{5,6},{6,7},{7,8},{8,9},{9,10},{10,1... | collective-permute-start | bytes 3538952 | tf_op jit(solution)/shard_map/ppermute | solution.py:331
  6.0 6.8 %collective-permute-start.1 = (bf16[32,18432]{1,0:T(8,128)(2,1)S(1)}, bf16[32,18432]{1,0:T(8,128)(2,1)}, u32[]{:S(2)}, u32[]{:S(2)}) collective-permute-start(bf16[32,18432]{1,0:T(8,128)(2,1)S(1)} %reshape.45.x_ref), channel_id=1, source_target_pairs={{1,0},{2,1},{3,2},{4,3},{5,4},{6,5},{7,6},{8,7},{9,8},{10,9},{11,1... | collective-permute-start | bytes 3538952 | tf_op jit(solution)/shard_map/ppermute | solution.py:332
  13.5 0.0 copy-done.14
  13.5 0.1 fusion.onehot_ref.onehot_hbm
  13.6 0.0 copy-done.4
  13.6 0.0 copy-done.10
  13.6 1.6 inner.1.mine_ref
  15.2 0.0 copy-start.1
  15.2 0.6 copy-done.1
  15.9 0.0 collective-permute-start.2
  15.9 4.8 %collective-permute-start.3 = (f32[32,128]{1,0:T(8,128)S(1)}, f32[32,128]{1,0:T(8,128)S(1)}, u32[]{:S(2)}, u32[]{:S(2)}) collective-permute-start(f32[32,128]{1,0:T(8,128)S(1)} %inner.1.mine_ref), channel_id=1, source_target_pairs={{1,0},{2,1},{3,2},{4,3},{5,4},{6,5},{7,6},{8,7},{9,8},{10,9},{11,1... | collective-permute-start | bytes 49160 | tf_op jit(solution)/shard_map/ppermute | solution.py:355
  20.7 0.0 copy-done.12
  20.7 0.1 reshape.46.pot_ref
  20.8 0.0 copy-done
  20.8 0.0 copy-start.15
  20.8 6.3 %local.1 = (f32[32,18432]{1,0:T(8,128)S(1)}, f32[32,128]{1,0:T(8,128)S(1)}) custom-call(bf16[32,18432]{1,0:T(8,128)(2,1)S(1)} %reshape.45.x_ref, f32[1,18432]{1,0:T(1,128)S(1)} %reshape.46.pot_ref, bf16[3,1024,256]{2,1,0:T(8,128)(2,1)S(1)} %copy-done), custom_call_target="tpu_custom_call" | custom-call | bytes 21000000 | tf_op jit(solution)/shard_map/local/pallas_call | solution.py:357
  27.1 0.0 copy-done.15
  27.1 0.1 pad.9.coupling_ref
  27.2 11.7 %collective-permute-done.2.below_hbm = f32[32,128]{1,0:T(8,128)S(1)} collective-permute-done((f32[32,128]{1,0:T(8,128)S(1)}, f32[32,128]{1,0:T(8,128)S(1)}, u32[]{:S(2)}, u32[]{:S(2)}) %collective-permute-start.2) | collective-permute-done | bytes 16416 | tf_op jit(solution)/shard_map/ppermute | solution.py:354
  38.9 0.0 copy-start.6
  38.9 0.6 copy-done.6
  39.5 0.0 collective-permute-done.3.above_hbm
  39.5 0.0 copy-start.8
  39.5 0.6 copy-done.8
  40.1 0.0 collective-permute-done.left_ref
  40.1 0.0 collective-permute-done.1.right_ref
  40.1 0.0 copy-start.7
  40.1 0.7 copy-done.7
  40.8 0.0 copy-start.9
  40.8 0.7 copy-done.9
  41.5 3.9 %hamilton.1 = (f32[32,18432]{1,0:T(8,128)S(1)}, f32[32,9,1,128]{3,2,1,0:T(1,128)S(1)}) custom-call(f32[32,18432]{1,0:T(8,128)S(1)} %get-tuple-element.6.h0_ref, bf16[32,18432]{1,0:T(8,128)(2,1)S(1)} %reshape.45.x_ref, bf16[32,18432]{1,0:T(8,128)(2,1)} %collective-permute-done.left_ref, bf16[32,18432]{1,0:T(8,128)(2,1)} %collective-permute-done.1.right_ref, ...), custom_call_target="tpu_custom_call" | custom-call | bytes 15000000 | tf_op jit(solution)/shard_map/hamilton/pallas_call | solution.py:371
  45.5 0.0 copy-start.3
  45.5 0.7 copy-done.3
  46.1 6.6 %all-to-all-start = ((f32[32,9,1,128]{3,2,1,0:T(1,128)}), f32[32,9,1,128]{3,2,1,0:T(1,128)}, u32[]{:S(2)}, u32[]{:S(2)}) async-start(f32[32,9,1,128]{3,2,1,0:T(1,128)} %copy-done.3), calls=%async_computation | async-start | bytes 294912 | tf_op jit(solution)/shard_map/all_to_all | solution.py:388
  52.8 9.5 %all-to-all-done.pay_ref = f32[32,9,1,128]{3,2,1,0:T(1,128)} async-done(((f32[32,9,1,128]{3,2,1,0:T(1,128)}), f32[32,9,1,128]{3,2,1,0:T(1,128)}, u32[]{:S(2)}, u32[]{:S(2)}) %all-to-all-start) | async-done | bytes 147488 | tf_op jit(solution)/shard_map/all_to_all | solution.py:388
  62.2 0.8 copy-done.2
  63.1 0.8 copy-done.5
  63.8 0.7 copy-done.11
  64.5 3.3 %residual.1 = bf16[8,32,2304]{2,1,0:T(8,128)(2,1)} custom-call(s32[64]{0:T(128)S(1)} %copy-done.11, s32[3]{0:T(128)S(1)} %and_select_fusion.3.near_ref, f32[32,18432]{1,0:T(8,128)S(1)} %get-tuple-element.8.h_ref, bf16[32,18432]{1,0:T(8,128)(2,1)S(1)} %reshape.45.x_ref, f32[32,9,1,128]{3,2,1,0:T(1,128)} %all-to-all-done.pay_ref, f32[64,128]{1,0:T(8,128)S(1)} %copy-done.5, ...), custom_call_target="tpu_custom_call" | custom-call | bytes 6000000 | tf_op jit(solution)/shard_map/residual/pallas_call | solution.py:391
  67.8 7.6 %all-to-all-start.1 = ((bf16[8,32,2304]{2,1,0:T(8,128)(2,1)}), bf16[8,32,2304]{2,1,0:T(8,128)(2,1)S(1)}, u32[]{:S(2)}, u32[]{:S(2)}) async-start(bf16[8,32,2304]{2,1,0:T(8,128)(2,1)} %residual.1), calls=%async_computation.1 | async-start | bytes 2359296 | tf_op jit(solution)/shard_map/all_to_all | solution.py:406
  75.4 16.5 %all-to-all-done.1 = bf16[8,32,2304]{2,1,0:T(8,128)(2,1)S(1)} async-done(((bf16[8,32,2304]{2,1,0:T(8,128)(2,1)}), bf16[8,32,2304]{2,1,0:T(8,128)(2,1)S(1)}, u32[]{:S(2)}, u32[]{:S(2)}) %all-to-all-start.1) | async-done | bytes 1179680 | tf_op jit(solution)/shard_map/all_to_all | solution.py:406
  91.9 4.6 %margin.3 = f32[4,256,256]{2,1,0:T(8,128)S(1)} custom-call(s32[1]{0:T(128)} %bitcast.7.core_ref, bf16[6,4,2,256,384]{4,3,2,1,0:T(8,128)(2,1)} %bitcast.27, bf16[6,4,2,256,384]{4,3,2,1,0:T(8,128)(2,1)} %bitcast.28, bf16[6,4,2,256,384]{4,3,2,1,0:T(8,128)(2,1)} %bitcast.29, bf16[6,4,2,256,384]{4,3,2,1,0:T(8,128)(2,1)} %bitcast.30, ...), custom_call_target="tpu_custom_call" | custom-call | bytes 9000000 | tf_op jit(solution)/shard_map/margin/pallas_call | solution.py:412
  96.5 1.0 collective-permute-start.4
  97.4 4.6 %margin.2 = f32[4,256,256]{2,1,0:T(8,128)S(1)} custom-call(s32[1]{0:T(128)} %bitcast.core_ref, bf16[6,4,2,256,384]{4,3,2,1,0:T(8,128)(2,1)} %bitcast.33, bf16[6,4,2,256,384]{4,3,2,1,0:T(8,128)(2,1)} %bitcast.34, bf16[6,4,2,256,384]{4,3,2,1,0:T(8,128)(2,1)} %bitcast.35, bf16[6,4,2,256,384]{4,3,2,1,0:T(8,128)(2,1)} %bitcast.36, ...), custom_call_target="tpu_custom_call" | custom-call | bytes 9000000 | tf_op jit(solution)/shard_map/margin/pallas_call | solution.py:412
  102.0 0.0 collective-permute-done.4
  102.0 0.1 add.55
  102.1 0.1 copy.13
  102.3 18.5 %all_to_all.30 = f32[16,64,256]{2,1,0:T(8,128)S(1)} all-to-all(f32[16,64,256]{2,1,0:T(8,128)S(1)} %bitcast.44), channel_id=1, replica_groups=mesh['x'=4,'core'=2,'z'=8,'y'=4] {'x','y'}, dimensions={0} | all-to-all | bytes 2097152 | tf_op jit(solution)/shard_map/all_to_all | solution.py:436
  120.8 0.1 reduce_sum.18
  120.9 9.6 %all_to_all.31 = f32[8,8,256]{2,1,0:T(8,128)S(1)} all-to-all(f32[8,8,256]{2,1,0:T(8,128)S(1)} %bitcast.47), channel_id=1, replica_groups=mesh['x'=4,'core'=2,'z'=8,'y'=4] {'z'}, dimensions={0} | all-to-all | bytes 131072 | tf_op jit(solution)/shard_map/all_to_all | solution.py:438
  130.5 0.0 copy-start.13
  130.5 9.2 %all_to_all.32 = bf16[8,8,256]{2,1,0:T(8,128)(2,1)S(1)} all-to-all(bf16[8,8,256]{2,1,0:T(8,128)(2,1)S(1)} %broadcast_in_dim.33), channel_id=1, replica_groups=mesh['x'=4,'core'=2,'z'=8,'y'=4] {'z'}, dimensions={0} | all-to-all | bytes 65536 | tf_op jit(solution)/shard_map/all_to_all | solution.py:302
  139.8 13.1 %all_to_all.33 = bf16[16,64,256]{2,1,0:T(8,128)(2,1)S(1)} all-to-all(bf16[16,64,256]{2,1,0:T(8,128)(2,1)S(1)} %broadcast_in_dim.35), channel_id=1, replica_groups=mesh['x'=4,'core'=2,'z'=8,'y'=4] {'x','y'}, dimensions={0} | all-to-all | bytes 1048576 | tf_op jit(solution)/shard_map/all_to_all | solution.py:302
  152.9 0.1 copy.14
  153.0 0.0 copy-done.13
  153.0 5.0 %collective-permute-start.5 = (bf16[4,256,256]{2,1,0:T(8,128)(2,1)S(1)}, bf16[4,256,256]{2,1,0:T(8,128)(2,1)S(1)}, u32[]{:S(2)}, u32[]{:S(2)}) collective-permute-start(bf16[4,256,256]{2,1,0:T(8,128)(2,1)S(1)} %bitcast.25), channel_id=1, source_target_pairs={{0,32},{32,0},{1,33},{33,1},{2,34},{34,2},{3,35},{35,3},{4,36},{36... | collective-permute-start | bytes 1572872 | tf_op jit(solution)/shard_map/ppermute | solution.py:443
  157.9 1.5 collective-permute-done.5.refs_5_
  159.5 8.4 %clean.1 = bf16[6,256,384]{2,1,0:T(8,128)(2,1)} custom-call(s32[1]{0:T(128)} %bitcast.core_ref, bf16[6,4,2,256,384]{4,3,2,1,0:T(8,128)(2,1)} %bitcast.39, bf16[6,4,2,256,384]{4,3,2,1,0:T(8,128)(2,1)} %bitcast.40, bf16[6,4,2,256,384]{4,3,2,1,0:T(8,128)(2,1)} %bitcast.41, bf16[6,4,2,256,384]{4,3,2,1,0:T(8,128)(2,1)} %bitcast.42, ...), custom_call_target="tpu_custom_call" | custom-call | bytes 15000000 | tf_op jit(solution)/shard_map/clean/pallas_call | solution.py:445
  (10 shorter events, 0.1 us)
Async XLA Ops:
  0.6 12.8 %copy-start.14 = (s32[64]{0:T(128)S(1)}, s32[64]{0:T(128)}, u32[]{:S(2)}) copy-start(s32[64]{0:T(128)} %param.14) | copy-start | bytes 772
  0.6 13.0 %copy-start.4 = (f32[64,128]{1,0:T(8,128)S(1)}, f32[64,128]{1,0:T(8,128)}, u32[]{:S(2)}) copy-start(f32[64,128]{1,0:T(8,128)} %proj_hbm.1) | copy-start | bytes 98308
  0.7 13.0 %copy-start.10 = (s32[64]{0:T(128)S(1)}, s32[64]{0:T(128)}, u32[]{:S(2)}) copy-start(s32[64]{0:T(128)} %block_ref.3) | copy-start | bytes 772
  0.7 20.0 %copy-start.12 = (f32[6,48,64]{2,1,0:T(8,128)S(1)}, f32[6,48,64]{2,1,0:T(8,128)}, u32[]{:S(2)}) copy-start(f32[6,48,64]{2,1,0:T(8,128)} %param.10) | copy-start | bytes 221188
  3.8 17.0 %copy-start = (bf16[3,1024,256]{2,1,0:T(8,128)(2,1)S(1)}, bf16[3,1024,256]{2,1,0:T(8,128)(2,1)}, u32[]{:S(2)}) copy-start(bf16[3,1024,256]{2,1,0:T(8,128)(2,1)} %constant.73.clone.w_ref) | copy-start | bytes 4718596
  3.8 36.3 %collective-permute-start = (bf16[32,18432]{1,0:T(8,128)(2,1)S(1)}, bf16[32,18432]{1,0:T(8,128)(2,1)}, u32[]{:S(2)}, u32[]{:S(2)}) collective-permute-start(bf16[32,18432]{1,0:T(8,128)(2,1)S(1)} %reshape.45.x_ref), channel_id=1, source_target_pairs={{0,1},{1,2},{2,3},{3,4},{4,5},{5,6},{6,7},{7,8},{8,9},{9,10},{10,1... | collective-permute-start | bytes 3538952 | tf_op jit(solution)/shard_map/ppermute | solution.py:331
  6.0 34.1 %collective-permute-start.1 = (bf16[32,18432]{1,0:T(8,128)(2,1)S(1)}, bf16[32,18432]{1,0:T(8,128)(2,1)}, u32[]{:S(2)}, u32[]{:S(2)}) collective-permute-start(bf16[32,18432]{1,0:T(8,128)(2,1)S(1)} %reshape.45.x_ref), channel_id=1, source_target_pairs={{1,0},{2,1},{3,2},{4,3},{5,4},{6,5},{7,6},{8,7},{9,8},{10,9},{11,1... | collective-permute-start | bytes 3538952 | tf_op jit(solution)/shard_map/ppermute | solution.py:332
  15.2 0.6 copy-start.1
  15.9 23.0 %collective-permute-start.2 = (f32[32,128]{1,0:T(8,128)S(1)}, f32[32,128]{1,0:T(8,128)S(1)}, u32[]{:S(2)}, u32[]{:S(2)}) collective-permute-start(f32[32,128]{1,0:T(8,128)S(1)} %inner.1.mine_ref), channel_id=1, source_target_pairs={{0,1},{1,2},{2,3},{3,4},{4,5},{5,6},{6,7},{7,8},{8,9},{9,10},{10,1... | collective-permute-start | bytes 49160 | tf_op jit(solution)/shard_map/ppermute | solution.py:354
  15.9 23.6 %collective-permute-start.3 = (f32[32,128]{1,0:T(8,128)S(1)}, f32[32,128]{1,0:T(8,128)S(1)}, u32[]{:S(2)}, u32[]{:S(2)}) collective-permute-start(f32[32,128]{1,0:T(8,128)S(1)} %inner.1.mine_ref), channel_id=1, source_target_pairs={{1,0},{2,1},{3,2},{4,3},{5,4},{6,5},{7,6},{8,7},{9,8},{10,9},{11,1... | collective-permute-start | bytes 49160 | tf_op jit(solution)/shard_map/ppermute | solution.py:355
  20.8 6.3 %copy-start.15 = (f32[32]{0:T(128)S(1)}, f32[32]{0:T(128)}, u32[]{:S(2)}) copy-start(f32[32]{0:T(128)} %param.12) | copy-start | bytes 388
  38.9 0.6 copy-start.6
  39.5 0.6 copy-start.8
  40.1 0.7 copy-start.7
  40.8 0.7 copy-start.9
  45.5 0.7 copy-start.3
  46.1 16.1 %all-to-all-start = ((f32[32,9,1,128]{3,2,1,0:T(1,128)}), f32[32,9,1,128]{3,2,1,0:T(1,128)}, u32[]{:S(2)}, u32[]{:S(2)}) async-start(f32[32,9,1,128]{3,2,1,0:T(1,128)} %copy-done.3), calls=%async_computation | async-start | bytes 294912 | tf_op jit(solution)/shard_map/all_to_all | solution.py:388
  62.2 0.8 copy-start.2
  63.1 0.8 copy-start.5
  63.8 0.7 copy-start.11
  67.8 24.1 %all-to-all-start.1 = ((bf16[8,32,2304]{2,1,0:T(8,128)(2,1)}), bf16[8,32,2304]{2,1,0:T(8,128)(2,1)S(1)}, u32[]{:S(2)}, u32[]{:S(2)}) async-start(bf16[8,32,2304]{2,1,0:T(8,128)(2,1)} %residual.1), calls=%async_computation.1 | async-start | bytes 2359296 | tf_op jit(solution)/shard_map/all_to_all | solution.py:406
  96.5 5.5 %collective-permute-start.4 = (f32[4,256,256]{2,1,0:T(8,128)S(1)}, f32[4,256,256]{2,1,0:T(8,128)S(1)}, u32[]{:S(2)}, u32[]{:S(2)}) collective-permute-start(f32[4,256,256]{2,1,0:T(8,128)S(1)} %margin.3), channel_id=1, source_target_pairs={{0,32},{32,0},{1,33},{33,1},{2,34},{34,2},{3,35},{35,3},{4,36},{36... | collective-permute-start | bytes 3145736 | tf_op jit(solution)/shard_map/ppermute | solution.py:432
  130.5 22.5 %copy-start.13 = (f32[8,256]{1,0:T(8,128)}, f32[8,256]{1,0:T(8,128)S(1)}, u32[]{:S(2)}) copy-start(f32[8,256]{1,0:T(8,128)S(1)} %reduce_sum.19) | copy-start | bytes 24580
  153.0 6.5 %collective-permute-start.5 = (bf16[4,256,256]{2,1,0:T(8,128)(2,1)S(1)}, bf16[4,256,256]{2,1,0:T(8,128)(2,1)S(1)}, u32[]{:S(2)}, u32[]{:S(2)}) collective-permute-start(bf16[4,256,256]{2,1,0:T(8,128)(2,1)S(1)} %bitcast.25), channel_id=1, source_target_pairs={{0,32},{32,0},{1,33},{33,1},{2,34},{34,2},{3,35},{35,3},{4,36},{36... | collective-permute-start | bytes 1572872 | tf_op jit(solution)/shard_map/ppermute | solution.py:443

commit v5 on v4

--- a/solution.py
+++ b/solution.py
@@ -60,7 +60,9 @@
     return np.stack(terms)
 
 
-def inner_kernel(block_ref, x_ref, proj_ref, onehot_ref, share_ref):
+def inner_kernel(block_ref, place_ref, x_ref, proj_ref, onehot_ref, share_ref, out_ref):
+    for i in range(out_ref.shape[0]):
+        out_ref[i] = place_ref[i]
     rows = x_ref.shape[0]
     slots = proj_ref.shape[0]
     lane = lax.broadcasted_iota(jnp.int32, (rows, BS), 1)
@@ -111,9 +113,9 @@
 def hamilton_kernel(
     planes,
     h0_ref,
-    x_ref,
-    left_ref,
-    right_ref,
+    x_hbm,
+    left_hbm,
+    right_hbm,
     den_ref,
     mine_ref,
     coupling_ref,
@@ -121,18 +123,34 @@
     above_hbm,
     h_ref,
     pay_ref,
+    x_ref,
+    left_ref,
+    right_ref,
     below_ref,
     above_ref,
     sems,
+    late_sems,
 ):
-    late = [
-        pltpu.make_async_copy(below_hbm, below_ref, sems.at[0]),
-        pltpu.make_async_copy(above_hbm, above_ref, sems.at[1]),
-    ]
-    for copy in late:
-        copy.start()
     rows, cells = x_ref.shape
     plane = cells // planes
+    chunks = sems.shape[0]
+    chunk = plane // chunks
+    copies = []
+    for k in range(chunks):
+        for p in range(planes):
+            where = slice(p * plane + k * chunk, p * plane + (k + 1) * chunk)
+            for i, (src, dst) in enumerate(
+                ((x_hbm, x_ref), (left_hbm, left_ref), (right_hbm, right_ref))
+            ):
+                copies.append(
+                    pltpu.make_async_copy(src.at[:, where], dst.at[:, where], sems.at[k, p, i])
+                )
+    late = [
+        pltpu.make_async_copy(below_hbm, below_ref, late_sems.at[0]),
+        pltpu.make_async_copy(above_hbm, above_ref, late_sems.at[1]),
+    ]
+    for copy in copies + late:
+        copy.start()
     n = BS // 4
 
     def halo(step, carry):
@@ -159,7 +177,12 @@
         return tuple(sums)
 
     zero = jnp.zeros((16, BS), F32)
-    num = lax.fori_loop(0, plane // BS, halo, (zero,) * (rows // 16))
+    num = (zero,) * (rows // 16)
+    steps = chunk // BS
+    for k in range(chunks):
+        for copy in copies[k * planes * 3 : (k + 1) * planes * 3]:
+            copy.wait()
+        num = lax.fori_loop(k * steps, (k + 1) * steps, halo, num)
     num = jnp.concatenate(num, axis=0)
 
     for copy in late:
@@ -189,26 +212,33 @@
 def residual_kernel(
     planes,
     block_ref,
-    near_ref,
+    place_ref,
     h_ref,
-    x_ref,
+    x_hbm,
     pay_ref,
     proj_hbm,
     onehot_hbm,
     r_ref,
     full_ref,
+    x_ref,
     proj_ref,
     onehot_ref,
     sems,
 ):
+    rows, cells = x_ref.shape
+    plane = cells // planes
+    copies = []
+    for p in range(planes):
+        where = slice(p * plane, (p + 1) * plane)
+        copies.append(
+            pltpu.make_async_copy(x_hbm.at[:, where], x_ref.at[:, where], sems.at[2 + p])
+        )
     late = [
         pltpu.make_async_copy(proj_hbm, proj_ref, sems.at[0]),
         pltpu.make_async_copy(onehot_hbm, onehot_ref, sems.at[1]),
     ]
-    for copy in late:
+    for copy in copies + late:
         copy.start()
-    rows, cells = x_ref.shape
-    plane = cells // planes
     slots = proj_ref.shape[0]
     n = BS // 4
     short = rows // 4
@@ -219,13 +249,15 @@
     den = jnp.sum(jnp.where(lane == row + rows, sums, 0.0), axis=1, keepdims=True)
     energy = jnp.broadcast_to(num / den, (rows, BS))
     for at in range(0, cells, BS):
+        if at % plane == 0:
+            copies[at // plane].wait()
         where = slice(at, at + BS)
         full_ref[:, where] = h_ref[:, where] - energy * x_ref[:, where].astype(F32)
 
     table = jnp.zeros((rows, BS), F32)
     for section in range(3):
         packed = jnp.concatenate(
-            [pay_ref[near_ref[section], r] for r in range(short)], axis=0
+            [pay_ref[place_ref[section], r] for r in range(short)], axis=0
         )
         pieces = [
             packed if g == section else pltpu.roll(packed, (section - g) % 4 * n, 1)
@@ -254,42 +286,59 @@
             r_ref[c, :, p * part : (p + 1) * part] = full_ref[:, src : src + part].astype(BF16)
 
 
-def margin_kernel(planes, core_ref, *refs):
-    *locked_refs, r_ref, out_ref = refs
-    part = r_ref.shape[1] // planes
-    acc = None
-    for p in range(planes):
-        term = lax.dot_general(
-            locked_refs[p][0, 0, 0],
-            r_ref[:, p * part : (p + 1) * part],
-            (((1,), (1,)), ((), ())),
-            preferred_element_type=F32,
-        )
-        acc = term if acc is None else acc + term
-    out_ref[0] = acc
-
-
-def clean_kernel(core_ref, *refs):
-    *locked_refs, mine_ref, other_ref, r_ref, out_ref, turned_ref = refs
-    n_x = mine_ref.shape[0]
-    core = core_ref[0]
-
-    @pl.when(pl.program_id(0) == 0)
-    def _():
-        for i in range(n_x):
-            turned_ref[0, i] = mine_ref[i].T
-            turned_ref[1, i] = other_ref[i].T
-
-    acc = None
-    for side in range(2):
-        for i in range(n_x):
-            term = jnp.dot(
-                turned_ref[side, i],
-                locked_refs[i][0, 0, jnp.where(side == 0, core, 1 - core)],
+def margin_kernel(side, place_ref, locked_ref, r_ref, out_ref):
+    planes, n_x, _, _, part = locked_ref.shape
+    core = place_ref[3 + side]
+    for i in range(n_x):
+        acc = None
+        for p in range(planes):
+            term = lax.dot_general(
+                locked_ref[p, i, core],
+                r_ref[:, p * part : (p + 1) * part],
+                (((1,), (1,)), ((), ())),
                 preferred_element_type=F32,
             )
             acc = term if acc is None else acc + term
-    out_ref[0] = (r_ref[...].astype(F32) - acc).astype(BF16)
+        out_ref[i] = acc
+
+
+def pair_kernel(kept_ref, given_ref, out_ref):
+    n_x, share_rows, _ = kept_ref.shape
+    n_y = out_ref.shape[0] // n_x
+    for i in range(n_x):
+        for at in range(0, share_rows, 8):
+            z, y = divmod(at // 8, n_y)
+            out_ref[i * n_y + y, z * 8 : z * 8 + 8] = (
+                kept_ref[i, at : at + 8] + given_ref[i, at : at + 8]
+            )
+
+
+def sum_kernel(in_ref, out_ref):
+    acc = in_ref[0]
+    for i in range(1, in_ref.shape[0]):
+        acc += in_ref[i]
+    out_ref[...] = acc
+
+
+def clean_kernel(side, place_ref, locked_ref, coeff_ref, r_ref, out_ref, turned_ref):
+    planes, n_x, _, share_rows, part = locked_ref.shape
+    n_y = coeff_ref.shape[0] // n_x
+    core = place_ref[3 + side]
+    for i in range(n_x):
+        pieces = [coeff_ref[i * n_y + y].astype(F32) for y in range(n_y)]
+        whole = [
+            pieces[at % n_y][at // n_y * 8 : at // n_y * 8 + 8] for at in range(share_rows // 8)
+        ]
+        turned_ref[i] = jnp.concatenate(whole, axis=0).T.astype(BF16)
+    for p in range(planes):
+        term = None
+        for i in range(n_x):
+            more = jnp.dot(turned_ref[i], locked_ref[p, i, core], preferred_element_type=F32)
+            term = more if term is None else term + more
+        if side == 0:
+            out_ref[p] = r_ref[:, p * part : (p + 1) * part].astype(F32) - term
+        else:
+            out_ref[p] = (r_ref[p] - term).astype(BF16)
 
 
 def ring(size):
@@ -342,15 +391,21 @@
     onehot = (column[:, None] == jnp.arange(BS, dtype=jnp.int32)[None, :]).astype(F32)
     coupling_row = jnp.pad(coupling[None], ((0, 0), (n, BS - 2 * n)))
 
-    shares = pl.pallas_call(
+    near = (here + domains + jnp.arange(-1, 2, dtype=jnp.int32)) % domains
+    place = jnp.concatenate([near, jnp.stack([core, 1 - core]), jnp.zeros(3, jnp.int32)])
+    shares, place = pl.pallas_call(
         inner_kernel,
-        out_shape=jax.ShapeDtypeStruct((rows, BS), F32),
-        in_specs=[SMEM, VMEM, VMEM, VMEM],
-        out_specs=VMEM,
+        out_shape=(
+            jax.ShapeDtypeStruct((rows, BS), F32),
+            jax.ShapeDtypeStruct((8,), jnp.int32),
+        ),
+        in_specs=[SMEM, SMEM, VMEM, VMEM, VMEM],
+        out_specs=(VMEM, SMEM),
         compiler_params=params(8),
         cost_estimate=cost(2),
         name="inner",
-    )(slot_block, x, projectors, onehot)
+    )(slot_block, place.astype(jnp.int32), x, projectors, onehot)
+    x_hbm = pltpu.with_memory_space_constraint(x, pltpu.HBM)
     below = lax.ppermute(shares, DOM, up)
     above = lax.ppermute(shares, DOM, down)
 
@@ -374,96 +429,86 @@
             jax.ShapeDtypeStruct((rows, cells), F32),
             jax.ShapeDtypeStruct((domains, rows // 4 + 1, 1, BS), F32),
         ),
-        in_specs=[VMEM] * 7 + [ANY] * 2,
+        in_specs=[VMEM] + [ANY] * 3 + [VMEM] * 3 + [ANY] * 2,
         out_specs=(VMEM, VMEM),
-        scratch_shapes=[
-            pltpu.VMEM((rows, BS), F32),
-            pltpu.VMEM((rows, BS), F32),
-            pltpu.SemaphoreType.DMA((2,)),
-        ],
+        scratch_shapes=[pltpu.VMEM((rows, cells), BF16)] * 3
+        + [pltpu.VMEM((rows, BS), F32)] * 2
+        + [pltpu.SemaphoreType.DMA((3, planes, 3)), pltpu.SemaphoreType.DMA((2,))],
         compiler_params=params(24),
         cost_estimate=cost(5),
         name="hamilton",
-    )(h0, x, left, right, den, shares, coupling_row, below, above)
+    )(h0, x_hbm, left, right, den, shares, coupling_row, below, above)
     pay = lax.all_to_all(pay, DOM, 0, 0, tiled=True)
-    near = (here + domains + jnp.arange(-1, 2, dtype=jnp.int32)) % domains
 
     residual = pl.pallas_call(
         functools.partial(residual_kernel, planes),
         out_shape=jax.ShapeDtypeStruct((groups, rows, width), BF16),
-        in_specs=[SMEM, SMEM] + [VMEM] * 3 + [ANY] * 2,
+        in_specs=[SMEM, SMEM, VMEM, ANY, VMEM, ANY, ANY],
         out_specs=VMEM,
         scratch_shapes=[
             pltpu.VMEM((rows, cells), F32),
+            pltpu.VMEM((rows, cells), BF16),
             pltpu.VMEM((slots, BS), F32),
             pltpu.VMEM((BS, BS), F32),
-            pltpu.SemaphoreType.DMA((2,)),
+            pltpu.SemaphoreType.DMA((2 + planes,)),
         ],
         compiler_params=params(24),
         cost_estimate=cost(2),
         name="residual",
-    )(slot_block, near.astype(jnp.int32), hamilton, x, pay, projectors, onehot)
+    )(slot_block, place, hamilton, x_hbm, pay, projectors, onehot)
     residual = lax.all_to_all(residual, BAND, 0, 0, tiled=True).reshape(bands, width)
 
     by_plane = locked.transpose(1, 0, 2).reshape(planes, n_x, 2, share_rows, part)
-    by_plane = pltpu.with_memory_space_constraint(by_plane, pltpu.HBM)
+    by_plane = pltpu.with_memory_space_constraint(by_plane, pltpu.VMEM)
 
     def margin_call(side):
         return pl.pallas_call(
-            functools.partial(margin_kernel, planes),
+            functools.partial(margin_kernel, side),
             out_shape=jax.ShapeDtypeStruct((n_x, share_rows, bands), F32),
-            grid_spec=pltpu.PrefetchScalarGridSpec(
-                num_scalar_prefetch=1,
-                grid=(n_x,),
-                in_specs=[
-                    pl.BlockSpec(
-                        (1, 1, 1, share_rows, part), lambda i, c, p=p: (p, i, c[0], 0, 0)
-                    )
-                    for p in range(planes)
-                ]
-                + [pl.BlockSpec((bands, width), lambda i, c: (0, 0))],
-                out_specs=pl.BlockSpec((1, share_rows, bands), lambda i, c: (i, 0, 0)),
-            ),
-            compiler_params=params(24),
+            in_specs=[SMEM, VMEM, VMEM],
+            out_specs=VMEM,
+            compiler_params=params(8),
             cost_estimate=cost(3),
             name="margin",
-        )(side.reshape(1), *[by_plane] * planes, residual)
-
-    given = lax.ppermute(margin_call(1 - core), "core", swap)
-    pair = margin_call(core) + given
-    share = pair.reshape(n_x, n_z, n_y, -1, bands).transpose(0, 2, 1, 3, 4)
-    share = share.reshape(n_x * n_y, -1, bands)
-    share = jnp.sum(lax.all_to_all(share, SHORT, 0, 0, tiled=True), axis=0)
-    share = share.reshape(n_z, -1, bands)
-    margins = jnp.sum(lax.all_to_all(share, "z", 0, 0, tiled=True), axis=0)
-
-    coeffs = spread(margins.astype(BF16), "z").reshape(-1, bands)
-    coeffs = spread(coeffs, SHORT).reshape(n_x, n_y, n_z, -1, bands)
-    coeffs = coeffs.transpose(0, 2, 1, 3, 4).reshape(n_x, share_rows, bands)
+        )(place, by_plane, residual)
+
+    def small_call(kernel, shape, name, *operands):
+        return pl.pallas_call(
+            kernel,
+            out_shape=jax.ShapeDtypeStruct(shape, F32),
+            in_specs=[VMEM] * len(operands),
+            out_specs=VMEM,
+            compiler_params=params(8),
+            cost_estimate=cost(1),
+            name=name,
+        )(*operands)
+
+    given = lax.ppermute(margin_call(1), "core", swap)
+    kept = margin_call(0)
+    share = small_call(pair_kernel, (n_x * n_y, n_z * 8, bands), "pair", kept, given)
+    share = lax.all_to_all(share, SHORT, 0, 0, tiled=True)
+    share = small_call(sum_kernel, (n_z * 8, bands), "sum", share).reshape(n_z, 8, bands)
+    margins = lax.all_to_all(share, "z", 0, 0, tiled=True)
+    margins = small_call(sum_kernel, (8, bands), "sum", margins)
+
+    coeffs = spread(margins.astype(BF16), "z").reshape(n_z * 8, bands)
+    coeffs = spread(coeffs, SHORT).reshape(n_x * n_y, n_z * 8, bands)
     other = lax.ppermute(coeffs, "core", swap)
-    whole_block = pl.BlockSpec((n_x, share_rows, bands), lambda p, c: (0, 0, 0))
-    orthogonal = pl.pallas_call(
-        clean_kernel,
-        out_shape=jax.ShapeDtypeStruct((planes, bands, part), BF16),
-        grid_spec=pltpu.PrefetchScalarGridSpec(
-            num_scalar_prefetch=1,
-            grid=(planes,),
-            in_specs=[
-                pl.BlockSpec((1, 1, 2, share_rows, part), lambda p, c, i=i: (p, i, 0, 0, 0))
-                for i in range(n_x)
-            ]
-            + [
-                whole_block,
-                whole_block,
-                pl.BlockSpec((bands, part), lambda p, c: (0, p)),
-            ],
-            out_specs=pl.BlockSpec((1, bands, part), lambda p, c: (p, 0, 0)),
-            scratch_shapes=[pltpu.VMEM((2, n_x, bands, share_rows), BF16)],
-        ),
-        compiler_params=params(24),
-        cost_estimate=cost(5),
-        name="clean",
-    )(core.reshape(1), *[by_plane] * n_x, coeffs, other, residual)
+
+    def clean_call(side, coeffs, before, kind):
+        return pl.pallas_call(
+            functools.partial(clean_kernel, side),
+            out_shape=jax.ShapeDtypeStruct((planes, bands, part), kind),
+            in_specs=[SMEM, VMEM, VMEM, VMEM],
+            out_specs=VMEM,
+            scratch_shapes=[pltpu.VMEM((n_x, bands, share_rows), BF16)],
+            compiler_params=params(8),
+            cost_estimate=cost(3),
+            name="clean",
+        )(place, by_plane, coeffs, before)
+
+    part_clean = clean_call(0, coeffs, residual, F32)
+    orthogonal = clean_call(1, other, part_clean, BF16)
     return orthogonal.transpose(1, 0, 2), margins
 
 

time: 169 us -> 155 us (0.917)
  blocking collectives: 50.5 us -> 86.5 us
  waiting for transfers between devices: 39.2 us -> 16 us
  starting transfers between devices: 34 us -> 19.8 us
  local copies, waits for them, and re-layouts: 9.75 us -> 3.44 us
  Pallas kernels: 32.6 us -> 26.8 us
    all_to_all x2 -> x4, blocking collectives: 28.1 us -> 64.6 us  [the longest x1 23.7 us: per_device(): lax.all_to_all(residual, BAND, 0, 0, tiled=True).reshape(bands, width)]
    all_to_all x2 -> x0, waiting for transfers between devices: 26 us -> none  [the longest x1 16.5 us: per_device(): lax.all_to_all(residual, BAND, 0, 0, tiled=True).reshape(bands, width)]
    all_to_all x2 -> x0, starting transfers between devices: 14.2 us -> none  [the longest x1 7.63 us: per_device(): lax.all_to_all(residual, BAND, 0, 0, tiled=True).reshape(bands, width)]
    ppermute x1, waiting for transfers between devices: 0.01 us -> 10.7 us  [per_device(): above = lax.ppermute(shares, DOM, down)]
    ppermute x1, waiting for transfers between devices: 11.7 us -> 5.31 us  [per_device(): below = lax.ppermute(shares, DOM, up)]
    unnamed x32 -> x16, local copies, waits for them, and re-layouts: 6.22 us -> 0.04 us
    pallas_call x4 -> x8, Pallas kernels: 19.1 us -> 13.4 us  [the longest x2 5.93 us: clean_call(): pl.pallas_call(functools.partial(clean_kernel, side), out_shape=jax.Shape...]
    ppermute x1, starting transfers between devices: 2.2 us -> 0.01 us  [per_device(): left = lax.ppermute(x, DOM, up)]
  transfers between devices with their start and end apart: 8 -> 6, of which waited for: 4 -> 2; matrix products, arithmetic and copies ran while one was open for 0% -> 0% of each run, Pallas kernels for 7% -> 8%
where the time goes in v5:
time: 155 us
  blocking collectives  86.5 us (56%)
  Pallas kernels  26.8 us (17%)
  starting transfers between devices  19.8 us (13%)
  waiting for transfers between devices  16 us (10%)
  local copies, waits for them, and re-layouts  3.44 us (2%)
    all_to_all x1, blocking collectives, per_device(): lax.all_to_all(residual, BAND, 0, 0, tiled=True).reshape(bands, width)  23.7 us
    all_to_all x2, blocking collectives, spread(): lax.all_to_all(jnp.broadcast_to(value[None], (size,) + value.shape), axis...  21.9 us
    all_to_all x1, blocking collectives, per_device(): share = lax.all_to_all(share, SHORT, 0, 0, tiled=True)  18.8 us
    all_to_all x1, blocking collectives, per_device(): pay = lax.all_to_all(pay, DOM, 0, 0, tiled=True)  12.5 us
    ppermute x1, waiting for transfers between devices, per_device(): above = lax.ppermute(shares, DOM, down)  10.7 us
    all_to_all x1, blocking collectives, per_device(): margins = lax.all_to_all(share, 'z', 0, 0, tiled=True)  9.6 us
    ppermute x1, starting transfers between devices, per_device(): right = lax.ppermute(x, DOM, down)  8.93 us
    pallas_call x1, Pallas kernels, per_device(): pl.pallas_call(functools.partial(local_kernel, planes), out_shape=(jax.Sh...  6.31 us
  transfers between devices with their start and end apart: 6, of which 2 were waited for; matrix products, arithmetic and copies ran while one was open for 0% of the time, Pallas kernels for 8%

profile of v5, /device:TPU:1, one launch (start us, length us, event | category | flops | bytes accessed | tf_op | source)
XLA Modules:
  0.0 155.0 jit_solution(15324223506614918997)
XLA Ops:
  0.6 0.0 copy-start.6
  0.6 0.0 copy-start.4
  0.7 0.0 copy-start.3
  0.7 0.0 copy-start.5
  0.7 3.1 %reshape.22.x_ref.x_hbm = bf16[32,18432]{1,0:T(8,128)(2,1)S(1)} reshape(bf16[32,6,48,64]{3,2,1,0:T(8,128)(2,1)} %param.9) | data formatting | bytes 2359296 | tf_op jit(solution)/shard_map/reshape | solution.py:379
  3.8 0.0 copy-start.1
  3.8 0.0 copy-start.7
  3.8 0.0 copy-start.2
  3.8 8.9 %collective-permute-start.1 = (bf16[32,18432]{1,0:T(8,128)(2,1)S(1)}, bf16[32,18432]{1,0:T(8,128)(2,1)}, u32[]{:S(2)}, u32[]{:S(2)}) collective-permute-start(bf16[32,18432]{1,0:T(8,128)(2,1)S(1)} %reshape.22.x_ref.x_hbm), channel_id=1, source_target_pairs={{1,0},{2,1},{3,2},{4,3},{5,4},{6,5},{7,6},{8,7},{9,8},{10,9},{11,1... | collective-permute-start | bytes 3538952 | tf_op jit(solution)/shard_map/ppermute | solution.py:381
  12.8 0.0 collective-permute-start
  13.4 0.0 copy-done.6
  13.5 0.1 pad_add_fusion.place_ref
  13.6 0.1 fusion.onehot_ref.onehot_hbm
  13.7 0.0 copy-done.4
  13.7 0.0 copy-done.3
  13.7 2.0 %inner.1 = (f32[32,128]{1,0:T(8,128)S(1)}, s32[8]{0:T(128)S(1)}) custom-call(s32[64]{0:T(128)S(1)} %copy-done.4, s32[8]{0:T(128)S(1)} %pad_add_fusion.place_ref, bf16[32,18432]{1,0:T(8,128)(2,1)S(1)} %reshape.22.x_ref.x_hbm, f32[64,128]{1,0:T(8,128)S(1)} %copy-done.3, f32[128,128]{1,0:T(8,128)S(1)} %fusion.onehot_ref.onehot_hbm), custom_call_target="tpu_custom_call" | custom-call | bytes 6000000 | tf_op jit(solution)/shard_map/inner/pallas_call | solution.py:396
  15.7 4.9 %collective-permute-start.3 = (f32[32,128]{1,0:T(8,128)S(1)}, f32[32,128]{1,0:T(8,128)S(1)}, u32[]{:S(2)}, u32[]{:S(2)}) collective-permute-start(f32[32,128]{1,0:T(8,128)S(1)} %get-tuple-element.11.mine_ref), channel_id=1, source_target_pairs={{1,0},{2,1},{3,2},{4,3},{5,4},{6,5},{7,6},{8,7},{9,8},{10,9},{11,1... | collective-permute-start | bytes 49160 | tf_op jit(solution)/shard_map/ppermute | solution.py:410
  20.5 0.0 collective-permute-start.2
  20.5 0.0 copy-done.5
  20.5 0.1 reshape.24.pot_ref
  20.7 0.0 copy-done.7
  20.7 0.1 pad.9.coupling_ref
  20.8 0.0 copy-done.2
  20.8 6.3 %local.1 = (f32[32,18432]{1,0:T(8,128)S(1)}, f32[32,128]{1,0:T(8,128)S(1)}) custom-call(bf16[32,18432]{1,0:T(8,128)(2,1)S(1)} %reshape.22.x_ref.x_hbm, f32[1,18432]{1,0:T(1,128)S(1)} %reshape.24.pot_ref, bf16[3,1024,256]{2,1,0:T(8,128)(2,1)S(1)} %copy-done.2), custom_call_target="tpu_custom_call" | custom-call | bytes 21000000 | tf_op jit(solution)/shard_map/local/pallas_call | solution.py:412
  27.1 0.0 copy-done.1
  27.1 10.7 %collective-permute-done.3.above_hbm = f32[32,128]{1,0:T(8,128)S(1)} collective-permute-done((f32[32,128]{1,0:T(8,128)S(1)}, f32[32,128]{1,0:T(8,128)S(1)}, u32[]{:S(2)}, u32[]{:S(2)}) %collective-permute-start.3) | collective-permute-done | bytes 16416 | tf_op jit(solution)/shard_map/ppermute | solution.py:410
  37.8 5.3 %collective-permute-done.2.below_hbm = f32[32,128]{1,0:T(8,128)S(1)} collective-permute-done((f32[32,128]{1,0:T(8,128)S(1)}, f32[32,128]{1,0:T(8,128)S(1)}, u32[]{:S(2)}, u32[]{:S(2)}) %collective-permute-start.2) | collective-permute-done | bytes 16416 | tf_op jit(solution)/shard_map/ppermute | solution.py:409
  43.1 0.0 collective-permute-done.1.right_hbm
  43.1 0.0 collective-permute-done.left_hbm
  43.1 0.0 copy-start
  43.1 4.2 %hamilton.1 = (f32[32,18432]{1,0:T(8,128)S(1)}, f32[32,9,1,128]{3,2,1,0:T(1,128)S(1)}) custom-call(f32[32,18432]{1,0:T(8,128)S(1)} %get-tuple-element.9.h0_ref, bf16[32,18432]{1,0:T(8,128)(2,1)} %copy-done.1, bf16[32,18432]{1,0:T(8,128)(2,1)} %collective-permute-done.left_hbm, bf16[32,18432]{1,0:T(8,128)(2,1)} %collective-permute-done.1.right_hbm, ...), custom_call_target="tpu_custom_call" | custom-call | bytes 15000000 | tf_op jit(solution)/shard_map/hamilton/pallas_call | solution.py:426
  47.3 12.5 %all_to_all.30.pay_ref = f32[32,9,1,128]{3,2,1,0:T(1,128)S(1)} all-to-all(f32[32,9,1,128]{3,2,1,0:T(1,128)S(1)} %get-tuple-element.13), channel_id=1, replica_groups=mesh['x'=4,'core'=2,'z'=8,'y'=4] {'z','y'}, dimensions={0} | all-to-all | bytes 294912 | tf_op jit(solution)/shard_map/all_to_all | solution.py:441
  59.9 2.9 %residual.1 = bf16[8,32,2304]{2,1,0:T(8,128)(2,1)S(1)} custom-call(s32[64]{0:T(128)S(1)} %copy-done.4, s32[8]{0:T(128)S(1)} %get-tuple-element.8.place_ref, f32[32,18432]{1,0:T(8,128)S(1)} %get-tuple-element.12.h_ref, bf16[32,18432]{1,0:T(8,128)(2,1)} %copy-done.1, f32[32,9,1,128]{3,2,1,0:T(1,128)S(1)} %all_to_all.30.pay_ref, f32[64,128]{1,0:T(8,128)S(1)} %copy-done.3, ...), custom_call_target="tpu_custom_call" | custom-call | bytes 6000000 | tf_op jit(solution)/shard_map/residual/pallas_call | solution.py:443
  62.8 23.7 %all_to_all.31 = bf16[8,32,2304]{2,1,0:T(8,128)(2,1)S(1)} all-to-all(bf16[8,32,2304]{2,1,0:T(8,128)(2,1)S(1)} %residual.1), channel_id=1, replica_groups=mesh['x'=4,'core'=2,'z'=8,'y'=4] {'x','core'}, dimensions={0} | all-to-all | bytes 2359296 | tf_op jit(solution)/shard_map/all_to_all | solution.py:459
  86.4 0.0 copy-done
  86.4 2.4 %margin.3 = f32[4,256,256]{2,1,0:T(8,128)S(1)} custom-call(s32[8]{0:T(128)S(1)} %get-tuple-element.8.place_ref, bf16[6,4,2,256,384]{4,3,2,1,0:T(8,128)(2,1)S(1)} %bitcast.14, bf16[256,2304]{1,0:T(8,128)(2,1)S(1)} %bitcast.18), custom_call_target="tpu_custom_call" | custom-call | bytes 9000000 | tf_op jit(solution)/shard_map/margin/pallas_call | solution.py:465
  88.8 1.0 collective-permute-start.4
  89.8 2.4 %margin.2.kept_ref = f32[4,256,256]{2,1,0:T(8,128)S(1)} custom-call(s32[8]{0:T(128)S(1)} %get-tuple-element.8.place_ref, bf16[6,4,2,256,384]{4,3,2,1,0:T(8,128)(2,1)S(1)} %bitcast.15, bf16[256,2304]{1,0:T(8,128)(2,1)S(1)} %bitcast.19), custom_call_target="tpu_custom_call" | custom-call | bytes 9000000 | tf_op jit(solution)/shard_map/margin/pallas_call | solution.py:465
  92.1 0.0 collective-permute-done.4.given_ref
  92.1 0.1 pair.1
  92.3 18.8 %all_to_all.32.in_ref = f32[16,64,256]{2,1,0:T(8,128)S(1)} all-to-all(f32[16,64,256]{2,1,0:T(8,128)S(1)} %pair.1), channel_id=1, replica_groups=mesh['x'=4,'core'=2,'z'=8,'y'=4] {'x','y'}, dimensions={0} | all-to-all | bytes 2097152 | tf_op jit(solution)/shard_map/all_to_all | solution.py:489
  111.0 0.1 sum.2
  111.1 9.6 %all_to_all.33.in_ref = f32[8,8,256]{2,1,0:T(8,128)S(1)} all-to-all(f32[8,8,256]{2,1,0:T(8,128)S(1)} %bitcast.21), channel_id=1, replica_groups=mesh['x'=4,'core'=2,'z'=8,'y'=4] {'z'}, dimensions={0} | all-to-all | bytes 131072 | tf_op jit(solution)/shard_map/all_to_all | solution.py:491
  120.7 0.6 sum.3
  121.3 0.7 convert_element_type.9
  122.0 9.2 %all_to_all.34 = bf16[8,8,256]{2,1,0:T(8,128)(2,1)S(1)} all-to-all(bf16[8,8,256]{2,1,0:T(8,128)(2,1)S(1)} %broadcast_in_dim.33), channel_id=1, replica_groups=mesh['x'=4,'core'=2,'z'=8,'y'=4] {'z'}, dimensions={0} | all-to-all | bytes 65536 | tf_op jit(solution)/shard_map/all_to_all | solution.py:351
  131.3 12.7 %all_to_all.35.coeff_ref = bf16[16,64,256]{2,1,0:T(8,128)(2,1)S(1)} all-to-all(bf16[16,64,256]{2,1,0:T(8,128)(2,1)S(1)} %broadcast_in_dim.35), channel_id=1, replica_groups=mesh['x'=4,'core'=2,'z'=8,'y'=4] {'x','y'}, dimensions={0} | all-to-all | bytes 1048576 | tf_op jit(solution)/shard_map/all_to_all | solution.py:351
  144.0 5.0 %collective-permute-start.5 = (bf16[16,64,256]{2,1,0:T(8,128)(2,1)S(1)}, bf16[16,64,256]{2,1,0:T(8,128)(2,1)S(1)}, u32[]{:S(2)}, u32[]{:S(2)}) collective-permute-start(bf16[16,64,256]{2,1,0:T(8,128)(2,1)S(1)} %all_to_all.35.coeff_ref), channel_id=1, source_target_pairs={{0,32},{32,0},{1,33},{33,1},{2,34},{34,2},{3,35},{35,3},{4,36},{36... | collective-permute-start | bytes 1572872 | tf_op jit(solution)/shard_map/ppermute | solution.py:496
  149.0 2.5 %clean.2.r_ref = f32[6,256,384]{2,1,0:T(8,128)S(1)} custom-call(s32[8]{0:T(128)S(1)} %get-tuple-element.8.place_ref, bf16[6,4,2,256,384]{4,3,2,1,0:T(8,128)(2,1)S(1)} %bitcast.16, bf16[16,64,256]{2,1,0:T(8,128)(2,1)S(1)} %all_to_all.35.coeff_ref, bf16[256,2304]{1,0:T(8,128)(2,1)S(1)} %bitcast.20), custom_call_target="tpu_custom_call" | custom-call | bytes 9000000 | tf_op jit(solution)/shard_map/clean/pallas_call | solution.py:499
  151.5 0.0 collective-permute-done.5.coeff_ref
  151.5 3.5 %clean.3 = bf16[6,256,384]{2,1,0:T(8,128)(2,1)} custom-call(s32[8]{0:T(128)S(1)} %get-tuple-element.8.place_ref, bf16[6,4,2,256,384]{4,3,2,1,0:T(8,128)(2,1)S(1)} %bitcast.17, bf16[16,64,256]{2,1,0:T(8,128)(2,1)S(1)} %collective-permute-done.5.coeff_ref, f32[6,256,384]{2,1,0:T(8,128)S(1)} %clean.2.r_ref), custom_call_target="tpu_custom_call" | custom-call | bytes 9000000 | tf_op jit(solution)/shard_map/clean/pallas_call | solution.py:499
  (6 shorter events, 0.1 us)
Async XLA Ops:
  0.6 12.8 %copy-start.6 = (s32[64]{0:T(128)S(1)}, s32[64]{0:T(128)}, u32[]{:S(2)}) copy-start(s32[64]{0:T(128)} %param.14) | copy-start | bytes 772
  0.6 13.1 %copy-start.4 = (s32[64]{0:T(128)S(1)}, s32[64]{0:T(128)}, u32[]{:S(2)}) copy-start(s32[64]{0:T(128)} %block_ref.3) | copy-start | bytes 772
  0.7 13.1 %copy-start.3 = (f32[64,128]{1,0:T(8,128)S(1)}, f32[64,128]{1,0:T(8,128)}, u32[]{:S(2)}) copy-start(f32[64,128]{1,0:T(8,128)} %proj_hbm.1) | copy-start | bytes 98308
  0.7 19.9 %copy-start.5 = (f32[6,48,64]{2,1,0:T(8,128)S(1)}, f32[6,48,64]{2,1,0:T(8,128)}, u32[]{:S(2)}) copy-start(f32[6,48,64]{2,1,0:T(8,128)} %param.10) | copy-start | bytes 221188
  3.8 23.3 %copy-start.1 = (bf16[32,18432]{1,0:T(8,128)(2,1)}, bf16[32,18432]{1,0:T(8,128)(2,1)S(1)}, u32[]{:S(2)}) copy-start(bf16[32,18432]{1,0:T(8,128)(2,1)S(1)} %reshape.22.x_ref.x_hbm) | copy-start | bytes 3538948
  3.8 16.9 %copy-start.7 = (f32[32]{0:T(128)S(1)}, f32[32]{0:T(128)}, u32[]{:S(2)}) copy-start(f32[32]{0:T(128)} %param.12) | copy-start | bytes 388
  3.8 16.9 %copy-start.2 = (bf16[3,1024,256]{2,1,0:T(8,128)(2,1)S(1)}, bf16[3,1024,256]{2,1,0:T(8,128)(2,1)}, u32[]{:S(2)}) copy-start(bf16[3,1024,256]{2,1,0:T(8,128)(2,1)} %constant.73.clone.w_ref) | copy-start | bytes 4718596
  3.8 39.2 %collective-permute-start.1 = (bf16[32,18432]{1,0:T(8,128)(2,1)S(1)}, bf16[32,18432]{1,0:T(8,128)(2,1)}, u32[]{:S(2)}, u32[]{:S(2)}) collective-permute-start(bf16[32,18432]{1,0:T(8,128)(2,1)S(1)} %reshape.22.x_ref.x_hbm), channel_id=1, source_target_pairs={{1,0},{2,1},{3,2},{4,3},{5,4},{6,5},{7,6},{8,7},{9,8},{10,9},{11,1... | collective-permute-start | bytes 3538952 | tf_op jit(solution)/shard_map/ppermute | solution.py:381
  12.8 30.3 %collective-permute-start = (bf16[32,18432]{1,0:T(8,128)(2,1)S(1)}, bf16[32,18432]{1,0:T(8,128)(2,1)}, u32[]{:S(2)}, u32[]{:S(2)}) collective-permute-start(bf16[32,18432]{1,0:T(8,128)(2,1)S(1)} %reshape.22.x_ref.x_hbm), channel_id=1, source_target_pairs={{0,1},{1,2},{2,3},{3,4},{4,5},{5,6},{6,7},{7,8},{8,9},{9,10},{10,1... | collective-permute-start | bytes 3538952 | tf_op jit(solution)/shard_map/ppermute | solution.py:380
  15.7 22.1 %collective-permute-start.3 = (f32[32,128]{1,0:T(8,128)S(1)}, f32[32,128]{1,0:T(8,128)S(1)}, u32[]{:S(2)}, u32[]{:S(2)}) collective-permute-start(f32[32,128]{1,0:T(8,128)S(1)} %get-tuple-element.11.mine_ref), channel_id=1, source_target_pairs={{1,0},{2,1},{3,2},{4,3},{5,4},{6,5},{7,6},{8,7},{9,8},{10,9},{11,1... | collective-permute-start | bytes 49160 | tf_op jit(solution)/shard_map/ppermute | solution.py:410
  20.5 22.5 %collective-permute-start.2 = (f32[32,128]{1,0:T(8,128)S(1)}, f32[32,128]{1,0:T(8,128)S(1)}, u32[]{:S(2)}, u32[]{:S(2)}) collective-permute-start(f32[32,128]{1,0:T(8,128)S(1)} %get-tuple-element.11.mine_ref), channel_id=1, source_target_pairs={{0,1},{1,2},{2,3},{3,4},{4,5},{5,6},{6,7},{7,8},{8,9},{9,10},{10,1... | collective-permute-start | bytes 49160 | tf_op jit(solution)/shard_map/ppermute | solution.py:409
  43.1 43.4 %copy-start = (bf16[2048,6,384]{2,0,1:T(8,128)(2,1)S(1)}, bf16[2048,6,384]{2,0,1:T(8,128)(2,1)}, u32[]{:S(2)}) copy-start(bf16[2048,6,384]{2,0,1:T(8,128)(2,1)} %param.16) | copy-start | bytes 28311556
  88.8 3.3 %collective-permute-start.4 = (f32[4,256,256]{2,1,0:T(8,128)S(1)}, f32[4,256,256]{2,1,0:T(8,128)S(1)}, u32[]{:S(2)}, u32[]{:S(2)}) collective-permute-start(f32[4,256,256]{2,1,0:T(8,128)S(1)} %margin.3), channel_id=1, source_target_pairs={{0,32},{32,0},{1,33},{33,1},{2,34},{34,2},{3,35},{35,3},{4,36},{36... | collective-permute-start | bytes 3145736 | tf_op jit(solution)/shard_map/ppermute | solution.py:486
  144.0 7.5 %collective-permute-start.5 = (bf16[16,64,256]{2,1,0:T(8,128)(2,1)S(1)}, bf16[16,64,256]{2,1,0:T(8,128)(2,1)S(1)}, u32[]{:S(2)}, u32[]{:S(2)}) collective-permute-start(bf16[16,64,256]{2,1,0:T(8,128)(2,1)S(1)} %all_to_all.35.coeff_ref), channel_id=1, source_target_pairs={{0,32},{32,0},{1,33},{33,1},{2,34},{34,2},{3,35},{35,3},{4,36},{36... | collective-permute-start | bytes 1572872 | tf_op jit(solution)/shard_map/ppermute | solution.py:496

commit v6 on v5

--- a/solution.py
+++ b/solution.py
@@ -306,18 +306,28 @@
     n_x, share_rows, _ = kept_ref.shape
     n_y = out_ref.shape[0] // n_x
     for i in range(n_x):
-        for at in range(0, share_rows, 8):
-            z, y = divmod(at // 8, n_y)
-            out_ref[i * n_y + y, z * 8 : z * 8 + 8] = (
+        for y in range(n_y):
+            pieces = [
                 kept_ref[i, at : at + 8] + given_ref[i, at : at + 8]
-            )
-
-
-def sum_kernel(in_ref, out_ref):
-    acc = in_ref[0]
+                for at in range(y * 8, share_rows, n_y * 8)
+            ]
+            out_ref[i * n_y + y] = jnp.concatenate(pieces, axis=0).astype(BF16)
+
+
+def sum_kernel(in_ref, out_ref, *copies):
+    acc = in_ref[0].astype(F32)
     for i in range(1, in_ref.shape[0]):
-        acc += in_ref[i]
+        acc += in_ref[i].astype(F32)
     out_ref[...] = acc
+    for ref in copies:
+        for i in range(ref.shape[0]):
+            ref[i] = acc
+
+
+def copies_kernel(in_ref, out_ref):
+    value = in_ref[...].astype(BF16)
+    for i in range(out_ref.shape[0]):
+        out_ref[i] = value
 
 
 def clean_kernel(side, place_ref, locked_ref, coeff_ref, r_ref, out_ref, turned_ref):
@@ -344,13 +354,6 @@
 def ring(size):
     up = [(i, (i + 1) % size) for i in range(size)]
     return up, [(j, i) for i, j in up]
-
-
-def spread(value, axis):
-    size = lax.axis_size(axis)
-    return lax.all_to_all(
-        jnp.broadcast_to(value[None], (size,) + value.shape), axis, 0, 0, tiled=True
-    )
 
 
 def per_device(
@@ -472,27 +475,32 @@
             name="margin",
         )(place, by_plane, residual)
 
-    def small_call(kernel, shape, name, *operands):
+    def small_call(kernel, shapes, name, *operands):
         return pl.pallas_call(
             kernel,
-            out_shape=jax.ShapeDtypeStruct(shape, F32),
+            out_shape=shapes,
             in_specs=[VMEM] * len(operands),
-            out_specs=VMEM,
+            out_specs=jax.tree.map(lambda _: VMEM, shapes),
             compiler_params=params(8),
             cost_estimate=cost(1),
             name=name,
         )(*operands)
 
+    short = jax.ShapeDtypeStruct((n_x * n_y, n_z * 8, bands), BF16)
+    whole = jax.ShapeDtypeStruct((n_z * 8, bands), F32)
+    eighth = jax.ShapeDtypeStruct((8, bands), F32)
     given = lax.ppermute(margin_call(1), "core", swap)
     kept = margin_call(0)
-    share = small_call(pair_kernel, (n_x * n_y, n_z * 8, bands), "pair", kept, given)
+    share = small_call(pair_kernel, short, "pair", kept, given)
     share = lax.all_to_all(share, SHORT, 0, 0, tiled=True)
-    share = small_call(sum_kernel, (n_z * 8, bands), "sum", share).reshape(n_z, 8, bands)
-    margins = lax.all_to_all(share, "z", 0, 0, tiled=True)
-    margins = small_call(sum_kernel, (8, bands), "sum", margins)
-
-    coeffs = spread(margins.astype(BF16), "z").reshape(n_z * 8, bands)
-    coeffs = spread(coeffs, SHORT).reshape(n_x * n_y, n_z * 8, bands)
+    share = small_call(sum_kernel, whole, "sum", share).reshape(n_z, 8, bands)
+    share = lax.all_to_all(share, "z", 0, 0, tiled=True)
+    spread_out = jax.ShapeDtypeStruct((n_z, 8, bands), F32)
+    margins, coeffs = small_call(sum_kernel, (eighth, spread_out), "sum", share)
+
+    coeffs = lax.all_to_all(coeffs, "z", 0, 0, tiled=True).reshape(n_z * 8, bands)
+    coeffs = small_call(copies_kernel, short, "copies", coeffs)
+    coeffs = lax.all_to_all(coeffs, SHORT, 0, 0, tiled=True)
     other = lax.ppermute(coeffs, "core", swap)
 
     def clean_call(side, coeffs, before, kind):

time: 155 us -> 149 us (0.961)
  blocking collectives: 86.5 us -> 81.2 us
    all_to_all x1, blocking collectives: 18.8 us -> 13.2 us  [per_device(): share = lax.all_to_all(share, SHORT, 0, 0, tiled=True)]
  transfers between devices with their start and end apart: 6 -> 6, of which waited for: 2 -> 2; matrix products, arithmetic and copies ran while one was open for 0% -> 0% of each run, Pallas kernels for 8% -> 9%
where the time goes in v6:
time: 149 us
  blocking collectives  81.2 us (54%)
  Pallas kernels  26.9 us (18%)
  starting transfers between devices  19.8 us (13%)
  waiting for transfers between devices  16 us (11%)
  local copies, waits for them, and re-layouts  3.39 us (2%)
  between operations  1.53 us (1%)
    all_to_all x1, blocking collectives, per_device(): lax.all_to_all(residual, BAND, 0, 0, tiled=True).reshape(bands, width)  23.7 us
    all_to_all x1, blocking collectives, per_device(): share = lax.all_to_all(share, SHORT, 0, 0, tiled=True)  13.2 us
    all_to_all x1, blocking collectives, per_device(): coeffs = lax.all_to_all(coeffs, SHORT, 0, 0, tiled=True)  12.7 us
    all_to_all x1, blocking collectives, per_device(): pay = lax.all_to_all(pay, DOM, 0, 0, tiled=True)  12.5 us
    ppermute x1, waiting for transfers between devices, per_device(): above = lax.ppermute(shares, DOM, down)  10.7 us
    all_to_all x1, blocking collectives, per_device(): share = lax.all_to_all(share, 'z', 0, 0, tiled=True)  9.6 us
    all_to_all x1, blocking collectives, per_device(): lax.all_to_all(coeffs, 'z', 0, 0, tiled=True).reshape(n_z * 8, bands)  9.59 us
    ppermute x1, starting transfers between devices, per_device(): right = lax.ppermute(x, DOM, down)  8.93 us
  transfers between devices with their start and end apart: 6, of which 2 were waited for; matrix products, arithmetic and copies ran while one was open for 0% of the time, Pallas kernels for 9%

profile of v6, /device:TPU:1, one launch (start us, length us, event | category | flops | bytes accessed | tf_op | source)
XLA Modules:
  0.0 149.0 jit_solution(223760458908885116)
XLA Ops:
  0.6 0.0 copy-start.6
  0.6 0.0 copy-start.4
  0.7 0.0 copy-start.3
  0.7 0.0 copy-start.5
  0.7 3.1 %reshape.23.x_ref.x_hbm = bf16[32,18432]{1,0:T(8,128)(2,1)S(1)} reshape(bf16[32,6,48,64]{3,2,1,0:T(8,128)(2,1)} %param.9) | data formatting | bytes 2359296 | tf_op jit(solution)/shard_map/reshape | solution.py:382
  3.8 0.0 copy-start.1
  3.8 0.0 copy-start.7
  3.8 0.0 copy-start.2
  3.8 8.9 %collective-permute-start.1 = (bf16[32,18432]{1,0:T(8,128)(2,1)S(1)}, bf16[32,18432]{1,0:T(8,128)(2,1)}, u32[]{:S(2)}, u32[]{:S(2)}) collective-permute-start(bf16[32,18432]{1,0:T(8,128)(2,1)S(1)} %reshape.23.x_ref.x_hbm), channel_id=1, source_target_pairs={{1,0},{2,1},{3,2},{4,3},{5,4},{6,5},{7,6},{8,7},{9,8},{10,9},{11,1... | collective-permute-start | bytes 3538952 | tf_op jit(solution)/shard_map/ppermute | solution.py:384
  12.8 0.0 collective-permute-start
  13.4 0.0 copy-done.6
  13.5 0.1 pad_add_fusion.place_ref
  13.6 0.1 fusion.onehot_ref.onehot_hbm
  13.7 0.0 copy-done.4
  13.7 0.0 copy-done.3
  13.7 2.0 %inner.1 = (f32[32,128]{1,0:T(8,128)S(1)}, s32[8]{0:T(128)S(1)}) custom-call(s32[64]{0:T(128)S(1)} %copy-done.4, s32[8]{0:T(128)S(1)} %pad_add_fusion.place_ref, bf16[32,18432]{1,0:T(8,128)(2,1)S(1)} %reshape.23.x_ref.x_hbm, f32[64,128]{1,0:T(8,128)S(1)} %copy-done.3, f32[128,128]{1,0:T(8,128)S(1)} %fusion.onehot_ref.onehot_hbm), custom_call_target="tpu_custom_call" | custom-call | bytes 6000000 | tf_op jit(solution)/shard_map/inner/pallas_call | solution.py:399
  15.7 4.9 %collective-permute-start.3 = (f32[32,128]{1,0:T(8,128)S(1)}, f32[32,128]{1,0:T(8,128)S(1)}, u32[]{:S(2)}, u32[]{:S(2)}) collective-permute-start(f32[32,128]{1,0:T(8,128)S(1)} %get-tuple-element.13.mine_ref), channel_id=1, source_target_pairs={{1,0},{2,1},{3,2},{4,3},{5,4},{6,5},{7,6},{8,7},{9,8},{10,9},{11,1... | collective-permute-start | bytes 49160 | tf_op jit(solution)/shard_map/ppermute | solution.py:413
  20.5 0.0 collective-permute-start.2
  20.5 0.0 copy-done.5
  20.5 0.1 reshape.25.pot_ref
  20.7 0.0 copy-done.7
  20.7 0.1 pad.9.coupling_ref
  20.8 0.0 copy-done.2
  20.8 6.3 %local.1 = (f32[32,18432]{1,0:T(8,128)S(1)}, f32[32,128]{1,0:T(8,128)S(1)}) custom-call(bf16[32,18432]{1,0:T(8,128)(2,1)S(1)} %reshape.23.x_ref.x_hbm, f32[1,18432]{1,0:T(1,128)S(1)} %reshape.25.pot_ref, bf16[3,1024,256]{2,1,0:T(8,128)(2,1)S(1)} %copy-done.2), custom_call_target="tpu_custom_call" | custom-call | bytes 21000000 | tf_op jit(solution)/shard_map/local/pallas_call | solution.py:415
  27.1 0.0 copy-done.1
  27.1 10.7 %collective-permute-done.3.above_hbm = f32[32,128]{1,0:T(8,128)S(1)} collective-permute-done((f32[32,128]{1,0:T(8,128)S(1)}, f32[32,128]{1,0:T(8,128)S(1)}, u32[]{:S(2)}, u32[]{:S(2)}) %collective-permute-start.3) | collective-permute-done | bytes 16416 | tf_op jit(solution)/shard_map/ppermute | solution.py:413
  37.8 5.3 %collective-permute-done.2.below_hbm = f32[32,128]{1,0:T(8,128)S(1)} collective-permute-done((f32[32,128]{1,0:T(8,128)S(1)}, f32[32,128]{1,0:T(8,128)S(1)}, u32[]{:S(2)}, u32[]{:S(2)}) %collective-permute-start.2) | collective-permute-done | bytes 16416 | tf_op jit(solution)/shard_map/ppermute | solution.py:412
  43.1 0.0 collective-permute-done.1.right_hbm
  43.1 0.0 collective-permute-done.left_hbm
  43.1 0.0 copy-start
  43.1 4.2 %hamilton.1 = (f32[32,18432]{1,0:T(8,128)S(1)}, f32[32,9,1,128]{3,2,1,0:T(1,128)S(1)}) custom-call(f32[32,18432]{1,0:T(8,128)S(1)} %get-tuple-element.11.h0_ref, bf16[32,18432]{1,0:T(8,128)(2,1)} %copy-done.1, bf16[32,18432]{1,0:T(8,128)(2,1)} %collective-permute-done.left_hbm, bf16[32,18432]{1,0:T(8,128)(2,1)} %collective-permute-done.1.right_hbm, ...), custom_call_target="tpu_custom_call" | custom-call | bytes 15000000 | tf_op jit(solution)/shard_map/hamilton/pallas_call | solution.py:429
  47.3 12.5 %all_to_all.30.pay_ref = f32[32,9,1,128]{3,2,1,0:T(1,128)S(1)} all-to-all(f32[32,9,1,128]{3,2,1,0:T(1,128)S(1)} %get-tuple-element.15), channel_id=1, replica_groups=mesh['x'=4,'core'=2,'z'=8,'y'=4] {'z','y'}, dimensions={0} | all-to-all | bytes 294912 | tf_op jit(solution)/shard_map/all_to_all | solution.py:444
  59.9 2.9 %residual.1 = bf16[8,32,2304]{2,1,0:T(8,128)(2,1)S(1)} custom-call(s32[64]{0:T(128)S(1)} %copy-done.4, s32[8]{0:T(128)S(1)} %get-tuple-element.10.place_ref, f32[32,18432]{1,0:T(8,128)S(1)} %get-tuple-element.14.h_ref, bf16[32,18432]{1,0:T(8,128)(2,1)} %copy-done.1, f32[32,9,1,128]{3,2,1,0:T(1,128)S(1)} %all_to_all.30.pay_ref, f32[64,128]{1,0:T(8,128)S(1)} %copy-done.3, ...), custom_call_target="tpu_custom_call" | custom-call | bytes 6000000 | tf_op jit(solution)/shard_map/residual/pallas_call | solution.py:446
  62.8 23.7 %all_to_all.31 = bf16[8,32,2304]{2,1,0:T(8,128)(2,1)S(1)} all-to-all(bf16[8,32,2304]{2,1,0:T(8,128)(2,1)S(1)} %residual.1), channel_id=1, replica_groups=mesh['x'=4,'core'=2,'z'=8,'y'=4] {'x','core'}, dimensions={0} | all-to-all | bytes 2359296 | tf_op jit(solution)/shard_map/all_to_all | solution.py:462
  86.4 0.0 copy-done
  86.4 2.3 %margin.3 = f32[4,256,256]{2,1,0:T(8,128)S(1)} custom-call(s32[8]{0:T(128)S(1)} %get-tuple-element.10.place_ref, bf16[6,4,2,256,384]{4,3,2,1,0:T(8,128)(2,1)S(1)} %bitcast.14, bf16[256,2304]{1,0:T(8,128)(2,1)S(1)} %bitcast.18), custom_call_target="tpu_custom_call" | custom-call | bytes 9000000 | tf_op jit(solution)/shard_map/margin/pallas_call | solution.py:468
  88.8 1.0 collective-permute-start.4
  89.7 2.3 %margin.2.kept_ref = f32[4,256,256]{2,1,0:T(8,128)S(1)} custom-call(s32[8]{0:T(128)S(1)} %get-tuple-element.10.place_ref, bf16[6,4,2,256,384]{4,3,2,1,0:T(8,128)(2,1)S(1)} %bitcast.15, bf16[256,2304]{1,0:T(8,128)(2,1)S(1)} %bitcast.19), custom_call_target="tpu_custom_call" | custom-call | bytes 9000000 | tf_op jit(solution)/shard_map/margin/pallas_call | solution.py:468
  92.1 0.0 collective-permute-done.4.given_ref
  92.1 0.1 pair.1
  92.2 13.2 %all_to_all.32.in_ref = bf16[16,64,256]{2,1,0:T(8,128)(2,1)S(1)} all-to-all(bf16[16,64,256]{2,1,0:T(8,128)(2,1)S(1)} %pair.1), channel_id=1, replica_groups=mesh['x'=4,'core'=2,'z'=8,'y'=4] {'x','y'}, dimensions={0} | all-to-all | bytes 1048576 | tf_op jit(solution)/shard_map/all_to_all | solution.py:495
  105.4 0.1 sum.2
  105.5 9.6 %all_to_all.33.in_ref = f32[8,8,256]{2,1,0:T(8,128)S(1)} all-to-all(f32[8,8,256]{2,1,0:T(8,128)S(1)} %bitcast.21), channel_id=1, replica_groups=mesh['x'=4,'core'=2,'z'=8,'y'=4] {'z'}, dimensions={0} | all-to-all | bytes 131072 | tf_op jit(solution)/shard_map/all_to_all | solution.py:497
  115.1 0.6 sum.3
  115.7 9.6 %all_to_all.34 = f32[8,8,256]{2,1,0:T(8,128)S(1)} all-to-all(f32[8,8,256]{2,1,0:T(8,128)S(1)} %get-tuple-element.16), channel_id=1, replica_groups=mesh['x'=4,'core'=2,'z'=8,'y'=4] {'z'}, dimensions={0} | all-to-all | bytes 131072 | tf_op jit(solution)/shard_map/all_to_all | solution.py:501
  125.3 12.7 %all_to_all.35.coeff_ref = bf16[16,64,256]{2,1,0:T(8,128)(2,1)S(1)} all-to-all(bf16[16,64,256]{2,1,0:T(8,128)(2,1)S(1)} %copies.1), channel_id=1, replica_groups=mesh['x'=4,'core'=2,'z'=8,'y'=4] {'x','y'}, dimensions={0} | all-to-all | bytes 1048576 | tf_op jit(solution)/shard_map/all_to_all | solution.py:503
  138.0 5.1 %collective-permute-start.5 = (bf16[16,64,256]{2,1,0:T(8,128)(2,1)S(1)}, bf16[16,64,256]{2,1,0:T(8,128)(2,1)S(1)}, u32[]{:S(2)}, u32[]{:S(2)}) collective-permute-start(bf16[16,64,256]{2,1,0:T(8,128)(2,1)S(1)} %all_to_all.35.coeff_ref), channel_id=1, source_target_pairs={{0,32},{32,0},{1,33},{33,1},{2,34},{34,2},{3,35},{35,3},{4,36},{36... | collective-permute-start | bytes 1572872 | tf_op jit(solution)/shard_map/ppermute | solution.py:504
  143.0 2.4 %clean.2.r_ref = f32[6,256,384]{2,1,0:T(8,128)S(1)} custom-call(s32[8]{0:T(128)S(1)} %get-tuple-element.10.place_ref, bf16[6,4,2,256,384]{4,3,2,1,0:T(8,128)(2,1)S(1)} %bitcast.16, bf16[16,64,256]{2,1,0:T(8,128)(2,1)S(1)} %all_to_all.35.coeff_ref, bf16[256,2304]{1,0:T(8,128)(2,1)S(1)} %bitcast.20), custom_call_target="tpu_custom_call" | custom-call | bytes 9000000 | tf_op jit(solution)/shard_map/clean/pallas_call | solution.py:507
  145.5 0.0 collective-permute-done.5.coeff_ref
  145.5 3.5 %clean.3 = bf16[6,256,384]{2,1,0:T(8,128)(2,1)} custom-call(s32[8]{0:T(128)S(1)} %get-tuple-element.10.place_ref, bf16[6,4,2,256,384]{4,3,2,1,0:T(8,128)(2,1)S(1)} %bitcast.17, bf16[16,64,256]{2,1,0:T(8,128)(2,1)S(1)} %collective-permute-done.5.coeff_ref, f32[6,256,384]{2,1,0:T(8,128)S(1)} %clean.2.r_ref), custom_call_target="tpu_custom_call" | custom-call | bytes 9000000 | tf_op jit(solution)/shard_map/clean/pallas_call | solution.py:507
  (5 shorter events, 0.1 us)
Async XLA Ops:
  0.6 12.8 %copy-start.6 = (s32[64]{0:T(128)S(1)}, s32[64]{0:T(128)}, u32[]{:S(2)}) copy-start(s32[64]{0:T(128)} %param.14) | copy-start | bytes 772
  0.6 13.1 %copy-start.4 = (s32[64]{0:T(128)S(1)}, s32[64]{0:T(128)}, u32[]{:S(2)}) copy-start(s32[64]{0:T(128)} %block_ref.3) | copy-start | bytes 772
  0.7 13.1 %copy-start.3 = (f32[64,128]{1,0:T(8,128)S(1)}, f32[64,128]{1,0:T(8,128)}, u32[]{:S(2)}) copy-start(f32[64,128]{1,0:T(8,128)} %proj_hbm.1) | copy-start | bytes 98308
  0.7 19.9 %copy-start.5 = (f32[6,48,64]{2,1,0:T(8,128)S(1)}, f32[6,48,64]{2,1,0:T(8,128)}, u32[]{:S(2)}) copy-start(f32[6,48,64]{2,1,0:T(8,128)} %param.10) | copy-start | bytes 221188
  3.8 23.3 %copy-start.1 = (bf16[32,18432]{1,0:T(8,128)(2,1)}, bf16[32,18432]{1,0:T(8,128)(2,1)S(1)}, u32[]{:S(2)}) copy-start(bf16[32,18432]{1,0:T(8,128)(2,1)S(1)} %reshape.23.x_ref.x_hbm) | copy-start | bytes 3538948
  3.8 16.9 %copy-start.7 = (f32[32]{0:T(128)S(1)}, f32[32]{0:T(128)}, u32[]{:S(2)}) copy-start(f32[32]{0:T(128)} %param.12) | copy-start | bytes 388
  3.8 16.9 %copy-start.2 = (bf16[3,1024,256]{2,1,0:T(8,128)(2,1)S(1)}, bf16[3,1024,256]{2,1,0:T(8,128)(2,1)}, u32[]{:S(2)}) copy-start(bf16[3,1024,256]{2,1,0:T(8,128)(2,1)} %constant.73.clone.w_ref) | copy-start | bytes 4718596
  3.8 39.2 %collective-permute-start.1 = (bf16[32,18432]{1,0:T(8,128)(2,1)S(1)}, bf16[32,18432]{1,0:T(8,128)(2,1)}, u32[]{:S(2)}, u32[]{:S(2)}) collective-permute-start(bf16[32,18432]{1,0:T(8,128)(2,1)S(1)} %reshape.23.x_ref.x_hbm), channel_id=1, source_target_pairs={{1,0},{2,1},{3,2},{4,3},{5,4},{6,5},{7,6},{8,7},{9,8},{10,9},{11,1... | collective-permute-start | bytes 3538952 | tf_op jit(solution)/shard_map/ppermute | solution.py:384
  12.8 30.3 %collective-permute-start = (bf16[32,18432]{1,0:T(8,128)(2,1)S(1)}, bf16[32,18432]{1,0:T(8,128)(2,1)}, u32[]{:S(2)}, u32[]{:S(2)}) collective-permute-start(bf16[32,18432]{1,0:T(8,128)(2,1)S(1)} %reshape.23.x_ref.x_hbm), channel_id=1, source_target_pairs={{0,1},{1,2},{2,3},{3,4},{4,5},{5,6},{6,7},{7,8},{8,9},{9,10},{10,1... | collective-permute-start | bytes 3538952 | tf_op jit(solution)/shard_map/ppermute | solution.py:383
  15.7 22.1 %collective-permute-start.3 = (f32[32,128]{1,0:T(8,128)S(1)}, f32[32,128]{1,0:T(8,128)S(1)}, u32[]{:S(2)}, u32[]{:S(2)}) collective-permute-start(f32[32,128]{1,0:T(8,128)S(1)} %get-tuple-element.13.mine_ref), channel_id=1, source_target_pairs={{1,0},{2,1},{3,2},{4,3},{5,4},{6,5},{7,6},{8,7},{9,8},{10,9},{11,1... | collective-permute-start | bytes 49160 | tf_op jit(solution)/shard_map/ppermute | solution.py:413
  20.5 22.5 %collective-permute-start.2 = (f32[32,128]{1,0:T(8,128)S(1)}, f32[32,128]{1,0:T(8,128)S(1)}, u32[]{:S(2)}, u32[]{:S(2)}) collective-permute-start(f32[32,128]{1,0:T(8,128)S(1)} %get-tuple-element.13.mine_ref), channel_id=1, source_target_pairs={{0,1},{1,2},{2,3},{3,4},{4,5},{5,6},{6,7},{7,8},{8,9},{9,10},{10,1... | collective-permute-start | bytes 49160 | tf_op jit(solution)/shard_map/ppermute | solution.py:412
  43.1 43.4 %copy-start = (bf16[2048,6,384]{2,0,1:T(8,128)(2,1)S(1)}, bf16[2048,6,384]{2,0,1:T(8,128)(2,1)}, u32[]{:S(2)}) copy-start(bf16[2048,6,384]{2,0,1:T(8,128)(2,1)} %param.16) | copy-start | bytes 28311556
  88.8 3.3 %collective-permute-start.4 = (f32[4,256,256]{2,1,0:T(8,128)S(1)}, f32[4,256,256]{2,1,0:T(8,128)S(1)}, u32[]{:S(2)}, u32[]{:S(2)}) collective-permute-start(f32[4,256,256]{2,1,0:T(8,128)S(1)} %margin.3), channel_id=1, source_target_pairs={{0,32},{32,0},{1,33},{33,1},{2,34},{34,2},{3,35},{35,3},{4,36},{36... | collective-permute-start | bytes 3145736 | tf_op jit(solution)/shard_map/ppermute | solution.py:492
  138.0 7.5 %collective-permute-start.5 = (bf16[16,64,256]{2,1,0:T(8,128)(2,1)S(1)}, bf16[16,64,256]{2,1,0:T(8,128)(2,1)S(1)}, u32[]{:S(2)}, u32[]{:S(2)}) collective-permute-start(bf16[16,64,256]{2,1,0:T(8,128)(2,1)S(1)} %all_to_all.35.coeff_ref), channel_id=1, source_target_pairs={{0,32},{32,0},{1,33},{33,1},{2,34},{34,2},{3,35},{35,3},{4,36},{36... | collective-permute-start | bytes 1572872 | tf_op jit(solution)/shard_map/ppermute | solution.py:504

commit v7 on v6

--- a/solution.py
+++ b/solution.py
@@ -113,7 +113,7 @@
 def hamilton_kernel(
     planes,
     h0_ref,
-    x_hbm,
+    x_ref,
     left_hbm,
     right_hbm,
     den_ref,
@@ -123,7 +123,6 @@
     above_hbm,
     h_ref,
     pay_ref,
-    x_ref,
     left_ref,
     right_ref,
     below_ref,
@@ -140,7 +139,7 @@
         for p in range(planes):
             where = slice(p * plane + k * chunk, p * plane + (k + 1) * chunk)
             for i, (src, dst) in enumerate(
-                ((x_hbm, x_ref), (left_hbm, left_ref), (right_hbm, right_ref))
+                ((left_hbm, left_ref), (right_hbm, right_ref))
             ):
                 copies.append(
                     pltpu.make_async_copy(src.at[:, where], dst.at[:, where], sems.at[k, p, i])
@@ -180,7 +179,7 @@
     num = (zero,) * (rows // 16)
     steps = chunk // BS
     for k in range(chunks):
-        for copy in copies[k * planes * 3 : (k + 1) * planes * 3]:
+        for copy in copies[k * planes * 2 : (k + 1) * planes * 2]:
             copy.wait()
         num = lax.fori_loop(k * steps, (k + 1) * steps, halo, num)
     num = jnp.concatenate(num, axis=0)
@@ -214,30 +213,23 @@
     block_ref,
     place_ref,
     h_ref,
-    x_hbm,
+    x_ref,
     pay_ref,
     proj_hbm,
     onehot_hbm,
     r_ref,
     full_ref,
-    x_ref,
     proj_ref,
     onehot_ref,
     sems,
 ):
     rows, cells = x_ref.shape
     plane = cells // planes
-    copies = []
-    for p in range(planes):
-        where = slice(p * plane, (p + 1) * plane)
-        copies.append(
-            pltpu.make_async_copy(x_hbm.at[:, where], x_ref.at[:, where], sems.at[2 + p])
-        )
     late = [
         pltpu.make_async_copy(proj_hbm, proj_ref, sems.at[0]),
         pltpu.make_async_copy(onehot_hbm, onehot_ref, sems.at[1]),
     ]
-    for copy in copies + late:
+    for copy in late:
         copy.start()
     slots = proj_ref.shape[0]
     n = BS // 4
@@ -249,8 +241,6 @@
     den = jnp.sum(jnp.where(lane == row + rows, sums, 0.0), axis=1, keepdims=True)
     energy = jnp.broadcast_to(num / den, (rows, BS))
     for at in range(0, cells, BS):
-        if at % plane == 0:
-            copies[at // plane].wait()
         where = slice(at, at + BS)
         full_ref[:, where] = h_ref[:, where] - energy * x_ref[:, where].astype(F32)
 
@@ -314,20 +304,24 @@
             out_ref[i * n_y + y] = jnp.concatenate(pieces, axis=0).astype(BF16)
 
 
-def sum_kernel(in_ref, out_ref, *copies):
+def partial_kernel(in_ref, out_ref):
     acc = in_ref[0].astype(F32)
     for i in range(1, in_ref.shape[0]):
         acc += in_ref[i].astype(F32)
-    out_ref[...] = acc
-    for ref in copies:
-        for i in range(ref.shape[0]):
-            ref[i] = acc
-
-
-def copies_kernel(in_ref, out_ref):
-    value = in_ref[...].astype(BF16)
+    value = acc.astype(BF16)
     for i in range(out_ref.shape[0]):
         out_ref[i] = value
+
+
+def total_kernel(place_ref, in_ref, margin_ref, coeff_ref, total_ref):
+    acc = in_ref[0].astype(F32)
+    for i in range(1, in_ref.shape[0]):
+        acc += in_ref[i].astype(F32)
+    total_ref[...] = acc
+    value = acc.astype(BF16)
+    for i in range(coeff_ref.shape[0]):
+        coeff_ref[i] = value
+    margin_ref[...] = total_ref[pl.ds(pl.multiple_of(place_ref[5] * 8, 8), 8)]
 
 
 def clean_kernel(side, place_ref, locked_ref, coeff_ref, r_ref, out_ref, turned_ref):
@@ -395,7 +389,7 @@
     coupling_row = jnp.pad(coupling[None], ((0, 0), (n, BS - 2 * n)))
 
     near = (here + domains + jnp.arange(-1, 2, dtype=jnp.int32)) % domains
-    place = jnp.concatenate([near, jnp.stack([core, 1 - core]), jnp.zeros(3, jnp.int32)])
+    place = jnp.concatenate([near, jnp.stack([core, 1 - core, lax.axis_index("z"), 0, 0])])
     shares, place = pl.pallas_call(
         inner_kernel,
         out_shape=(
@@ -408,7 +402,6 @@
         cost_estimate=cost(2),
         name="inner",
     )(slot_block, place.astype(jnp.int32), x, projectors, onehot)
-    x_hbm = pltpu.with_memory_space_constraint(x, pltpu.HBM)
     below = lax.ppermute(shares, DOM, up)
     above = lax.ppermute(shares, DOM, down)
 
@@ -432,33 +425,32 @@
             jax.ShapeDtypeStruct((rows, cells), F32),
             jax.ShapeDtypeStruct((domains, rows // 4 + 1, 1, BS), F32),
         ),
-        in_specs=[VMEM] + [ANY] * 3 + [VMEM] * 3 + [ANY] * 2,
+        in_specs=[VMEM] * 2 + [ANY] * 2 + [VMEM] * 3 + [ANY] * 2,
         out_specs=(VMEM, VMEM),
-        scratch_shapes=[pltpu.VMEM((rows, cells), BF16)] * 3
+        scratch_shapes=[pltpu.VMEM((rows, cells), BF16)] * 2
         + [pltpu.VMEM((rows, BS), F32)] * 2
-        + [pltpu.SemaphoreType.DMA((3, planes, 3)), pltpu.SemaphoreType.DMA((2,))],
+        + [pltpu.SemaphoreType.DMA((3, planes, 2)), pltpu.SemaphoreType.DMA((2,))],
         compiler_params=params(24),
         cost_estimate=cost(5),
         name="hamilton",
-    )(h0, x_hbm, left, right, den, shares, coupling_row, below, above)
+    )(h0, x, left, right, den, shares, coupling_row, below, above)
     pay = lax.all_to_all(pay, DOM, 0, 0, tiled=True)
 
     residual = pl.pallas_call(
         functools.partial(residual_kernel, planes),
         out_shape=jax.ShapeDtypeStruct((groups, rows, width), BF16),
-        in_specs=[SMEM, SMEM, VMEM, ANY, VMEM, ANY, ANY],
+        in_specs=[SMEM, SMEM, VMEM, VMEM, VMEM, ANY, ANY],
         out_specs=VMEM,
         scratch_shapes=[
             pltpu.VMEM((rows, cells), F32),
-            pltpu.VMEM((rows, cells), BF16),
             pltpu.VMEM((slots, BS), F32),
             pltpu.VMEM((BS, BS), F32),
-            pltpu.SemaphoreType.DMA((2 + planes,)),
+            pltpu.SemaphoreType.DMA((2,)),
         ],
         compiler_params=params(24),
         cost_estimate=cost(2),
         name="residual",
-    )(slot_block, place, hamilton, x_hbm, pay, projectors, onehot)
+    )(slot_block, place, hamilton, x, pay, projectors, onehot)
     residual = lax.all_to_all(residual, BAND, 0, 0, tiled=True).reshape(bands, width)
 
     by_plane = locked.transpose(1, 0, 2).reshape(planes, n_x, 2, share_rows, part)
@@ -475,31 +467,39 @@
             name="margin",
         )(place, by_plane, residual)
 
-    def small_call(kernel, shapes, name, *operands):
-        return pl.pallas_call(
-            kernel,
-            out_shape=shapes,
-            in_specs=[VMEM] * len(operands),
-            out_specs=jax.tree.map(lambda _: VMEM, shapes),
-            compiler_params=params(8),
-            cost_estimate=cost(1),
-            name=name,
-        )(*operands)
-
-    short = jax.ShapeDtypeStruct((n_x * n_y, n_z * 8, bands), BF16)
-    whole = jax.ShapeDtypeStruct((n_z * 8, bands), F32)
-    eighth = jax.ShapeDtypeStruct((8, bands), F32)
     given = lax.ppermute(margin_call(1), "core", swap)
     kept = margin_call(0)
-    share = small_call(pair_kernel, short, "pair", kept, given)
+    short = jax.ShapeDtypeStruct((n_x * n_y, n_z * 8, bands), BF16)
+    share = pl.pallas_call(
+        pair_kernel,
+        out_shape=short,
+        in_specs=[VMEM, VMEM],
+        out_specs=VMEM,
+        compiler_params=params(8),
+        cost_estimate=cost(1),
+        name="pair",
+    )(kept, given)
     share = lax.all_to_all(share, SHORT, 0, 0, tiled=True)
-    share = small_call(sum_kernel, whole, "sum", share).reshape(n_z, 8, bands)
+    share = pl.pallas_call(
+        partial_kernel,
+        out_shape=jax.ShapeDtypeStruct((n_z, n_z * 8, bands), BF16),
+        in_specs=[VMEM],
+        out_specs=VMEM,
+        compiler_params=params(8),
+        cost_estimate=cost(1),
+        name="partial",
+    )(share)
     share = lax.all_to_all(share, "z", 0, 0, tiled=True)
-    spread_out = jax.ShapeDtypeStruct((n_z, 8, bands), F32)
-    margins, coeffs = small_call(sum_kernel, (eighth, spread_out), "sum", share)
-
-    coeffs = lax.all_to_all(coeffs, "z", 0, 0, tiled=True).reshape(n_z * 8, bands)
-    coeffs = small_call(copies_kernel, short, "copies", coeffs)
+    margins, coeffs = pl.pallas_call(
+        total_kernel,
+        out_shape=(jax.ShapeDtypeStruct((8, bands), F32), short),
+        in_specs=[SMEM, VMEM],
+        out_specs=(VMEM, VMEM),
+        scratch_shapes=[pltpu.VMEM((n_z * 8, bands), F32)],
+        compiler_params=params(8),
+        cost_estimate=cost(1),
+        name="total",
+    )(place, share)
     coeffs = lax.all_to_all(coeffs, SHORT, 0, 0, tiled=True)
     other = lax.ppermute(coeffs, "core", swap)
 

time: 149 us -> 141 us (0.946)
  blocking collectives: 81.2 us -> 74.4 us
    all_to_all x1 -> x0, blocking collectives: 9.59 us -> none  [per_device(): lax.all_to_all(coeffs, 'z', 0, 0, tiled=True).reshape(n_z * 8, bands)]
    all_to_all x1, blocking collectives: 9.6 us -> 11.6 us  [per_device(): share = lax.all_to_all(share, 'z', 0, 0, tiled=True)]
where the time goes in v7:
time: 141 us
  blocking collectives  74.4 us (53%)
  Pallas kernels  26.2 us (19%)
  starting transfers between devices  18.9 us (13%)
  waiting for transfers between devices  16 us (11%)
  local copies, waits for them, and re-layouts  3.47 us (2%)
  between operations  1.5 us (1%)
    all_to_all x1, blocking collectives, per_device(): lax.all_to_all(residual, BAND, 0, 0, tiled=True).reshape(bands, width)  23.7 us
    all_to_all x1, blocking collectives, per_device(): coeffs = lax.all_to_all(coeffs, SHORT, 0, 0, tiled=True)  13.4 us
    all_to_all x1, blocking collectives, per_device(): share = lax.all_to_all(share, SHORT, 0, 0, tiled=True)  13.2 us
    all_to_all x1, blocking collectives, per_device(): pay = lax.all_to_all(pay, DOM, 0, 0, tiled=True)  12.5 us
    all_to_all x1, blocking collectives, per_device(): share = lax.all_to_all(share, 'z', 0, 0, tiled=True)  11.6 us
    ppermute x1, waiting for transfers between devices, per_device(): above = lax.ppermute(shares, DOM, down)  10.7 us
    ppermute x1, starting transfers between devices, per_device(): right = lax.ppermute(x, DOM, down)  8.93 us
    pallas_call x1, Pallas kernels, per_device(): pl.pallas_call(functools.partial(local_kernel, planes), out_shape=(jax.Sh...  6.31 us
  transfers between devices with their start and end apart: 6, of which 2 were waited for; matrix products, arithmetic and copies ran while one was open for 0% of the time, Pallas kernels for 9%

profile of v7, /device:TPU:1, one launch (start us, length us, event | category | flops | bytes accessed | tf_op | source)
XLA Modules:
  0.0 140.6 jit_solution(11604661053001744965)
XLA Ops:
  0.6 0.0 copy-start.5
  0.6 0.0 copy-start.3
  0.7 0.0 copy-start.2
  0.7 0.0 copy-start.4
  0.7 3.1 %reshape.17.x_ref = bf16[32,18432]{1,0:T(8,128)(2,1)S(1)} reshape(bf16[32,6,48,64]{3,2,1,0:T(8,128)(2,1)} %param.9) | data formatting | bytes 2359296 | tf_op jit(solution)/shard_map/reshape | solution.py:376
  3.8 0.0 copy-start.6
  3.8 0.0 copy-start.1
  3.8 8.9 %collective-permute-start.1 = (bf16[32,18432]{1,0:T(8,128)(2,1)S(1)}, bf16[32,18432]{1,0:T(8,128)(2,1)}, u32[]{:S(2)}, u32[]{:S(2)}) collective-permute-start(bf16[32,18432]{1,0:T(8,128)(2,1)S(1)} %reshape.17.x_ref), channel_id=1, source_target_pairs={{1,0},{2,1},{3,2},{4,3},{5,4},{6,5},{7,6},{8,7},{9,8},{10,9},{11,1... | collective-permute-start | bytes 3538952 | tf_op jit(solution)/shard_map/ppermute | solution.py:378
  12.8 0.0 collective-permute-start
  13.4 0.0 copy-done.5
  13.5 0.1 concatenate.3.place_ref
  13.6 0.1 fusion.onehot_ref.onehot_hbm
  13.7 0.0 copy-done.3
  13.7 0.0 copy-done.2
  13.7 2.0 %inner.1 = (f32[32,128]{1,0:T(8,128)S(1)}, s32[8]{0:T(128)S(1)}) custom-call(s32[64]{0:T(128)S(1)} %copy-done.3, s32[8]{0:T(128)S(1)} %concatenate.3.place_ref, bf16[32,18432]{1,0:T(8,128)(2,1)S(1)} %reshape.17.x_ref, f32[64,128]{1,0:T(8,128)S(1)} %copy-done.2, f32[128,128]{1,0:T(8,128)S(1)} %fusion.onehot_ref.onehot_hbm), custom_call_target="tpu_custom_call" | custom-call | bytes 6000000 | tf_op jit(solution)/shard_map/inner/pallas_call | solution.py:393
  15.7 4.9 %collective-permute-start.3 = (f32[32,128]{1,0:T(8,128)S(1)}, f32[32,128]{1,0:T(8,128)S(1)}, u32[]{:S(2)}, u32[]{:S(2)}) collective-permute-start(f32[32,128]{1,0:T(8,128)S(1)} %get-tuple-element.13.mine_ref), channel_id=1, source_target_pairs={{1,0},{2,1},{3,2},{4,3},{5,4},{6,5},{7,6},{8,7},{9,8},{10,9},{11,1... | collective-permute-start | bytes 49160 | tf_op jit(solution)/shard_map/ppermute | solution.py:406
  20.5 0.0 collective-permute-start.2
  20.5 0.0 copy-done.4
  20.5 0.1 reshape.19.pot_ref
  20.7 0.0 copy-done.6
  20.7 0.1 pad.9.coupling_ref
  20.8 0.0 copy-done.1
  20.8 6.3 %local.1 = (f32[32,18432]{1,0:T(8,128)S(1)}, f32[32,128]{1,0:T(8,128)S(1)}) custom-call(bf16[32,18432]{1,0:T(8,128)(2,1)S(1)} %reshape.17.x_ref, f32[1,18432]{1,0:T(1,128)S(1)} %reshape.19.pot_ref, bf16[3,1024,256]{2,1,0:T(8,128)(2,1)S(1)} %copy-done.1), custom_call_target="tpu_custom_call" | custom-call | bytes 21000000 | tf_op jit(solution)/shard_map/local/pallas_call | solution.py:408
  27.1 10.7 %collective-permute-done.3.above_hbm = f32[32,128]{1,0:T(8,128)S(1)} collective-permute-done((f32[32,128]{1,0:T(8,128)S(1)}, f32[32,128]{1,0:T(8,128)S(1)}, u32[]{:S(2)}, u32[]{:S(2)}) %collective-permute-start.3) | collective-permute-done | bytes 16416 | tf_op jit(solution)/shard_map/ppermute | solution.py:406
  37.8 5.3 %collective-permute-done.2.below_hbm = f32[32,128]{1,0:T(8,128)S(1)} collective-permute-done((f32[32,128]{1,0:T(8,128)S(1)}, f32[32,128]{1,0:T(8,128)S(1)}, u32[]{:S(2)}, u32[]{:S(2)}) %collective-permute-start.2) | collective-permute-done | bytes 16416 | tf_op jit(solution)/shard_map/ppermute | solution.py:405
  43.1 0.0 collective-permute-done.1.right_hbm
  43.1 0.0 collective-permute-done.left_hbm
  43.1 0.0 copy-start
  43.1 3.9 %hamilton.1 = (f32[32,18432]{1,0:T(8,128)S(1)}, f32[32,9,1,128]{3,2,1,0:T(1,128)S(1)}) custom-call(f32[32,18432]{1,0:T(8,128)S(1)} %get-tuple-element.11.h0_ref, bf16[32,18432]{1,0:T(8,128)(2,1)S(1)} %reshape.17.x_ref, bf16[32,18432]{1,0:T(8,128)(2,1)} %collective-permute-done.left_hbm, bf16[32,18432]{1,0:T(8,128)(2,1)} %collective-permute-done.1.right_hbm, ...), custom_call_target="tpu_custom_call" | custom-call | bytes 15000000 | tf_op jit(solution)/shard_map/hamilton/pallas_call | solution.py:422
  47.0 12.5 %all_to_all.25.pay_ref = f32[32,9,1,128]{3,2,1,0:T(1,128)S(1)} all-to-all(f32[32,9,1,128]{3,2,1,0:T(1,128)S(1)} %get-tuple-element.15), channel_id=1, replica_groups=mesh['x'=4,'core'=2,'z'=8,'y'=4] {'z','y'}, dimensions={0} | all-to-all | bytes 294912 | tf_op jit(solution)/shard_map/all_to_all | solution.py:437
  59.6 1.9 %residual.1 = bf16[8,32,2304]{2,1,0:T(8,128)(2,1)S(1)} custom-call(s32[64]{0:T(128)S(1)} %copy-done.3, s32[8]{0:T(128)S(1)} %get-tuple-element.10.place_ref, f32[32,18432]{1,0:T(8,128)S(1)} %get-tuple-element.14.h_ref, bf16[32,18432]{1,0:T(8,128)(2,1)S(1)} %reshape.17.x_ref, f32[32,9,1,128]{3,2,1,0:T(1,128)S(1)} %all_to_all.25.pay_ref, ...), custom_call_target="tpu_custom_call" | custom-call | bytes 6000000 | tf_op jit(solution)/shard_map/residual/pallas_call | solution.py:439
  61.5 23.7 %all_to_all.26 = bf16[8,32,2304]{2,1,0:T(8,128)(2,1)S(1)} all-to-all(bf16[8,32,2304]{2,1,0:T(8,128)(2,1)S(1)} %residual.1), channel_id=1, replica_groups=mesh['x'=4,'core'=2,'z'=8,'y'=4] {'x','core'}, dimensions={0} | all-to-all | bytes 2359296 | tf_op jit(solution)/shard_map/all_to_all | solution.py:454
  85.1 0.0 copy-done
  85.1 2.4 %margin.3 = f32[4,256,256]{2,1,0:T(8,128)S(1)} custom-call(s32[8]{0:T(128)S(1)} %get-tuple-element.10.place_ref, bf16[6,4,2,256,384]{4,3,2,1,0:T(8,128)(2,1)S(1)} %bitcast.13, bf16[256,2304]{1,0:T(8,128)(2,1)S(1)} %bitcast.17), custom_call_target="tpu_custom_call" | custom-call | bytes 9000000 | tf_op jit(solution)/shard_map/margin/pallas_call | solution.py:460
  87.5 1.0 collective-permute-start.4
  88.5 2.4 %margin.2.kept_ref = f32[4,256,256]{2,1,0:T(8,128)S(1)} custom-call(s32[8]{0:T(128)S(1)} %get-tuple-element.10.place_ref, bf16[6,4,2,256,384]{4,3,2,1,0:T(8,128)(2,1)S(1)} %bitcast.14, bf16[256,2304]{1,0:T(8,128)(2,1)S(1)} %bitcast.18), custom_call_target="tpu_custom_call" | custom-call | bytes 9000000 | tf_op jit(solution)/shard_map/margin/pallas_call | solution.py:460
  90.8 0.0 collective-permute-done.4.given_ref
  90.8 0.1 pair.1
  90.9 13.2 %all_to_all.27.in_ref = bf16[16,64,256]{2,1,0:T(8,128)(2,1)S(1)} all-to-all(bf16[16,64,256]{2,1,0:T(8,128)(2,1)S(1)} %pair.1), channel_id=1, replica_groups=mesh['x'=4,'core'=2,'z'=8,'y'=4] {'x','y'}, dimensions={0} | all-to-all | bytes 1048576 | tf_op jit(solution)/shard_map/all_to_all | solution.py:482
  104.1 0.1 partial.1
  104.2 11.6 %all_to_all.28.in_ref = bf16[8,64,256]{2,1,0:T(8,128)(2,1)S(1)} all-to-all(bf16[8,64,256]{2,1,0:T(8,128)(2,1)S(1)} %partial.1), channel_id=1, replica_groups=mesh['x'=4,'core'=2,'z'=8,'y'=4] {'z'}, dimensions={0} | all-to-all | bytes 524288 | tf_op jit(solution)/shard_map/all_to_all | solution.py:492
  115.8 1.2 total.1
  117.0 13.4 %all_to_all.29.coeff_ref = bf16[16,64,256]{2,1,0:T(8,128)(2,1)S(1)} all-to-all(bf16[16,64,256]{2,1,0:T(8,128)(2,1)S(1)} %get-tuple-element.16), channel_id=1, replica_groups=mesh['x'=4,'core'=2,'z'=8,'y'=4] {'x','y'}, dimensions={0} | all-to-all | bytes 1048576 | tf_op jit(solution)/shard_map/all_to_all | solution.py:503
  130.4 4.2 %collective-permute-start.5 = (bf16[16,64,256]{2,1,0:T(8,128)(2,1)S(1)}, bf16[16,64,256]{2,1,0:T(8,128)(2,1)S(1)}, u32[]{:S(2)}, u32[]{:S(2)}) collective-permute-start(bf16[16,64,256]{2,1,0:T(8,128)(2,1)S(1)} %all_to_all.29.coeff_ref), channel_id=1, source_target_pairs={{0,32},{32,0},{1,33},{33,1},{2,34},{34,2},{3,35},{35,3},{4,36},{36... | collective-permute-start | bytes 1572872 | tf_op jit(solution)/shard_map/ppermute | solution.py:504
  134.6 2.5 %clean.2.r_ref = f32[6,256,384]{2,1,0:T(8,128)S(1)} custom-call(s32[8]{0:T(128)S(1)} %get-tuple-element.10.place_ref, bf16[6,4,2,256,384]{4,3,2,1,0:T(8,128)(2,1)S(1)} %bitcast.15, bf16[16,64,256]{2,1,0:T(8,128)(2,1)S(1)} %all_to_all.29.coeff_ref, bf16[256,2304]{1,0:T(8,128)(2,1)S(1)} %bitcast.19), custom_call_target="tpu_custom_call" | custom-call | bytes 9000000 | tf_op jit(solution)/shard_map/clean/pallas_call | solution.py:507
  137.1 0.0 collective-permute-done.5.coeff_ref
  137.1 3.5 %clean.3 = bf16[6,256,384]{2,1,0:T(8,128)(2,1)} custom-call(s32[8]{0:T(128)S(1)} %get-tuple-element.10.place_ref, bf16[6,4,2,256,384]{4,3,2,1,0:T(8,128)(2,1)S(1)} %bitcast.16, bf16[16,64,256]{2,1,0:T(8,128)(2,1)S(1)} %collective-permute-done.5.coeff_ref, f32[6,256,384]{2,1,0:T(8,128)S(1)} %clean.2.r_ref), custom_call_target="tpu_custom_call" | custom-call | bytes 9000000 | tf_op jit(solution)/shard_map/clean/pallas_call | solution.py:507
  (4 shorter events, 0.0 us)
Async XLA Ops:
  0.6 12.8 %copy-start.5 = (s32[64]{0:T(128)S(1)}, s32[64]{0:T(128)}, u32[]{:S(2)}) copy-start(s32[64]{0:T(128)} %param.14) | copy-start | bytes 772
  0.6 13.1 %copy-start.3 = (s32[64]{0:T(128)S(1)}, s32[64]{0:T(128)}, u32[]{:S(2)}) copy-start(s32[64]{0:T(128)} %block_ref.3) | copy-start | bytes 772
  0.7 13.1 %copy-start.2 = (f32[64,128]{1,0:T(8,128)S(1)}, f32[64,128]{1,0:T(8,128)}, u32[]{:S(2)}) copy-start(f32[64,128]{1,0:T(8,128)} %proj_hbm.1) | copy-start | bytes 98308
  0.7 19.9 %copy-start.4 = (f32[6,48,64]{2,1,0:T(8,128)S(1)}, f32[6,48,64]{2,1,0:T(8,128)}, u32[]{:S(2)}) copy-start(f32[6,48,64]{2,1,0:T(8,128)} %param.10) | copy-start | bytes 221188
  3.8 16.9 %copy-start.6 = (f32[32]{0:T(128)S(1)}, f32[32]{0:T(128)}, u32[]{:S(2)}) copy-start(f32[32]{0:T(128)} %param.12) | copy-start | bytes 388
  3.8 16.9 %copy-start.1 = (bf16[3,1024,256]{2,1,0:T(8,128)(2,1)S(1)}, bf16[3,1024,256]{2,1,0:T(8,128)(2,1)}, u32[]{:S(2)}) copy-start(bf16[3,1024,256]{2,1,0:T(8,128)(2,1)} %constant.73.clone.w_ref) | copy-start | bytes 4718596
  3.8 39.2 %collective-permute-start.1 = (bf16[32,18432]{1,0:T(8,128)(2,1)S(1)}, bf16[32,18432]{1,0:T(8,128)(2,1)}, u32[]{:S(2)}, u32[]{:S(2)}) collective-permute-start(bf16[32,18432]{1,0:T(8,128)(2,1)S(1)} %reshape.17.x_ref), channel_id=1, source_target_pairs={{1,0},{2,1},{3,2},{4,3},{5,4},{6,5},{7,6},{8,7},{9,8},{10,9},{11,1... | collective-permute-start | bytes 3538952 | tf_op jit(solution)/shard_map/ppermute | solution.py:378
  12.8 30.3 %collective-permute-start = (bf16[32,18432]{1,0:T(8,128)(2,1)S(1)}, bf16[32,18432]{1,0:T(8,128)(2,1)}, u32[]{:S(2)}, u32[]{:S(2)}) collective-permute-start(bf16[32,18432]{1,0:T(8,128)(2,1)S(1)} %reshape.17.x_ref), channel_id=1, source_target_pairs={{0,1},{1,2},{2,3},{3,4},{4,5},{5,6},{6,7},{7,8},{8,9},{9,10},{10,1... | collective-permute-start | bytes 3538952 | tf_op jit(solution)/shard_map/ppermute | solution.py:377
  15.7 22.1 %collective-permute-start.3 = (f32[32,128]{1,0:T(8,128)S(1)}, f32[32,128]{1,0:T(8,128)S(1)}, u32[]{:S(2)}, u32[]{:S(2)}) collective-permute-start(f32[32,128]{1,0:T(8,128)S(1)} %get-tuple-element.13.mine_ref), channel_id=1, source_target_pairs={{1,0},{2,1},{3,2},{4,3},{5,4},{6,5},{7,6},{8,7},{9,8},{10,9},{11,1... | collective-permute-start | bytes 49160 | tf_op jit(solution)/shard_map/ppermute | solution.py:406
  20.5 22.5 %collective-permute-start.2 = (f32[32,128]{1,0:T(8,128)S(1)}, f32[32,128]{1,0:T(8,128)S(1)}, u32[]{:S(2)}, u32[]{:S(2)}) collective-permute-start(f32[32,128]{1,0:T(8,128)S(1)} %get-tuple-element.13.mine_ref), channel_id=1, source_target_pairs={{0,1},{1,2},{2,3},{3,4},{4,5},{5,6},{6,7},{7,8},{8,9},{9,10},{10,1... | collective-permute-start | bytes 49160 | tf_op jit(solution)/shard_map/ppermute | solution.py:405
  43.1 42.1 %copy-start = (bf16[2048,6,384]{2,0,1:T(8,128)(2,1)S(1)}, bf16[2048,6,384]{2,0,1:T(8,128)(2,1)}, u32[]{:S(2)}) copy-start(bf16[2048,6,384]{2,0,1:T(8,128)(2,1)} %param.16) | copy-start | bytes 28311556
  87.5 3.3 %collective-permute-start.4 = (f32[4,256,256]{2,1,0:T(8,128)S(1)}, f32[4,256,256]{2,1,0:T(8,128)S(1)}, u32[]{:S(2)}, u32[]{:S(2)}) collective-permute-start(f32[4,256,256]{2,1,0:T(8,128)S(1)} %margin.3), channel_id=1, source_target_pairs={{0,32},{32,0},{1,33},{33,1},{2,34},{34,2},{3,35},{35,3},{4,36},{36... | collective-permute-start | bytes 3145736 | tf_op jit(solution)/shard_map/ppermute | solution.py:470
  130.4 6.6 %collective-permute-start.5 = (bf16[16,64,256]{2,1,0:T(8,128)(2,1)S(1)}, bf16[16,64,256]{2,1,0:T(8,128)(2,1)S(1)}, u32[]{:S(2)}, u32[]{:S(2)}) collective-permute-start(bf16[16,64,256]{2,1,0:T(8,128)(2,1)S(1)} %all_to_all.29.coeff_ref), channel_id=1, source_target_pairs={{0,32},{32,0},{1,33},{33,1},{2,34},{34,2},{3,35},{35,3},{4,36},{36... | collective-permute-start | bytes 1572872 | tf_op jit(solution)/shard_map/ppermute | solution.py:504

commit v8 on v7

--- a/solution.py
+++ b/solution.py
@@ -24,7 +24,8 @@
 WIDTH = 6
 DOM = ("z", "y")
 BAND = ("x", "core")
-SHORT = ("x", "y")
+SHORT = ("y", "x")
+ENERGY = ("y", "z")
 F32 = jnp.float32
 BF16 = jnp.bfloat16
 VMEM = pl.BlockSpec(memory_space=pltpu.VMEM)
@@ -132,18 +133,11 @@
 ):
     rows, cells = x_ref.shape
     plane = cells // planes
-    chunks = sems.shape[0]
-    chunk = plane // chunks
     copies = []
-    for k in range(chunks):
-        for p in range(planes):
-            where = slice(p * plane + k * chunk, p * plane + (k + 1) * chunk)
-            for i, (src, dst) in enumerate(
-                ((left_hbm, left_ref), (right_hbm, right_ref))
-            ):
-                copies.append(
-                    pltpu.make_async_copy(src.at[:, where], dst.at[:, where], sems.at[k, p, i])
-                )
+    for i in range(rows // 16):
+        pick = slice(i * 16, (i + 1) * 16)
+        for j, (src, dst) in enumerate(((left_hbm, left_ref), (right_hbm, right_ref))):
+            copies.append(pltpu.make_async_copy(src.at[pick], dst.at[pick], sems.at[i, j]))
     late = [
         pltpu.make_async_copy(below_hbm, below_ref, late_sems.at[0]),
         pltpu.make_async_copy(above_hbm, above_ref, late_sems.at[1]),
@@ -152,13 +146,15 @@
         copy.start()
     n = BS // 4
 
-    def halo(step, carry):
-        sums = []
-        for top in range(0, rows, 16):
-            pick = slice(top, top + 16)
+    parts = []
+    for i in range(rows // 16):
+        pick = slice(i * 16, (i + 1) * 16)
+        for copy in copies[2 * i : 2 * i + 2]:
+            copy.wait()
+
+        def halo(step, num, pick=pick):
             before = []
             after = []
-            num = carry[top // 16]
             for p in range(planes):
                 where = pl.ds(pl.multiple_of(p * plane + step * BS, BS), BS)
                 before.append(left_ref[pick, where].astype(F32))
@@ -172,17 +168,10 @@
                     value += HALF[planes + j - p] * after[j]
                 h_ref[pick, where] = value
                 num += value * x_ref[pick, where].astype(F32)
-            sums.append(num)
-        return tuple(sums)
-
-    zero = jnp.zeros((16, BS), F32)
-    num = (zero,) * (rows // 16)
-    steps = chunk // BS
-    for k in range(chunks):
-        for copy in copies[k * planes * 2 : (k + 1) * planes * 2]:
-            copy.wait()
-        num = lax.fori_loop(k * steps, (k + 1) * steps, halo, num)
-    num = jnp.concatenate(num, axis=0)
+            return num
+
+        parts.append(lax.fori_loop(0, plane // BS, halo, jnp.zeros((16, BS), F32), unroll=2))
+    num = jnp.concatenate(parts, axis=0)
 
     for copy in late:
         copy.wait()
@@ -301,7 +290,7 @@
                 kept_ref[i, at : at + 8] + given_ref[i, at : at + 8]
                 for at in range(y * 8, share_rows, n_y * 8)
             ]
-            out_ref[i * n_y + y] = jnp.concatenate(pieces, axis=0).astype(BF16)
+            out_ref[y * n_x + i] = jnp.concatenate(pieces, axis=0).astype(BF16)
 
 
 def partial_kernel(in_ref, out_ref):
@@ -313,7 +302,7 @@
         out_ref[i] = value
 
 
-def total_kernel(place_ref, in_ref, margin_ref, coeff_ref, total_ref):
+def total_kernel(in_ref, total_ref, coeff_ref):
     acc = in_ref[0].astype(F32)
     for i in range(1, in_ref.shape[0]):
         acc += in_ref[i].astype(F32)
@@ -321,19 +310,26 @@
     value = acc.astype(BF16)
     for i in range(coeff_ref.shape[0]):
         coeff_ref[i] = value
-    margin_ref[...] = total_ref[pl.ds(pl.multiple_of(place_ref[5] * 8, 8), 8)]
-
-
-def clean_kernel(side, place_ref, locked_ref, coeff_ref, r_ref, out_ref, turned_ref):
+
+
+def clean_kernel(side, place_ref, locked_ref, coeff_ref, r_ref, *refs):
     planes, n_x, _, share_rows, part = locked_ref.shape
     n_y = coeff_ref.shape[0] // n_x
     core = place_ref[3 + side]
+    copies = []
+    if side == 0:
+        total_ref, out_ref, margin_hbm, turned_ref, sems = refs
+        own = pl.ds(pl.multiple_of(place_ref[5] * 8, 8), 8)
+        copies.append(pltpu.make_async_copy(total_ref.at[own], margin_hbm, sems.at[0]))
+        copies[0].start()
+    else:
+        out_ref, turned_ref, stage_ref, sems = refs
     for i in range(n_x):
-        pieces = [coeff_ref[i * n_y + y].astype(F32) for y in range(n_y)]
+        pieces = [coeff_ref[y * n_x + i].astype(F32) for y in range(n_y)]
         whole = [
             pieces[at % n_y][at // n_y * 8 : at // n_y * 8 + 8] for at in range(share_rows // 8)
         ]
-        turned_ref[i] = jnp.concatenate(whole, axis=0).T.astype(BF16)
+        turned_ref[i] = jnp.concatenate(whole, axis=0).astype(BF16).T
     for p in range(planes):
         term = None
         for i in range(n_x):
@@ -342,7 +338,12 @@
         if side == 0:
             out_ref[p] = r_ref[:, p * part : (p + 1) * part].astype(F32) - term
         else:
-            out_ref[p] = (r_ref[p] - term).astype(BF16)
+            stage_ref[p] = (r_ref[p] - term).astype(BF16)
+            copy = pltpu.make_async_copy(stage_ref.at[p], out_ref.at[p], sems.at[p])
+            copy.start()
+            copies.append(copy)
+    for copy in copies:
+        copy.wait()
 
 
 def ring(size):
@@ -389,6 +390,7 @@
     coupling_row = jnp.pad(coupling[None], ((0, 0), (n, BS - 2 * n)))
 
     near = (here + domains + jnp.arange(-1, 2, dtype=jnp.int32)) % domains
+    near = near % n_y * n_z + near // n_y
     place = jnp.concatenate([near, jnp.stack([core, 1 - core, lax.axis_index("z"), 0, 0])])
     shares, place = pl.pallas_call(
         inner_kernel,
@@ -429,12 +431,12 @@
         out_specs=(VMEM, VMEM),
         scratch_shapes=[pltpu.VMEM((rows, cells), BF16)] * 2
         + [pltpu.VMEM((rows, BS), F32)] * 2
-        + [pltpu.SemaphoreType.DMA((3, planes, 2)), pltpu.SemaphoreType.DMA((2,))],
+        + [pltpu.SemaphoreType.DMA((rows // 16, 2)), pltpu.SemaphoreType.DMA((2,))],
         compiler_params=params(24),
         cost_estimate=cost(5),
         name="hamilton",
     )(h0, x, left, right, den, shares, coupling_row, below, above)
-    pay = lax.all_to_all(pay, DOM, 0, 0, tiled=True)
+    pay = lax.all_to_all(pay, ENERGY, 0, 0, tiled=True)
 
     residual = pl.pallas_call(
         functools.partial(residual_kernel, planes),
@@ -490,33 +492,35 @@
         name="partial",
     )(share)
     share = lax.all_to_all(share, "z", 0, 0, tiled=True)
-    margins, coeffs = pl.pallas_call(
+    total, coeffs = pl.pallas_call(
         total_kernel,
-        out_shape=(jax.ShapeDtypeStruct((8, bands), F32), short),
-        in_specs=[SMEM, VMEM],
+        out_shape=(jax.ShapeDtypeStruct((n_z * 8, bands), F32), short),
+        in_specs=[VMEM],
         out_specs=(VMEM, VMEM),
-        scratch_shapes=[pltpu.VMEM((n_z * 8, bands), F32)],
         compiler_params=params(8),
         cost_estimate=cost(1),
         name="total",
-    )(place, share)
+    )(share)
     coeffs = lax.all_to_all(coeffs, SHORT, 0, 0, tiled=True)
     other = lax.ppermute(coeffs, "core", swap)
 
-    def clean_call(side, coeffs, before, kind):
+    def clean_call(side, *operands):
+        made = jax.ShapeDtypeStruct((planes, bands, part), BF16 if side else F32)
+        turned = pltpu.VMEM((n_x, bands, share_rows), BF16)
+        stage = [pltpu.VMEM((planes, bands, part), BF16)] * side
         return pl.pallas_call(
             functools.partial(clean_kernel, side),
-            out_shape=jax.ShapeDtypeStruct((planes, bands, part), kind),
-            in_specs=[SMEM, VMEM, VMEM, VMEM],
-            out_specs=VMEM,
-            scratch_shapes=[pltpu.VMEM((n_x, bands, share_rows), BF16)],
+            out_shape=made if side else (made, jax.ShapeDtypeStruct((8, bands), F32)),
+            in_specs=[SMEM] + [VMEM] * (len(operands) + 1),
+            out_specs=ANY if side else (VMEM, ANY),
+            scratch_shapes=[turned] + stage + [pltpu.SemaphoreType.DMA((planes,))],
             compiler_params=params(8),
             cost_estimate=cost(3),
             name="clean",
-        )(place, by_plane, coeffs, before)
-
-    part_clean = clean_call(0, coeffs, residual, F32)
-    orthogonal = clean_call(1, other, part_clean, BF16)
+        )(place, by_plane, *operands)
+
+    part_clean, margins = clean_call(0, coeffs, residual, total)
+    orthogonal = clean_call(1, other, part_clean)
     return orthogonal.transpose(1, 0, 2), margins
 
 

time: 141 us -> 139 us (0.986)
  Pallas kernels: 26.2 us -> 24.5 us
    pallas_call x3, Pallas kernels: 7.14 us -> 5.7 us  [the longest x2 5.64 us: clean_call(): pl.pallas_call(functools.partial(clean_kernel, side), out_shape=made if s...]
where the time goes in v8:
time: 139 us
  blocking collectives  74.5 us (54%)
  Pallas kernels  24.5 us (18%)
  starting transfers between devices  18.6 us (13%)
  waiting for transfers between devices  16 us (12%)
  local copies, waits for them, and re-layouts  3.47 us (2%)
  between operations  1.67 us (1%)
    all_to_all x1, blocking collectives, per_device(): lax.all_to_all(residual, BAND, 0, 0, tiled=True).reshape(bands, width)  23.7 us
    all_to_all x1, blocking collectives, per_device(): share = lax.all_to_all(share, SHORT, 0, 0, tiled=True)  13.6 us
    all_to_all x1, blocking collectives, per_device(): coeffs = lax.all_to_all(coeffs, SHORT, 0, 0, tiled=True)  12.8 us
    all_to_all x1, blocking collectives, per_device(): pay = lax.all_to_all(pay, ENERGY, 0, 0, tiled=True)  12.3 us
    all_to_all x1, blocking collectives, per_device(): share = lax.all_to_all(share, 'z', 0, 0, tiled=True)  12.2 us
    ppermute x1, waiting for transfers between devices, per_device(): above = lax.ppermute(shares, DOM, down)  10.7 us
    ppermute x1, starting transfers between devices, per_device(): right = lax.ppermute(x, DOM, down)  8.93 us
    pallas_call x1, Pallas kernels, per_device(): pl.pallas_call(functools.partial(local_kernel, planes), out_shape=(jax.Sh...  6.31 us
  transfers between devices with their start and end apart: 6, of which 2 were waited for; matrix products, arithmetic and copies ran while one was open for 0% of the time, Pallas kernels for 9%

profile of v8, /device:TPU:1, one launch (start us, length us, event | category | flops | bytes accessed | tf_op | source)
XLA Modules:
  0.0 138.9 jit_solution(6756189622619981265)
XLA Ops:
  0.6 0.0 copy-start.5
  0.6 0.0 copy-start.3
  0.7 0.0 copy-start.2
  0.7 0.0 copy-start.4
  0.7 3.1 %reshape.17.x_ref = bf16[32,18432]{1,0:T(8,128)(2,1)S(1)} reshape(bf16[32,6,48,64]{3,2,1,0:T(8,128)(2,1)} %param.9) | data formatting | bytes 2359296 | tf_op jit(solution)/shard_map/reshape | solution.py:377
  3.8 0.0 copy-start.6
  3.8 0.0 copy-start.1
  3.8 8.9 %collective-permute-start.1 = (bf16[32,18432]{1,0:T(8,128)(2,1)S(1)}, bf16[32,18432]{1,0:T(8,128)(2,1)}, u32[]{:S(2)}, u32[]{:S(2)}) collective-permute-start(bf16[32,18432]{1,0:T(8,128)(2,1)S(1)} %reshape.17.x_ref), channel_id=1, source_target_pairs={{1,0},{2,1},{3,2},{4,3},{5,4},{6,5},{7,6},{8,7},{9,8},{10,9},{11,1... | collective-permute-start | bytes 3538952 | tf_op jit(solution)/shard_map/ppermute | solution.py:379
  12.8 0.0 collective-permute-start
  13.4 0.0 copy-done.5
  13.5 0.1 concatenate.3.place_ref
  13.6 0.1 fusion.onehot_ref.onehot_hbm
  13.7 0.0 copy-done.3
  13.7 0.0 copy-done.2
  13.7 2.0 %inner.1 = (f32[32,128]{1,0:T(8,128)S(1)}, s32[8]{0:T(128)S(1)}) custom-call(s32[64]{0:T(128)S(1)} %copy-done.3, s32[8]{0:T(128)S(1)} %concatenate.3.place_ref, bf16[32,18432]{1,0:T(8,128)(2,1)S(1)} %reshape.17.x_ref, f32[64,128]{1,0:T(8,128)S(1)} %copy-done.2, f32[128,128]{1,0:T(8,128)S(1)} %fusion.onehot_ref.onehot_hbm), custom_call_target="tpu_custom_call" | custom-call | bytes 6000000 | tf_op jit(solution)/shard_map/inner/pallas_call | solution.py:395
  15.7 4.9 %collective-permute-start.3 = (f32[32,128]{1,0:T(8,128)S(1)}, f32[32,128]{1,0:T(8,128)S(1)}, u32[]{:S(2)}, u32[]{:S(2)}) collective-permute-start(f32[32,128]{1,0:T(8,128)S(1)} %get-tuple-element.15.mine_ref), channel_id=1, source_target_pairs={{1,0},{2,1},{3,2},{4,3},{5,4},{6,5},{7,6},{8,7},{9,8},{10,9},{11,1... | collective-permute-start | bytes 49160 | tf_op jit(solution)/shard_map/ppermute | solution.py:408
  20.5 0.0 collective-permute-start.2
  20.5 0.0 copy-done.4
  20.5 0.1 reshape.19.pot_ref
  20.7 0.0 copy-done.6
  20.7 0.1 pad.9.coupling_ref
  20.8 0.0 copy-done.1
  20.8 6.3 %local.1 = (f32[32,18432]{1,0:T(8,128)S(1)}, f32[32,128]{1,0:T(8,128)S(1)}) custom-call(bf16[32,18432]{1,0:T(8,128)(2,1)S(1)} %reshape.17.x_ref, f32[1,18432]{1,0:T(1,128)S(1)} %reshape.19.pot_ref, bf16[3,1024,256]{2,1,0:T(8,128)(2,1)S(1)} %copy-done.1), custom_call_target="tpu_custom_call" | custom-call | bytes 21000000 | tf_op jit(solution)/shard_map/local/pallas_call | solution.py:410
  27.1 10.7 %collective-permute-done.3.above_hbm = f32[32,128]{1,0:T(8,128)S(1)} collective-permute-done((f32[32,128]{1,0:T(8,128)S(1)}, f32[32,128]{1,0:T(8,128)S(1)}, u32[]{:S(2)}, u32[]{:S(2)}) %collective-permute-start.3) | collective-permute-done | bytes 16416 | tf_op jit(solution)/shard_map/ppermute | solution.py:408
  37.8 5.3 %collective-permute-done.2.below_hbm = f32[32,128]{1,0:T(8,128)S(1)} collective-permute-done((f32[32,128]{1,0:T(8,128)S(1)}, f32[32,128]{1,0:T(8,128)S(1)}, u32[]{:S(2)}, u32[]{:S(2)}) %collective-permute-start.2) | collective-permute-done | bytes 16416 | tf_op jit(solution)/shard_map/ppermute | solution.py:407
  43.1 0.0 collective-permute-done.1.right_hbm
  43.1 0.0 collective-permute-done.left_hbm
  43.1 0.0 copy-start
  43.1 3.7 %hamilton.1 = (f32[32,18432]{1,0:T(8,128)S(1)}, f32[32,9,1,128]{3,2,1,0:T(1,128)S(1)}) custom-call(f32[32,18432]{1,0:T(8,128)S(1)} %get-tuple-element.13.h0_ref, bf16[32,18432]{1,0:T(8,128)(2,1)S(1)} %reshape.17.x_ref, bf16[32,18432]{1,0:T(8,128)(2,1)} %collective-permute-done.left_hbm, bf16[32,18432]{1,0:T(8,128)(2,1)} %collective-permute-done.1.right_hbm, ...), custom_call_target="tpu_custom_call" | custom-call | bytes 15000000 | tf_op jit(solution)/shard_map/hamilton/pallas_call | solution.py:424
  46.8 12.3 %all_to_all.25.pay_ref = f32[32,9,1,128]{3,2,1,0:T(1,128)S(1)} all-to-all(f32[32,9,1,128]{3,2,1,0:T(1,128)S(1)} %get-tuple-element.17), channel_id=1, replica_groups=mesh['x'=4,'core'=2,'z'=8,'y'=4] {'y','z'}, dimensions={0} | all-to-all | bytes 294912 | tf_op jit(solution)/shard_map/all_to_all | solution.py:439
  59.1 1.9 %residual.1 = bf16[8,32,2304]{2,1,0:T(8,128)(2,1)S(1)} custom-call(s32[64]{0:T(128)S(1)} %copy-done.3, s32[8]{0:T(128)S(1)} %get-tuple-element.12.place_ref, f32[32,18432]{1,0:T(8,128)S(1)} %get-tuple-element.16.h_ref, bf16[32,18432]{1,0:T(8,128)(2,1)S(1)} %reshape.17.x_ref, f32[32,9,1,128]{3,2,1,0:T(1,128)S(1)} %all_to_all.25.pay_ref, ...), custom_call_target="tpu_custom_call" | custom-call | bytes 6000000 | tf_op jit(solution)/shard_map/residual/pallas_call | solution.py:441
  61.0 23.7 %all_to_all.26 = bf16[8,32,2304]{2,1,0:T(8,128)(2,1)S(1)} all-to-all(bf16[8,32,2304]{2,1,0:T(8,128)(2,1)S(1)} %residual.1), channel_id=1, replica_groups=mesh['x'=4,'core'=2,'z'=8,'y'=4] {'x','core'}, dimensions={0} | all-to-all | bytes 2359296 | tf_op jit(solution)/shard_map/all_to_all | solution.py:456
  84.7 0.0 copy-done
  84.7 2.4 %margin.3 = f32[4,256,256]{2,1,0:T(8,128)S(1)} custom-call(s32[8]{0:T(128)S(1)} %get-tuple-element.12.place_ref, bf16[6,4,2,256,384]{4,3,2,1,0:T(8,128)(2,1)S(1)} %bitcast.13, bf16[256,2304]{1,0:T(8,128)(2,1)S(1)} %bitcast.17), custom_call_target="tpu_custom_call" | custom-call | bytes 9000000 | tf_op jit(solution)/shard_map/margin/pallas_call | solution.py:462
  87.0 0.9 collective-permute-start.4
  88.0 2.4 %margin.2.kept_ref = f32[4,256,256]{2,1,0:T(8,128)S(1)} custom-call(s32[8]{0:T(128)S(1)} %get-tuple-element.12.place_ref, bf16[6,4,2,256,384]{4,3,2,1,0:T(8,128)(2,1)S(1)} %bitcast.14, bf16[256,2304]{1,0:T(8,128)(2,1)S(1)} %bitcast.18), custom_call_target="tpu_custom_call" | custom-call | bytes 9000000 | tf_op jit(solution)/shard_map/margin/pallas_call | solution.py:462
  90.3 0.0 collective-permute-done.4.given_ref
  90.4 0.1 pair.1
  90.5 13.6 %all_to_all.27.in_ref = bf16[16,64,256]{2,1,0:T(8,128)(2,1)S(1)} all-to-all(bf16[16,64,256]{2,1,0:T(8,128)(2,1)S(1)} %pair.1), channel_id=1, replica_groups=mesh['x'=4,'core'=2,'z'=8,'y'=4] {'y','x'}, dimensions={0} | all-to-all | bytes 1048576 | tf_op jit(solution)/shard_map/all_to_all | solution.py:484
  104.1 0.1 partial.1
  104.2 12.2 %all_to_all.28.in_ref = bf16[8,64,256]{2,1,0:T(8,128)(2,1)S(1)} all-to-all(bf16[8,64,256]{2,1,0:T(8,128)(2,1)S(1)} %partial.1), channel_id=1, replica_groups=mesh['x'=4,'core'=2,'z'=8,'y'=4] {'z'}, dimensions={0} | all-to-all | bytes 524288 | tf_op jit(solution)/shard_map/all_to_all | solution.py:494
  116.3 0.1 total.1
  116.4 12.8 %all_to_all.29.coeff_ref = bf16[16,64,256]{2,1,0:T(8,128)(2,1)S(1)} all-to-all(bf16[16,64,256]{2,1,0:T(8,128)(2,1)S(1)} %get-tuple-element.18), channel_id=1, replica_groups=mesh['x'=4,'core'=2,'z'=8,'y'=4] {'y','x'}, dimensions={0} | all-to-all | bytes 1048576 | tf_op jit(solution)/shard_map/all_to_all | solution.py:504
  129.2 3.9 %collective-permute-start.5 = (bf16[16,64,256]{2,1,0:T(8,128)(2,1)S(1)}, bf16[16,64,256]{2,1,0:T(8,128)(2,1)S(1)}, u32[]{:S(2)}, u32[]{:S(2)}) collective-permute-start(bf16[16,64,256]{2,1,0:T(8,128)(2,1)S(1)} %all_to_all.29.coeff_ref), channel_id=1, source_target_pairs={{0,32},{32,0},{1,33},{33,1},{2,34},{34,2},{3,35},{35,3},{4,36},{36... | collective-permute-start | bytes 1572872 | tf_op jit(solution)/shard_map/ppermute | solution.py:505
  133.1 2.5 %clean.2 = (f32[6,256,384]{2,1,0:T(8,128)S(1)}, f32[8,256]{1,0:T(8,128)}) custom-call(s32[8]{0:T(128)S(1)} %get-tuple-element.12.place_ref, bf16[6,4,2,256,384]{4,3,2,1,0:T(8,128)(2,1)S(1)} %bitcast.15, bf16[16,64,256]{2,1,0:T(8,128)(2,1)S(1)} %all_to_all.29.coeff_ref, bf16[256,2304]{1,0:T(8,128)(2,1)S(1)} %bitcast.19, f32[64,256]{1,0:T(8,128)S(1)} %get-tuple-element.19.refs_0_), custom_call_target="tpu_custom_call" | custom-call | bytes 9000000 | tf_op jit(solution)/shard_map/clean/pallas_call | solution.py:511
  135.6 0.0 collective-permute-done.5.coeff_ref
  135.6 3.2 %clean.3 = bf16[6,256,384]{2,1,0:T(8,128)(2,1)} custom-call(s32[8]{0:T(128)S(1)} %get-tuple-element.12.place_ref, bf16[6,4,2,256,384]{4,3,2,1,0:T(8,128)(2,1)S(1)} %bitcast.16, bf16[16,64,256]{2,1,0:T(8,128)(2,1)S(1)} %collective-permute-done.5.coeff_ref, f32[6,256,384]{2,1,0:T(8,128)S(1)} %get-tuple-element.20.r_ref), custom_call_target="tpu_custom_call" | custom-call | bytes 9000000 | tf_op jit(solution)/shard_map/clean/pallas_call | solution.py:511
  (4 shorter events, 0.1 us)
Async XLA Ops:
  0.6 12.8 %copy-start.5 = (s32[64]{0:T(128)S(1)}, s32[64]{0:T(128)}, u32[]{:S(2)}) copy-start(s32[64]{0:T(128)} %param.14) | copy-start | bytes 772
  0.6 13.1 %copy-start.3 = (s32[64]{0:T(128)S(1)}, s32[64]{0:T(128)}, u32[]{:S(2)}) copy-start(s32[64]{0:T(128)} %block_ref.3) | copy-start | bytes 772
  0.7 13.1 %copy-start.2 = (f32[64,128]{1,0:T(8,128)S(1)}, f32[64,128]{1,0:T(8,128)}, u32[]{:S(2)}) copy-start(f32[64,128]{1,0:T(8,128)} %proj_hbm.1) | copy-start | bytes 98308
  0.7 19.9 %copy-start.4 = (f32[6,48,64]{2,1,0:T(8,128)S(1)}, f32[6,48,64]{2,1,0:T(8,128)}, u32[]{:S(2)}) copy-start(f32[6,48,64]{2,1,0:T(8,128)} %param.10) | copy-start | bytes 221188
  3.8 16.9 %copy-start.6 = (f32[32]{0:T(128)S(1)}, f32[32]{0:T(128)}, u32[]{:S(2)}) copy-start(f32[32]{0:T(128)} %param.12) | copy-start | bytes 388
  3.8 16.9 %copy-start.1 = (bf16[3,1024,256]{2,1,0:T(8,128)(2,1)S(1)}, bf16[3,1024,256]{2,1,0:T(8,128)(2,1)}, u32[]{:S(2)}) copy-start(bf16[3,1024,256]{2,1,0:T(8,128)(2,1)} %constant.94.clone.w_ref) | copy-start | bytes 4718596
  3.8 39.2 %collective-permute-start.1 = (bf16[32,18432]{1,0:T(8,128)(2,1)S(1)}, bf16[32,18432]{1,0:T(8,128)(2,1)}, u32[]{:S(2)}, u32[]{:S(2)}) collective-permute-start(bf16[32,18432]{1,0:T(8,128)(2,1)S(1)} %reshape.17.x_ref), channel_id=1, source_target_pairs={{1,0},{2,1},{3,2},{4,3},{5,4},{6,5},{7,6},{8,7},{9,8},{10,9},{11,1... | collective-permute-start | bytes 3538952 | tf_op jit(solution)/shard_map/ppermute | solution.py:379
  12.8 30.3 %collective-permute-start = (bf16[32,18432]{1,0:T(8,128)(2,1)S(1)}, bf16[32,18432]{1,0:T(8,128)(2,1)}, u32[]{:S(2)}, u32[]{:S(2)}) collective-permute-start(bf16[32,18432]{1,0:T(8,128)(2,1)S(1)} %reshape.17.x_ref), channel_id=1, source_target_pairs={{0,1},{1,2},{2,3},{3,4},{4,5},{5,6},{6,7},{7,8},{8,9},{9,10},{10,1... | collective-permute-start | bytes 3538952 | tf_op jit(solution)/shard_map/ppermute | solution.py:378
  15.7 22.1 %collective-permute-start.3 = (f32[32,128]{1,0:T(8,128)S(1)}, f32[32,128]{1,0:T(8,128)S(1)}, u32[]{:S(2)}, u32[]{:S(2)}) collective-permute-start(f32[32,128]{1,0:T(8,128)S(1)} %get-tuple-element.15.mine_ref), channel_id=1, source_target_pairs={{1,0},{2,1},{3,2},{4,3},{5,4},{6,5},{7,6},{8,7},{9,8},{10,9},{11,1... | collective-permute-start | bytes 49160 | tf_op jit(solution)/shard_map/ppermute | solution.py:408
  20.5 22.5 %collective-permute-start.2 = (f32[32,128]{1,0:T(8,128)S(1)}, f32[32,128]{1,0:T(8,128)S(1)}, u32[]{:S(2)}, u32[]{:S(2)}) collective-permute-start(f32[32,128]{1,0:T(8,128)S(1)} %get-tuple-element.15.mine_ref), channel_id=1, source_target_pairs={{0,1},{1,2},{2,3},{3,4},{4,5},{5,6},{6,7},{7,8},{8,9},{9,10},{10,1... | collective-permute-start | bytes 49160 | tf_op jit(solution)/shard_map/ppermute | solution.py:407
  43.1 41.6 %copy-start = (bf16[2048,6,384]{2,0,1:T(8,128)(2,1)S(1)}, bf16[2048,6,384]{2,0,1:T(8,128)(2,1)}, u32[]{:S(2)}) copy-start(bf16[2048,6,384]{2,0,1:T(8,128)(2,1)} %param.16) | copy-start | bytes 28311556
  87.0 3.3 %collective-permute-start.4 = (f32[4,256,256]{2,1,0:T(8,128)S(1)}, f32[4,256,256]{2,1,0:T(8,128)S(1)}, u32[]{:S(2)}, u32[]{:S(2)}) collective-permute-start(f32[4,256,256]{2,1,0:T(8,128)S(1)} %margin.3), channel_id=1, source_target_pairs={{0,32},{32,0},{1,33},{33,1},{2,34},{34,2},{3,35},{35,3},{4,36},{36... | collective-permute-start | bytes 3145736 | tf_op jit(solution)/shard_map/ppermute | solution.py:472
  129.2 6.4 %collective-permute-start.5 = (bf16[16,64,256]{2,1,0:T(8,128)(2,1)S(1)}, bf16[16,64,256]{2,1,0:T(8,128)(2,1)S(1)}, u32[]{:S(2)}, u32[]{:S(2)}) collective-permute-start(bf16[16,64,256]{2,1,0:T(8,128)(2,1)S(1)} %all_to_all.29.coeff_ref), channel_id=1, source_target_pairs={{0,32},{32,0},{1,33},{33,1},{2,34},{34,2},{3,35},{35,3},{4,36},{36... | collective-permute-start | bytes 1572872 | tf_op jit(solution)/shard_map/ppermute | solution.py:505

commit v9 on v8

--- a/solution.py
+++ b/solution.py
@@ -24,7 +24,8 @@
 WIDTH = 6
 DOM = ("z", "y")
 BAND = ("x", "core")
-SHORT = ("y", "x")
+SHORT = ("x", "y")
+SPREAD = ("y", "x")
 ENERGY = ("y", "z")
 F32 = jnp.float32
 BF16 = jnp.bfloat16
@@ -170,7 +171,7 @@
                 num += value * x_ref[pick, where].astype(F32)
             return num
 
-        parts.append(lax.fori_loop(0, plane // BS, halo, jnp.zeros((16, BS), F32), unroll=2))
+        parts.append(lax.fori_loop(0, plane // BS, halo, jnp.zeros((16, BS), F32), unroll=4))
     num = jnp.concatenate(parts, axis=0)
 
     for copy in late:
@@ -290,7 +291,7 @@
                 kept_ref[i, at : at + 8] + given_ref[i, at : at + 8]
                 for at in range(y * 8, share_rows, n_y * 8)
             ]
-            out_ref[y * n_x + i] = jnp.concatenate(pieces, axis=0).astype(BF16)
+            out_ref[i * n_y + y] = jnp.concatenate(pieces, axis=0).astype(BF16)
 
 
 def partial_kernel(in_ref, out_ref):
@@ -501,7 +502,7 @@
         cost_estimate=cost(1),
         name="total",
     )(share)
-    coeffs = lax.all_to_all(coeffs, SHORT, 0, 0, tiled=True)
+    coeffs = lax.all_to_all(coeffs, SPREAD, 0, 0, tiled=True)
     other = lax.ppermute(coeffs, "core", swap)
 
     def clean_call(side, *operands):

time: 139 us -> 139 us (level)
  no operation moved by 1% of the time
where the time goes in v9:
time: 139 us
  blocking collectives  74.3 us (53%)
  Pallas kernels  24.3 us (17%)
  starting transfers between devices  18.9 us (14%)
  waiting for transfers between devices  16 us (12%)
  local copies, waits for them, and re-layouts  3.47 us (2%)
  between operations  1.67 us (1%)
    all_to_all x1, blocking collectives, per_device(): lax.all_to_all(residual, BAND, 0, 0, tiled=True).reshape(bands, width)  23.7 us
    all_to_all x1, blocking collectives, per_device(): coeffs = lax.all_to_all(coeffs, SPREAD, 0, 0, tiled=True)  13.5 us
    all_to_all x1, blocking collectives, per_device(): share = lax.all_to_all(share, SHORT, 0, 0, tiled=True)  13.2 us
    all_to_all x1, blocking collectives, per_device(): pay = lax.all_to_all(pay, ENERGY, 0, 0, tiled=True)  12.3 us
    all_to_all x1, blocking collectives, per_device(): share = lax.all_to_all(share, 'z', 0, 0, tiled=True)  11.7 us
    ppermute x1, waiting for transfers between devices, per_device(): above = lax.ppermute(shares, DOM, down)  10.7 us
    ppermute x1, starting transfers between devices, per_device(): right = lax.ppermute(x, DOM, down)  8.93 us
    pallas_call x1, Pallas kernels, per_device(): pl.pallas_call(functools.partial(local_kernel, planes), out_shape=(jax.Sh...  6.31 us
  transfers between devices with their start and end apart: 6, of which 2 were waited for; matrix products, arithmetic and copies ran while one was open for 0% of the time, Pallas kernels for 9%

profile of v9, /device:TPU:1, one launch (start us, length us, event | category | flops | bytes accessed | tf_op | source)
XLA Modules:
  0.0 138.8 jit_solution(4643897722042114162)
XLA Ops:
  0.6 0.0 copy-start.5
  0.6 0.0 copy-start.3
  0.7 0.0 copy-start.2
  0.7 0.0 copy-start.4
  0.7 3.1 %reshape.17.x_ref = bf16[32,18432]{1,0:T(8,128)(2,1)S(1)} reshape(bf16[32,6,48,64]{3,2,1,0:T(8,128)(2,1)} %param.9) | data formatting | bytes 2359296 | tf_op jit(solution)/shard_map/reshape | solution.py:378
  3.8 0.0 copy-start.6
  3.8 0.0 copy-start.1
  3.8 8.9 %collective-permute-start.1 = (bf16[32,18432]{1,0:T(8,128)(2,1)S(1)}, bf16[32,18432]{1,0:T(8,128)(2,1)}, u32[]{:S(2)}, u32[]{:S(2)}) collective-permute-start(bf16[32,18432]{1,0:T(8,128)(2,1)S(1)} %reshape.17.x_ref), channel_id=1, source_target_pairs={{1,0},{2,1},{3,2},{4,3},{5,4},{6,5},{7,6},{8,7},{9,8},{10,9},{11,1... | collective-permute-start | bytes 3538952 | tf_op jit(solution)/shard_map/ppermute | solution.py:380
  12.8 0.0 collective-permute-start
  13.4 0.0 copy-done.5
  13.5 0.1 concatenate.3.place_ref
  13.6 0.1 fusion.onehot_ref.onehot_hbm
  13.7 0.0 copy-done.3
  13.7 0.0 copy-done.2
  13.7 2.0 %inner.1 = (f32[32,128]{1,0:T(8,128)S(1)}, s32[8]{0:T(128)S(1)}) custom-call(s32[64]{0:T(128)S(1)} %copy-done.3, s32[8]{0:T(128)S(1)} %concatenate.3.place_ref, bf16[32,18432]{1,0:T(8,128)(2,1)S(1)} %reshape.17.x_ref, f32[64,128]{1,0:T(8,128)S(1)} %copy-done.2, f32[128,128]{1,0:T(8,128)S(1)} %fusion.onehot_ref.onehot_hbm), custom_call_target="tpu_custom_call" | custom-call | bytes 6000000 | tf_op jit(solution)/shard_map/inner/pallas_call | solution.py:396
  15.7 4.9 %collective-permute-start.3 = (f32[32,128]{1,0:T(8,128)S(1)}, f32[32,128]{1,0:T(8,128)S(1)}, u32[]{:S(2)}, u32[]{:S(2)}) collective-permute-start(f32[32,128]{1,0:T(8,128)S(1)} %get-tuple-element.15.mine_ref), channel_id=1, source_target_pairs={{1,0},{2,1},{3,2},{4,3},{5,4},{6,5},{7,6},{8,7},{9,8},{10,9},{11,1... | collective-permute-start | bytes 49160 | tf_op jit(solution)/shard_map/ppermute | solution.py:409
  20.5 0.0 collective-permute-start.2
  20.5 0.0 copy-done.4
  20.5 0.1 reshape.19.pot_ref
  20.7 0.0 copy-done.6
  20.7 0.1 pad.9.coupling_ref
  20.8 0.0 copy-done.1
  20.8 6.3 %local.1 = (f32[32,18432]{1,0:T(8,128)S(1)}, f32[32,128]{1,0:T(8,128)S(1)}) custom-call(bf16[32,18432]{1,0:T(8,128)(2,1)S(1)} %reshape.17.x_ref, f32[1,18432]{1,0:T(1,128)S(1)} %reshape.19.pot_ref, bf16[3,1024,256]{2,1,0:T(8,128)(2,1)S(1)} %copy-done.1), custom_call_target="tpu_custom_call" | custom-call | bytes 21000000 | tf_op jit(solution)/shard_map/local/pallas_call | solution.py:411
  27.1 10.7 %collective-permute-done.3.above_hbm = f32[32,128]{1,0:T(8,128)S(1)} collective-permute-done((f32[32,128]{1,0:T(8,128)S(1)}, f32[32,128]{1,0:T(8,128)S(1)}, u32[]{:S(2)}, u32[]{:S(2)}) %collective-permute-start.3) | collective-permute-done | bytes 16416 | tf_op jit(solution)/shard_map/ppermute | solution.py:409
  37.8 5.3 %collective-permute-done.2.below_hbm = f32[32,128]{1,0:T(8,128)S(1)} collective-permute-done((f32[32,128]{1,0:T(8,128)S(1)}, f32[32,128]{1,0:T(8,128)S(1)}, u32[]{:S(2)}, u32[]{:S(2)}) %collective-permute-start.2) | collective-permute-done | bytes 16416 | tf_op jit(solution)/shard_map/ppermute | solution.py:408
  43.1 0.0 collective-permute-done.1.right_hbm
  43.1 0.0 collective-permute-done.left_hbm
  43.1 0.0 copy-start
  43.1 3.6 %hamilton.1 = (f32[32,18432]{1,0:T(8,128)S(1)}, f32[32,9,1,128]{3,2,1,0:T(1,128)S(1)}) custom-call(f32[32,18432]{1,0:T(8,128)S(1)} %get-tuple-element.13.h0_ref, bf16[32,18432]{1,0:T(8,128)(2,1)S(1)} %reshape.17.x_ref, bf16[32,18432]{1,0:T(8,128)(2,1)} %collective-permute-done.left_hbm, bf16[32,18432]{1,0:T(8,128)(2,1)} %collective-permute-done.1.right_hbm, ...), custom_call_target="tpu_custom_call" | custom-call | bytes 15000000 | tf_op jit(solution)/shard_map/hamilton/pallas_call | solution.py:425
  46.6 12.3 %all_to_all.25.pay_ref = f32[32,9,1,128]{3,2,1,0:T(1,128)S(1)} all-to-all(f32[32,9,1,128]{3,2,1,0:T(1,128)S(1)} %get-tuple-element.17), channel_id=1, replica_groups=mesh['x'=4,'core'=2,'z'=8,'y'=4] {'y','z'}, dimensions={0} | all-to-all | bytes 294912 | tf_op jit(solution)/shard_map/all_to_all | solution.py:440
  58.9 1.9 %residual.1 = bf16[8,32,2304]{2,1,0:T(8,128)(2,1)S(1)} custom-call(s32[64]{0:T(128)S(1)} %copy-done.3, s32[8]{0:T(128)S(1)} %get-tuple-element.12.place_ref, f32[32,18432]{1,0:T(8,128)S(1)} %get-tuple-element.16.h_ref, bf16[32,18432]{1,0:T(8,128)(2,1)S(1)} %reshape.17.x_ref, f32[32,9,1,128]{3,2,1,0:T(1,128)S(1)} %all_to_all.25.pay_ref, ...), custom_call_target="tpu_custom_call" | custom-call | bytes 6000000 | tf_op jit(solution)/shard_map/residual/pallas_call | solution.py:442
  60.8 23.7 %all_to_all.26 = bf16[8,32,2304]{2,1,0:T(8,128)(2,1)S(1)} all-to-all(bf16[8,32,2304]{2,1,0:T(8,128)(2,1)S(1)} %residual.1), channel_id=1, replica_groups=mesh['x'=4,'core'=2,'z'=8,'y'=4] {'x','core'}, dimensions={0} | all-to-all | bytes 2359296 | tf_op jit(solution)/shard_map/all_to_all | solution.py:457
  84.5 0.0 copy-done
  84.5 2.4 %margin.3 = f32[4,256,256]{2,1,0:T(8,128)S(1)} custom-call(s32[8]{0:T(128)S(1)} %get-tuple-element.12.place_ref, bf16[6,4,2,256,384]{4,3,2,1,0:T(8,128)(2,1)S(1)} %bitcast.13, bf16[256,2304]{1,0:T(8,128)(2,1)S(1)} %bitcast.17), custom_call_target="tpu_custom_call" | custom-call | bytes 9000000 | tf_op jit(solution)/shard_map/margin/pallas_call | solution.py:463
  86.9 1.0 collective-permute-start.4
  87.8 2.4 %margin.2.kept_ref = f32[4,256,256]{2,1,0:T(8,128)S(1)} custom-call(s32[8]{0:T(128)S(1)} %get-tuple-element.12.place_ref, bf16[6,4,2,256,384]{4,3,2,1,0:T(8,128)(2,1)S(1)} %bitcast.14, bf16[256,2304]{1,0:T(8,128)(2,1)S(1)} %bitcast.18), custom_call_target="tpu_custom_call" | custom-call | bytes 9000000 | tf_op jit(solution)/shard_map/margin/pallas_call | solution.py:463
  90.2 0.0 collective-permute-done.4.given_ref
  90.2 0.1 pair.1
  90.3 13.2 %all_to_all.27.in_ref = bf16[16,64,256]{2,1,0:T(8,128)(2,1)S(1)} all-to-all(bf16[16,64,256]{2,1,0:T(8,128)(2,1)S(1)} %pair.1), channel_id=1, replica_groups=mesh['x'=4,'core'=2,'z'=8,'y'=4] {'x','y'}, dimensions={0} | all-to-all | bytes 1048576 | tf_op jit(solution)/shard_map/all_to_all | solution.py:485
  103.5 0.1 partial.1
  103.6 11.7 %all_to_all.28.in_ref = bf16[8,64,256]{2,1,0:T(8,128)(2,1)S(1)} all-to-all(bf16[8,64,256]{2,1,0:T(8,128)(2,1)S(1)} %partial.1), channel_id=1, replica_groups=mesh['x'=4,'core'=2,'z'=8,'y'=4] {'z'}, dimensions={0} | all-to-all | bytes 524288 | tf_op jit(solution)/shard_map/all_to_all | solution.py:495
  115.2 0.1 total.1
  115.3 13.5 %all_to_all.29.coeff_ref = bf16[16,64,256]{2,1,0:T(8,128)(2,1)S(1)} all-to-all(bf16[16,64,256]{2,1,0:T(8,128)(2,1)S(1)} %get-tuple-element.18), channel_id=1, replica_groups=mesh['x'=4,'core'=2,'z'=8,'y'=4] {'y','x'}, dimensions={0} | all-to-all | bytes 1048576 | tf_op jit(solution)/shard_map/all_to_all | solution.py:505
  128.8 4.2 %collective-permute-start.5 = (bf16[16,64,256]{2,1,0:T(8,128)(2,1)S(1)}, bf16[16,64,256]{2,1,0:T(8,128)(2,1)S(1)}, u32[]{:S(2)}, u32[]{:S(2)}) collective-permute-start(bf16[16,64,256]{2,1,0:T(8,128)(2,1)S(1)} %all_to_all.29.coeff_ref), channel_id=1, source_target_pairs={{0,32},{32,0},{1,33},{33,1},{2,34},{34,2},{3,35},{35,3},{4,36},{36... | collective-permute-start | bytes 1572872 | tf_op jit(solution)/shard_map/ppermute | solution.py:506
  132.9 2.5 %clean.2 = (f32[6,256,384]{2,1,0:T(8,128)S(1)}, f32[8,256]{1,0:T(8,128)}) custom-call(s32[8]{0:T(128)S(1)} %get-tuple-element.12.place_ref, bf16[6,4,2,256,384]{4,3,2,1,0:T(8,128)(2,1)S(1)} %bitcast.15, bf16[16,64,256]{2,1,0:T(8,128)(2,1)S(1)} %all_to_all.29.coeff_ref, bf16[256,2304]{1,0:T(8,128)(2,1)S(1)} %bitcast.19, f32[64,256]{1,0:T(8,128)S(1)} %get-tuple-element.19.refs_0_), custom_call_target="tpu_custom_call" | custom-call | bytes 9000000 | tf_op jit(solution)/shard_map/clean/pallas_call | solution.py:512
  135.4 0.0 collective-permute-done.5.coeff_ref
  135.4 3.2 %clean.3 = bf16[6,256,384]{2,1,0:T(8,128)(2,1)} custom-call(s32[8]{0:T(128)S(1)} %get-tuple-element.12.place_ref, bf16[6,4,2,256,384]{4,3,2,1,0:T(8,128)(2,1)S(1)} %bitcast.16, bf16[16,64,256]{2,1,0:T(8,128)(2,1)S(1)} %collective-permute-done.5.coeff_ref, f32[6,256,384]{2,1,0:T(8,128)S(1)} %get-tuple-element.20.r_ref), custom_call_target="tpu_custom_call" | custom-call | bytes 9000000 | tf_op jit(solution)/shard_map/clean/pallas_call | solution.py:512
  (4 shorter events, 0.1 us)
Async XLA Ops:
  0.6 12.8 %copy-start.5 = (s32[64]{0:T(128)S(1)}, s32[64]{0:T(128)}, u32[]{:S(2)}) copy-start(s32[64]{0:T(128)} %param.14) | copy-start | bytes 772
  0.6 13.1 %copy-start.3 = (s32[64]{0:T(128)S(1)}, s32[64]{0:T(128)}, u32[]{:S(2)}) copy-start(s32[64]{0:T(128)} %block_ref.3) | copy-start | bytes 772
  0.7 13.1 %copy-start.2 = (f32[64,128]{1,0:T(8,128)S(1)}, f32[64,128]{1,0:T(8,128)}, u32[]{:S(2)}) copy-start(f32[64,128]{1,0:T(8,128)} %proj_hbm.1) | copy-start | bytes 98308
  0.7 19.9 %copy-start.4 = (f32[6,48,64]{2,1,0:T(8,128)S(1)}, f32[6,48,64]{2,1,0:T(8,128)}, u32[]{:S(2)}) copy-start(f32[6,48,64]{2,1,0:T(8,128)} %param.10) | copy-start | bytes 221188
  3.8 16.9 %copy-start.6 = (f32[32]{0:T(128)S(1)}, f32[32]{0:T(128)}, u32[]{:S(2)}) copy-start(f32[32]{0:T(128)} %param.12) | copy-start | bytes 388
  3.8 16.9 %copy-start.1 = (bf16[3,1024,256]{2,1,0:T(8,128)(2,1)S(1)}, bf16[3,1024,256]{2,1,0:T(8,128)(2,1)}, u32[]{:S(2)}) copy-start(bf16[3,1024,256]{2,1,0:T(8,128)(2,1)} %constant.94.clone.w_ref) | copy-start | bytes 4718596
  3.8 39.2 %collective-permute-start.1 = (bf16[32,18432]{1,0:T(8,128)(2,1)S(1)}, bf16[32,18432]{1,0:T(8,128)(2,1)}, u32[]{:S(2)}, u32[]{:S(2)}) collective-permute-start(bf16[32,18432]{1,0:T(8,128)(2,1)S(1)} %reshape.17.x_ref), channel_id=1, source_target_pairs={{1,0},{2,1},{3,2},{4,3},{5,4},{6,5},{7,6},{8,7},{9,8},{10,9},{11,1... | collective-permute-start | bytes 3538952 | tf_op jit(solution)/shard_map/ppermute | solution.py:380
  12.8 30.3 %collective-permute-start = (bf16[32,18432]{1,0:T(8,128)(2,1)S(1)}, bf16[32,18432]{1,0:T(8,128)(2,1)}, u32[]{:S(2)}, u32[]{:S(2)}) collective-permute-start(bf16[32,18432]{1,0:T(8,128)(2,1)S(1)} %reshape.17.x_ref), channel_id=1, source_target_pairs={{0,1},{1,2},{2,3},{3,4},{4,5},{5,6},{6,7},{7,8},{8,9},{9,10},{10,1... | collective-permute-start | bytes 3538952 | tf_op jit(solution)/shard_map/ppermute | solution.py:379
  15.7 22.1 %collective-permute-start.3 = (f32[32,128]{1,0:T(8,128)S(1)}, f32[32,128]{1,0:T(8,128)S(1)}, u32[]{:S(2)}, u32[]{:S(2)}) collective-permute-start(f32[32,128]{1,0:T(8,128)S(1)} %get-tuple-element.15.mine_ref), channel_id=1, source_target_pairs={{1,0},{2,1},{3,2},{4,3},{5,4},{6,5},{7,6},{8,7},{9,8},{10,9},{11,1... | collective-permute-start | bytes 49160 | tf_op jit(solution)/shard_map/ppermute | solution.py:409
  20.5 22.5 %collective-permute-start.2 = (f32[32,128]{1,0:T(8,128)S(1)}, f32[32,128]{1,0:T(8,128)S(1)}, u32[]{:S(2)}, u32[]{:S(2)}) collective-permute-start(f32[32,128]{1,0:T(8,128)S(1)} %get-tuple-element.15.mine_ref), channel_id=1, source_target_pairs={{0,1},{1,2},{2,3},{3,4},{4,5},{5,6},{6,7},{7,8},{8,9},{9,10},{10,1... | collective-permute-start | bytes 49160 | tf_op jit(solution)/shard_map/ppermute | solution.py:408
  43.1 41.5 %copy-start = (bf16[2048,6,384]{2,0,1:T(8,128)(2,1)S(1)}, bf16[2048,6,384]{2,0,1:T(8,128)(2,1)}, u32[]{:S(2)}) copy-start(bf16[2048,6,384]{2,0,1:T(8,128)(2,1)} %param.16) | copy-start | bytes 28311556
  86.9 3.3 %collective-permute-start.4 = (f32[4,256,256]{2,1,0:T(8,128)S(1)}, f32[4,256,256]{2,1,0:T(8,128)S(1)}, u32[]{:S(2)}, u32[]{:S(2)}) collective-permute-start(f32[4,256,256]{2,1,0:T(8,128)S(1)} %margin.3), channel_id=1, source_target_pairs={{0,32},{32,0},{1,33},{33,1},{2,34},{34,2},{3,35},{35,3},{4,36},{36... | collective-permute-start | bytes 3145736 | tf_op jit(solution)/shard_map/ppermute | solution.py:473
  128.8 6.7 %collective-permute-start.5 = (bf16[16,64,256]{2,1,0:T(8,128)(2,1)S(1)}, bf16[16,64,256]{2,1,0:T(8,128)(2,1)S(1)}, u32[]{:S(2)}, u32[]{:S(2)}) collective-permute-start(bf16[16,64,256]{2,1,0:T(8,128)(2,1)S(1)} %all_to_all.29.coeff_ref), channel_id=1, source_target_pairs={{0,32},{32,0},{1,33},{33,1},{2,34},{34,2},{3,35},{35,3},{4,36},{36... | collective-permute-start | bytes 1572872 | tf_op jit(solution)/shard_map/ppermute | solution.py:506
